TPU v7x, 1024 devices: a whole 4x4x32 slice. The times are simulated.
1024 devices in a mesh: dp: 16 (over x, y), opt: 64 (over z, core).
Axes of the slice: x: 4, y: 4, z: 32, core: 2. Of those that a mesh axis runs over, the one named last changes fastest.
Arguments:
- gradients: bfloat16 [16, 128, 512, 512], P('dp', 'opt'), may hold values from -0.59765625 to 0.59765625
- owner_map: int32 [128], replicated, may hold values from 0 to 63, as said below
- left_root: bfloat16 [320, 512, 512], P('opt', 'dp'), may hold values from -0.25 to 0.25
- right_basis: bfloat16 [320, 512, 512], P('opt'), may hold values from -0.25 to 0.25
- right_eigen: float32 [320, 512], P('opt'), may hold values from 0.01 to 100
- left_stat: float32 [320, 512, 512], P('opt', 'dp'), may hold values from -6 to 6
- right_stat: float32 [320, 512, 512], P('opt', 'dp'), may hold values from -6 to 6
Outputs:
- update: bfloat16 [320, 512, 512], P('opt')
- left_new: float32 [320, 512, 512], P('opt', 'dp')
- right_new: float32 [320, 512, 512], P('opt', 'dp')
Inputs may be any that keep to these rules, and one draw needn't show every extreme that they name: `owner_map`: blocks 2 * i to 2 * i + 1 go to different owners; no owner holds more than 5 blocks, and some owner holds exactly 5.
All inputs are finite; a program needn't handle non-finite values.
Results may differ from a plain program's by a relative error of at most 0.023.
Values may be sent and summed in bfloat16 or wider, within the bound.
No kernel may reach another device: no remote copies, remote signals or barrier semaphores. Data moves between devices by JAX's collectives and lax.ppermute only.
A program may use at most 32 MiB of HBM per device.

v0:
```python
import jax
import jax.numpy as jnp
from jax import lax
from jax.sharding import PartitionSpec as P

decay_rate = 0.9
epsilon = 1e-06


def body(gradients, owner_map, left_root, right_basis, right_eigen, left_stat, right_stat):
    partial_sum = gradients[0].astype(jnp.float32)
    summed = lax.psum_scatter(
        partial_sum.astype(jnp.bfloat16), "dp", scatter_dimension=1, tiled=True
    )
    block_count, slab_rows, block_width = summed.shape
    owner_count = lax.axis_size("opt")
    my_index = lax.axis_index("opt")
    capacity = left_stat.shape[0]
    targets = jnp.arange(owner_count, dtype=jnp.int32)
    my_owners = lax.dynamic_slice_in_dim(owner_map, my_index * block_count, block_count)
    picker = (targets[:, None] == my_owners[None, :]).astype(jnp.bfloat16)
    outgoing = jnp.dot(
        picker,
        summed.reshape(block_count, slab_rows * block_width),
        preferred_element_type=jnp.float32,
    )
    outgoing = outgoing.astype(jnp.bfloat16).reshape(owner_count, slab_rows, block_width)
    incoming = lax.all_to_all(outgoing, "opt", split_axis=0, concat_axis=0, tiled=True)
    from_sender = jnp.any(owner_map.reshape(owner_count, block_count) == my_index, axis=1)
    slot_of = jnp.cumsum(from_sender.astype(jnp.int32)) - 1
    placer = (
        (slot_of[None, :] == jnp.arange(capacity, dtype=jnp.int32)[:, None]) & from_sender[None, :]
    ).astype(jnp.bfloat16)
    owned_rows = jnp.dot(
        placer,
        incoming.reshape(owner_count, slab_rows * block_width),
        preferred_element_type=jnp.float32,
    )
    owned_rows = owned_rows.astype(jnp.bfloat16).reshape(capacity, slab_rows, block_width)
    row_base = lax.axis_index("dp") * slab_rows
    gathered = lax.all_gather(owned_rows, "dp", axis=1, tiled=True)
    columns = jnp.einsum("crb,cnb->crn", owned_rows, gathered, preferred_element_type=jnp.float32)
    left_gram = columns
    my_columns = lax.dynamic_slice_in_dim(gathered, row_base, slab_rows, 2)
    right_gram = jnp.einsum(
        "cnr,cnb->crb", my_columns, gathered, preferred_element_type=jnp.float32
    )
    left_applied = jnp.einsum(
        "crn,cnb->crb", left_root, gathered, preferred_element_type=jnp.float32
    )
    left_gram, right_gram, left_applied = (left_gram, right_gram, left_applied)
    left_new = decay_rate * left_stat + (1.0 - decay_rate) * left_gram
    right_new = decay_rate * right_stat + (1.0 - decay_rate) * right_gram
    applied = left_applied.astype(jnp.bfloat16)
    factor = (right_eigen + epsilon) ** (-0.25)
    scaled = jnp.einsum("crb,cbe->cre", applied, right_basis, preferred_element_type=jnp.float32)
    scaled = (scaled * factor[:, None, :]).astype(jnp.bfloat16)
    update = jnp.einsum(
        "cre,cbe->crb", scaled, right_basis, preferred_element_type=jnp.float32
    ).astype(jnp.bfloat16)
    gathered_update = lax.all_gather(update, "dp", axis=1, tiled=True)
    return (gathered_update, left_new, right_new)


def solution(mesh):
    in_specs = (
        P("dp", "opt", None, None),
        P(),
        P("opt", "dp", None),
        P("opt", None, None),
        P("opt", None),
        P("opt", "dp", None),
        P("opt", "dp", None),
    )
    out_specs = (P("opt", None, None), P("opt", "dp", None), P("opt", "dp", None))
    return jax.shard_map(body, mesh=mesh, in_specs=in_specs, out_specs=out_specs, check_vma=False)
```

profile of v0, /device:TPU:1, one launch (start us, length us, event | category | flops | bytes accessed | tf_op | source)
XLA Modules:
  0.0 520.7 jit_solution(1658024344506115282)
XLA Ops:
  7.2 0.7 reduce-scatter.2.cloned.1.call-update
  7.9 0.8 dynamic_slice.6
  8.7 120.0 %reduce-scatter.2.cloned.1.call-done = bf16[2,32,512]{2,1,0:T(8,128)(2,1)} async-done(((bf16[2,512,512]{2,1,0:T(8,128)(2,1)}), bf16[2,32,512]{2,1,0:T(8,128)(2,1)}) %reduce-scatter.2.cloned.1.call-update) | async-done | bytes 65552 | tf_op jit(solution)/shard_map/reduce_scatter | solution.py:12
  128.7 0.9 copy.15
  129.6 0.7 convolution_convert_fusion
  130.3 2.1 copy.16
  132.4 25.8 %all-to-all-start = ((bf16[64,32,512]{2,1,0:T(8,128)(2,1)}), bf16[64,32,512]{2,1,0:T(8,128)(2,1)}, u32[]{:S(2)}, u32[]{:S(2)}) async-start(bf16[64,32,512]{2,1,0:T(8,128)(2,1)} %bitcast.23), calls=%async_computation.1 | async-start | bytes 4194304 | tf_op jit(solution)/shard_map/all_to_all | solution.py:28
  158.2 0.0 all-gather.3.cloned.1.call-start
  158.2 0.1 eq.37
  158.4 0.1 reduce_or.9
  158.5 0.1 copy.12
  158.6 0.1 reduce-window.8
  158.7 0.1 add_reduce_fusion
  158.8 197.0 %all-to-all-done = bf16[64,32,512]{2,1,0:T(8,128)(2,1)} async-done(((bf16[64,32,512]{2,1,0:T(8,128)(2,1)}), bf16[64,32,512]{2,1,0:T(8,128)(2,1)}, u32[]{:S(2)}, u32[]{:S(2)}) %all-to-all-start) | async-done | bytes 2097184 | tf_op jit(solution)/shard_map/all_to_all | solution.py:28
  355.8 2.9 copy.17
  358.7 0.4 convolution_convert_fusion.1
  359.0 0.7 copy.20
  359.9 63.5 %all-gather.3.cloned.1.call-done = bf16[5,512,512]{2,1,0:T(8,128)(2,1)} async-done(((bf16[5,32,512]{2,1,0:T(8,128)(2,1)}), bf16[5,512,512]{2,1,0:T(8,128)(2,1)}) %all-gather.3.cloned.1.call-update) | async-done | bytes 2621456 | tf_op jit(solution)/shard_map/all_gather | solution.py:41
  423.4 3.1 fusion.4
  426.5 1.5 convolution_convert_fusion.3
  428.1 3.6 fusion.3
  431.7 1.6 fusion.2
  433.3 77.4 %all-gather.5.cloned.1.call-done = bf16[5,512,512]{2,1,0:T(8,128)(2,1)} async-done(((bf16[5,32,512]{2,1,0:T(8,128)(2,1)}), bf16[5,512,512]{2,1,0:T(8,128)(2,1)}) %all-gather.5.cloned.1.call-update) | async-done | bytes 2621456 | tf_op jit(solution)/shard_map/all_gather | solution.py:61
  510.7 3.5 copy.22
  (23 shorter events, 0.2 us)
Async XLA Ops:
  7.2 416.2 %copy-start = (bf16[5,512,512]{2,1,0:T(8,128)(2,1)S(1)}, bf16[5,512,512]{2,1,0:T(8,128)(2,1)}, u32[]{:S(2)}) copy-start(bf16[5,512,512]{2,1,0:T(8,128)(2,1)} %param.10) | copy-start | bytes 7864324
  7.2 121.5 %reduce-scatter.2.cloned.1.call-start = ((), (), s32[]{:S(2)}) async-start(), calls=%async_computation.2 | async-start | bytes 1114112 | tf_op jit(solution)/shard_map/reduce_scatter | solution.py:12
  132.4 25.8 %copy-start.7 = (s32[128]{0:T(128)S(1)}, s32[128]{0:T(128)}, u32[]{:S(2)}) copy-start(s32[128]{0:T(128)} %param.8) | copy-start | bytes 1540
  132.4 223.4 %all-to-all-start = ((bf16[64,32,512]{2,1,0:T(8,128)(2,1)}), bf16[64,32,512]{2,1,0:T(8,128)(2,1)}, u32[]{:S(2)}, u32[]{:S(2)}) async-start(bf16[64,32,512]{2,1,0:T(8,128)(2,1)} %bitcast.23), calls=%async_computation.1 | async-start | bytes 4194304 | tf_op jit(solution)/shard_map/all_to_all | solution.py:28
  158.2 265.2 %all-gather.3.cloned.1.call-start = ((), (), s32[]{:S(2)}) async-start(), calls=%async_computation.3 | async-start | bytes 2785280 | tf_op jit(solution)/shard_map/all_gather | solution.py:41
  355.8 4.1 copy-start.6
  355.8 67.6 %copy-start.5 = (bf16[5,32,512]{2,1,0:T(8,128)(2,1)S(1)}, bf16[5,32,512]{2,1,0:T(8,128)(2,1)}, u32[]{:S(2)}) copy-start(bf16[5,32,512]{2,1,0:T(8,128)(2,1)} %param.9) | copy-start | bytes 491524
  359.8 150.9 %all-gather.5.cloned.1.call-start = ((), (), s32[]{:S(2)}) async-start(), calls=%async_computation.4 | async-start | bytes 2785280 | tf_op jit(solution)/shard_map/all_gather | solution.py:61
  426.5 1.6 copy-start.3
  426.5 5.2 %copy-start.2 = (bf16[1,5,32,512]{3,2,1,0:T(8,128)(2,1)S(1)}, bf16[1,5,32,512]{3,2,1,0:T(8,128)(2,1)}, u32[]{:S(2)}) copy-start(bf16[1,5,32,512]{3,2,1,0:T(8,128)(2,1)} %copy.20) | copy-start | bytes 491524
  428.0 3.7 copy-start.4
  428.1 3.6 copy-start.1
Sparse Core Ops, SparseCore 0:
  13.3 115.4 reduce-scatter.1
  359.9 63.4 all-gather.2
  429.0 81.6 all-gather.4
where the time goes:
time: 521 us
  waiting for transfers between devices  459 us (88%)
  starting transfers between devices  25.9 us (5%)
  between operations  13.9 us (3%)
  local copies, waits for them, and re-layouts  11.2 us (2%)
  matrix products  10.9 us (2%)
    all_to_all x1, waiting for transfers between devices, body(): lax.all_to_all(outgoing, 'opt', split_axis=0, concat_axis=0, tiled=True)  197 us
    reduce_scatter x1, waiting for transfers between devices, body(): lax.psum_scatter(partial_sum.astype(jnp.bfloat16), 'dp', scatter_dimensio...  120 us
    all_gather x1, waiting for transfers between devices, body(): gathered_update = lax.all_gather(update, 'dp', axis=1, tiled=True)  77.4 us
    all_gather x1, waiting for transfers between devices, body(): gathered = lax.all_gather(owned_rows, 'dp', axis=1, tiled=True)  63.5 us
    all_to_all x1, starting transfers between devices, body(): lax.all_to_all(outgoing, 'opt', split_axis=0, concat_axis=0, tiled=True)  25.8 us
  transfers between devices with their start and end apart: 4, of which 4 were waited for; matrix products, arithmetic and copies ran while one was open for 1% of the time, Pallas kernels for 0%

commit v1 on v0

v1 whole, which is shorter than its diff:
```python
import jax
import jax.numpy as jnp
from jax import lax
from jax.sharding import Mesh, PartitionSpec as P

decay_rate = 0.9
epsilon = 1e-06
NEAR = 4


def broadcast_gather(x, axis):
    n = lax.axis_size(axis)
    copies = jnp.broadcast_to(x[None], (n,) + x.shape)
    return lax.all_to_all(copies, axis, split_axis=0, concat_axis=0, tiled=True)


def body(gradients, owner_map, left_root, right_basis, right_eigen, left_stat, right_stat):
    n_dp, n_far, n_near = lax.axis_size("dp"), lax.axis_size("far"), lax.axis_size("near")
    _, blocks, width, _ = gradients.shape
    cap, rows, _ = left_stat.shape
    my_dp, my_near = lax.axis_index("dp"), lax.axis_index("near")
    row_tiles, col_tiles = rows // 8, width // 128

    root = lax.all_gather(left_root, "dp", axis=1, tiled=True)

    sent = gradients.reshape(blocks, n_dp, row_tiles, 8, col_tiles, 128)
    sent = sent.transpose(1, 2, 4, 0, 3, 5).reshape(n_dp, n_far, blocks * 8, 128)
    parts = lax.all_to_all(sent, "dp", split_axis=0, concat_axis=0, tiled=True)
    summed = jnp.sum(parts.astype(jnp.float32), axis=0).astype(jnp.bfloat16)

    spread = lax.all_to_all(summed, "far", split_axis=0, concat_axis=0, tiled=True)
    tiles = broadcast_gather(spread, "near")
    tiles = tiles.reshape(n_near, n_far, blocks, 8, 128)

    owners = owner_map
    same = owners[:, None] == owners[None, :]
    order = jnp.arange(owners.shape[0], dtype=jnp.int32)
    slot = jnp.sum((same & (order[None, :] < order[:, None])).astype(jnp.int32), axis=1)
    place = jnp.where(owners % n_near == my_near, owners // n_near * cap + slot, -1)
    place = place.reshape(n_far, n_near, blocks).transpose(1, 0, 2).reshape(-1)
    pick = (jnp.arange(n_far * cap, dtype=jnp.int32)[:, None] == place[None, :]).astype(jnp.bfloat16)
    chosen = jnp.dot(
        pick, tiles.reshape(-1, 8 * 128), preferred_element_type=jnp.float32
    ).astype(jnp.bfloat16)
    deliver = chosen.reshape(n_far, cap * 8, 128)
    arrived = lax.all_to_all(deliver, "far", split_axis=0, concat_axis=0, tiled=True)

    owned = arrived.reshape(row_tiles, col_tiles, cap, 8, 128)
    owned = owned.transpose(2, 0, 3, 1, 4).reshape(cap, rows, width)
    gathered = broadcast_gather(owned, "dp").transpose(1, 0, 2, 3).reshape(cap, width, width)

    left_gram = jnp.einsum("crb,cnb->crn", owned, gathered, preferred_element_type=jnp.float32)
    my_columns = lax.dynamic_slice_in_dim(gathered, my_dp * rows, rows, 2)
    right_gram = jnp.einsum("cnr,cnb->crb", my_columns, gathered, preferred_element_type=jnp.float32)
    left_new = decay_rate * left_stat + (1.0 - decay_rate) * left_gram
    right_new = decay_rate * right_stat + (1.0 - decay_rate) * right_gram

    applied = jnp.einsum(
        "crn,cnb->crb", root, gathered, preferred_element_type=jnp.float32
    ).astype(jnp.bfloat16)
    factor = (right_eigen + epsilon) ** (-0.25)
    scaled = jnp.einsum("crb,cbe->cre", applied, right_basis, preferred_element_type=jnp.float32)
    scaled = (scaled * factor[:, None, :]).astype(jnp.bfloat16)
    update = jnp.einsum(
        "cre,cbe->crb", scaled, right_basis, preferred_element_type=jnp.float32
    ).astype(jnp.bfloat16)
    return (update, left_new, right_new)


def solution(mesh):
    n_dp, n_opt = mesh.devices.shape
    inner = Mesh(mesh.devices.reshape(n_dp, n_opt // NEAR, NEAR), ("dp", "far", "near"))
    opt = ("far", "near")
    in_specs = (
        P("dp", opt, None, None),
        P(),
        P(opt, "dp", None),
        P(opt, None, None),
        P(opt, None),
        P(opt, "dp", None),
        P(opt, "dp", None),
    )
    out_specs = (P(opt, None, None), P(opt, "dp", None), P(opt, "dp", None))
    return jax.shard_map(body, mesh=inner, in_specs=in_specs, out_specs=out_specs, check_vma=False)
```

time: 521 us -> 205 us (0.39)
  the two profiles are of different devices: /device:TPU:1 before, /device:TPU:96 now
where the time goes in v1:
time: 205 us
  blocking collectives  108 us (53%)
  waiting for transfers between devices  47.6 us (23%)
  matrix products  16.9 us (8%)
  between operations  14.2 us (7%)
  starting transfers between devices  8.27 us (4%)
  local copies, waits for them, and re-layouts  8.22 us (4%)
    all_to_all x1, blocking collectives, body(): lax.all_to_all(summed, 'far', split_axis=0, concat_axis=0, tiled=True)  48.3 us
    all_to_all x2, waiting for transfers between devices, broadcast_gather(): return lax.all_to_all(copies, axis, split_axis=0, concat_axis=0, tiled=True)  46.9 us
    all_to_all x1, blocking collectives, body(): lax.all_to_all(deliver, 'far', split_axis=0, concat_axis=0, tiled=True)  35.8 us
    all_to_all x1, blocking collectives, body(): parts = lax.all_to_all(sent, 'dp', split_axis=0, concat_axis=0, tiled=True)  23.8 us
    all_to_all x2, starting transfers between devices, broadcast_gather(): return lax.all_to_all(copies, axis, split_axis=0, concat_axis=0, tiled=True)  8.27 us
    dot_general x1, matrix products, body(): jnp.einsum('crb,cbe->cre', applied, right_basis, preferred_element_type=j...  7.9 us
    dot_general x1, matrix products, body(): jnp.einsum('cre,cbe->crb', scaled, right_basis, preferred_element_type=jn...  5.69 us
  transfers between devices with their start and end apart: 3, of which 2 were waited for; matrix products, arithmetic and copies ran while one was open for 3% of the time, Pallas kernels for 0%

profile of v1, /device:TPU:96, one launch (start us, length us, event | category | flops | bytes accessed | tf_op | source)
XLA Modules:
  0.0 204.7 jit_solution(2015110346249173639)
XLA Ops:
  7.2 1.6 copy.37
  8.8 23.8 %all_to_all.25 = bf16[16,16,16,128]{3,2,1,0:T(8,128)(2,1)} all-to-all(bf16[16,16,16,128]{3,2,1,0:T(8,128)(2,1)S(1)} %bitcast.27), channel_id=1, replica_groups=mesh['dp'=16,'far'=16,'near'=4] {'dp'}, dimensions={0} | all-to-all | bytes 2097152 | tf_op jit(solution)/shard_map/all_to_all | solution.py:28
  32.6 1.4 reduce_sum.22
  34.0 48.3 %all_to_all.26 = bf16[16,16,128]{2,1,0:T(8,128)(2,1)S(1)} all-to-all(bf16[16,16,128]{2,1,0:T(8,128)(2,1)S(1)} %reduce_sum.22), channel_id=1, replica_groups=mesh['dp'=16,'far'=16,'near'=4] {'far'}, dimensions={0} | all-to-all | bytes 131072 | tf_op jit(solution)/shard_map/all_to_all | solution.py:31
  82.3 0.7 broadcast_in_dim.7
  83.0 3.7 %all-to-all-start.2 = ((bf16[4,16,16,128]{3,2,1,0:T(8,128)(2,1)}), bf16[4,16,16,128]{3,2,1,0:T(8,128)(2,1)S(1)}, u32[]{:S(2)}, u32[]{:S(2)}) async-start(bf16[4,16,16,128]{3,2,1,0:T(8,128)(2,1)} %broadcast_in_dim.7), calls=%async_computation.2 | async-start | bytes 524288 | tf_op jit(solution)/shard_map/all_to_all | solution.py:14
  86.7 0.7 all-gather.2.cloned.1.call-update
  87.5 0.2 convert_reduce_fusion
  87.7 0.2 reshape.31
  87.8 0.1 eq.42
  88.0 3.1 %all-to-all-done.2 = bf16[4,16,16,128]{3,2,1,0:T(8,128)(2,1)S(1)} async-done(((bf16[4,16,16,128]{3,2,1,0:T(8,128)(2,1)}), bf16[4,16,16,128]{3,2,1,0:T(8,128)(2,1)S(1)}, u32[]{:S(2)}, u32[]{:S(2)}) %all-to-all-start.2) | async-done | bytes 262176 | tf_op jit(solution)/shard_map/all_to_all | solution.py:14
  91.1 0.1 reshape_reshape.3
  91.2 0.2 convolution_convert_fusion
  91.4 0.1 reshape.34
  91.5 35.8 %all_to_all.27 = bf16[16,40,128]{2,1,0:T(8,128)(2,1)S(1)} all-to-all(bf16[16,40,128]{2,1,0:T(8,128)(2,1)S(1)} %reshape.34), channel_id=1, replica_groups=mesh['dp'=16,'far'=16,'near'=4] {'far'}, dimensions={0} | all-to-all | bytes 327680 | tf_op jit(solution)/shard_map/all_to_all | solution.py:46
  127.4 1.8 broadcast_in_dim.10
  129.2 4.6 %all-to-all-start.4 = ((bf16[16,5,32,512]{3,2,1,0:T(8,128)(2,1)}), bf16[16,5,32,512]{3,2,1,0:T(8,128)(2,1)}, u32[]{:S(2)}, u32[]{:S(2)}) async-start(bf16[16,5,32,512]{3,2,1,0:T(8,128)(2,1)} %broadcast_in_dim.10), calls=%async_computation.4 | async-start | bytes 5242880 | tf_op jit(solution)/shard_map/all_to_all | solution.py:14
  133.8 43.8 %all-to-all-done.4 = bf16[16,5,32,512]{3,2,1,0:T(8,128)(2,1)} async-done(((bf16[16,5,32,512]{3,2,1,0:T(8,128)(2,1)}), bf16[16,5,32,512]{3,2,1,0:T(8,128)(2,1)}, u32[]{:S(2)}, u32[]{:S(2)}) %all-to-all-start.4) | async-done | bytes 2621472 | tf_op jit(solution)/shard_map/all_to_all | solution.py:14
  177.6 1.9 copy.39
  179.6 1.5 copy-done.1
  181.1 1.6 fusion.7
  182.7 7.9 %fusion.2 = f32[5,512,512]{2,1,0:T(8,128)} fusion(bf16[5,512,512]{2,1,0:T(8,128)(2,1)S(1)} %copy-done, bf16[5,512,512]{2,1,0:T(8,128)(2,1)} %bitcast.25, bf16[5,512,512]{2,1,0:T(8,128)(2,1)} %all-gather.2.cloned.1.call-done), kind=kOutput, calls=%fused_computation.3 | convolution fusion | flops 2685665280 | bytes 13107200 | tf_op jit(solution)/shard_map/crb,cbe->cre/dot_general | solution.py:62
  190.6 5.7 %fusion.4 = bf16[5,512,512]{2,1,0:T(8,128)(2,1)} fusion(bf16[5,512,512]{2,1,0:T(8,128)(2,1)S(1)} %copy-done, f32[5,512,512]{2,1,0:T(8,128)} %fusion.2, f32[5,512]{1,0:T(8,128)S(1)} %add_power_fusion), kind=kOutput, calls=%fused_computation.5 | convolution fusion | flops 1346109440 | bytes 10496000 | tf_op jit(solution)/shard_map/cre,cbe->crb/dot_general | solution.py:64
  196.3 1.5 fusion.8
  (19 shorter events, 0.1 us)
Async XLA Ops:
  7.2 175.6 %copy-start = (bf16[5,512,512]{2,1,0:T(8,128)(2,1)S(1)}, bf16[5,512,512]{2,1,0:T(8,128)(2,1)}, u32[]{:S(2)}) copy-start(bf16[5,512,512]{2,1,0:T(8,128)(2,1)} %param.10) | copy-start | bytes 7864324
  8.8 78.6 %copy-start.6 = (s32[128]{0:T(128)S(1)}, s32[128]{0:T(128)}, u32[]{:S(2)}) copy-start(s32[128]{0:T(128)} %param.8) | copy-start | bytes 1540
  83.0 8.1 %all-to-all-start.2 = ((bf16[4,16,16,128]{3,2,1,0:T(8,128)(2,1)}), bf16[4,16,16,128]{3,2,1,0:T(8,128)(2,1)S(1)}, u32[]{:S(2)}, u32[]{:S(2)}) async-start(bf16[4,16,16,128]{3,2,1,0:T(8,128)(2,1)} %broadcast_in_dim.7), calls=%async_computation.2 | async-start | bytes 524288 | tf_op jit(solution)/shard_map/all_to_all | solution.py:14
  86.7 96.0 %all-gather.2.cloned.1.call-start = ((), (), s32[]{:S(2)}) async-start(), calls=%async_computation.5 | async-start | bytes 2785280 | tf_op jit(solution)/shard_map/all_gather | solution.py:24
  129.2 4.6 %copy-start.5 = (f32[5,512]{1,0:T(8,128)S(1)}, f32[5,512]{1,0:T(8,128)}, u32[]{:S(2)}) copy-start(f32[5,512]{1,0:T(8,128)} %param.11) | copy-start | bytes 30724
  129.2 48.5 %all-to-all-start.4 = ((bf16[16,5,32,512]{3,2,1,0:T(8,128)(2,1)}), bf16[16,5,32,512]{3,2,1,0:T(8,128)(2,1)}, u32[]{:S(2)}, u32[]{:S(2)}) async-start(bf16[16,5,32,512]{3,2,1,0:T(8,128)(2,1)} %broadcast_in_dim.10), calls=%async_computation.4 | async-start | bytes 5242880 | tf_op jit(solution)/shard_map/all_to_all | solution.py:14
  133.8 47.3 %copy-start.3 = (f32[5,32,512]{2,1,0:T(8,128)S(1)}, f32[5,32,512]{2,1,0:T(8,128)}, u32[]{:S(2)}) copy-start(f32[5,32,512]{2,1,0:T(8,128)} %param.12) | copy-start | bytes 983044
  179.6 1.6 copy-start.1
  190.6 5.7 %copy-start.2 = (bf16[16,5,32,512]{3,2,0,1:T(8,128)(2,1)S(1)}, bf16[16,5,32,512]{3,2,0,1:T(8,128)(2,1)}, u32[]{:S(2)}) copy-start(bf16[16,5,32,512]{3,2,0,1:T(8,128)(2,1)} %copy-done.1) | copy-start | bytes 7864324
  190.6 5.7 %copy-start.4 = (f32[5,32,512]{2,1,0:T(8,128)S(1)}, f32[5,32,512]{2,1,0:T(8,128)}, u32[]{:S(2)}) copy-start(f32[5,32,512]{2,1,0:T(8,128)} %param.13) | copy-start | bytes 983044
Sparse Core Ops, SparseCore 0:
  91.8 85.5 all-gather.1

commit v2 on v1

--- a/solution.py
+++ b/solution.py
@@ -1,6 +1,8 @@
 import jax
 import jax.numpy as jnp
 from jax import lax
+from jax.experimental import pallas as pl
+from jax.experimental.pallas import tpu as pltpu
 from jax.sharding import Mesh, PartitionSpec as P
 
 decay_rate = 0.9
@@ -8,10 +10,89 @@
 NEAR = 4
 
 
-def broadcast_gather(x, axis):
-    n = lax.axis_size(axis)
+SIDE = 4
+ALL = ("dp", "far", "near")
+
+
+def broadcast_gather(x, axis, groups=None):
+    n = lax.axis_size(axis) if groups is None else len(groups[0])
     copies = jnp.broadcast_to(x[None], (n,) + x.shape)
-    return lax.all_to_all(copies, axis, split_axis=0, concat_axis=0, tiled=True)
+    return lax.all_to_all(
+        copies, axis, split_axis=0, concat_axis=0, tiled=True, axis_index_groups=groups
+    )
+
+
+def side_groups(n_dp, n_opt, parity):
+    groups = []
+    for opt in range(n_opt):
+        for fixed in range(SIDE):
+            along_x = [(v * SIDE + fixed) * n_opt + opt for v in range(SIDE)]
+            along_y = [(fixed * SIDE + v) * n_opt + opt for v in range(SIDE)]
+            groups.append(along_x if opt % 2 == parity else along_y)
+    return groups
+
+
+def contract(a, b, dim_a, dim_b):
+    return lax.dot_general(
+        a, b, (((dim_a,), (dim_b,)), ((), ())), preferred_element_type=jnp.float32
+    )
+
+
+def slot_kernel(where, recv, root, basis, factor, left, right, update, left_new, right_new, g, gram):
+    my_dp, core = where[0], where[1]
+    rows = left.shape[1]
+    for d in range(SIDE * SIDE):
+        x, y = d // SIDE, d % SIDE
+        first = jnp.where(core == 0, y, x)
+        second = jnp.where(core == 0, x, y)
+        g[d * rows : (d + 1) * rows, :] = recv[first, second, 0]
+    block = g[...]
+    applied = contract(root[0], block, 1, 0).astype(jnp.bfloat16)
+    own = g[pl.ds(pl.multiple_of(my_dp * rows, rows), rows), :]
+    left_new[0] = decay_rate * left[0] + (1.0 - decay_rate) * contract(own, block, 1, 1)
+    group = 128 // rows
+    lanes = pl.ds(pl.multiple_of(my_dp // group * 128, 128), 128)
+    gram[...] = contract(g[:, lanes], block, 0, 0)
+    mine = gram[pl.ds(pl.multiple_of(my_dp % group * rows, rows), rows), :]
+    right_new[0] = decay_rate * right[0] + (1.0 - decay_rate) * mine
+    scaled = (contract(applied, basis[0], 1, 0) * factor[0]).astype(jnp.bfloat16)
+    update[0] = contract(scaled, basis[0], 1, 1).astype(jnp.bfloat16)
+
+
+def slot_step(where, recv, root, basis, factor, left, right):
+    cap, width, _ = basis.shape
+    rows = left.shape[1]
+    whole = pl.BlockSpec((1, width, width), lambda s, w: (s, 0, 0))
+    slab = pl.BlockSpec((1, rows, width), lambda s, w: (s, 0, 0))
+    return pl.pallas_call(
+        slot_kernel,
+        grid_spec=pltpu.PrefetchScalarGridSpec(
+            num_scalar_prefetch=1,
+            grid=(cap,),
+            in_specs=[
+                pl.BlockSpec((SIDE, SIDE, 1, rows, width), lambda s, w: (0, 0, s, 0, 0)),
+                whole,
+                whole,
+                pl.BlockSpec((1, 1, width), lambda s, w: (s, 0, 0)),
+                slab,
+                slab,
+            ],
+            out_specs=[whole, slab, slab],
+            scratch_shapes=[
+                pltpu.VMEM((width, width), jnp.bfloat16),
+                pltpu.VMEM((128, width), jnp.float32),
+            ],
+        ),
+        out_shape=[
+            jax.ShapeDtypeStruct(basis.shape, jnp.bfloat16),
+            jax.ShapeDtypeStruct(left.shape, jnp.float32),
+            jax.ShapeDtypeStruct(right.shape, jnp.float32),
+        ],
+        compiler_params=pltpu.CompilerParams(vmem_limit_bytes=32 * 1024 * 1024),
+        cost_estimate=pl.CostEstimate(
+            flops=7 * cap * width**3, bytes_accessed=10 * cap * width**2, transcendentals=0
+        ),
+    )(where, recv, root, basis, factor, left, right)
 
 
 def body(gradients, owner_map, left_root, right_basis, right_eigen, left_stat, right_stat):
@@ -47,23 +128,17 @@
 
     owned = arrived.reshape(row_tiles, col_tiles, cap, 8, 128)
     owned = owned.transpose(2, 0, 3, 1, 4).reshape(cap, rows, width)
-    gathered = broadcast_gather(owned, "dp").transpose(1, 0, 2, 3).reshape(cap, width, width)
+    n_opt = n_far * n_near
+    line = broadcast_gather(owned, ALL, side_groups(n_dp, n_opt, 0))
+    line, root = lax.optimization_barrier((line, root))
+    recv = broadcast_gather(line, ALL, side_groups(n_dp, n_opt, 1))
+    recv = recv.reshape(SIDE, SIDE, cap, rows, width)
 
-    left_gram = jnp.einsum("crb,cnb->crn", owned, gathered, preferred_element_type=jnp.float32)
-    my_columns = lax.dynamic_slice_in_dim(gathered, my_dp * rows, rows, 2)
-    right_gram = jnp.einsum("cnr,cnb->crb", my_columns, gathered, preferred_element_type=jnp.float32)
-    left_new = decay_rate * left_stat + (1.0 - decay_rate) * left_gram
-    right_new = decay_rate * right_stat + (1.0 - decay_rate) * right_gram
-
-    applied = jnp.einsum(
-        "crn,cnb->crb", root, gathered, preferred_element_type=jnp.float32
-    ).astype(jnp.bfloat16)
     factor = (right_eigen + epsilon) ** (-0.25)
-    scaled = jnp.einsum("crb,cbe->cre", applied, right_basis, preferred_element_type=jnp.float32)
-    scaled = (scaled * factor[:, None, :]).astype(jnp.bfloat16)
-    update = jnp.einsum(
-        "cre,cbe->crb", scaled, right_basis, preferred_element_type=jnp.float32
-    ).astype(jnp.bfloat16)
+    where = jnp.stack([my_dp, my_near % 2]).astype(jnp.int32)
+    update, left_new, right_new = slot_step(
+        where, recv, root, right_basis, factor[:, None, :], left_stat, right_stat
+    )
     return (update, left_new, right_new)
 
 

time: 205 us -> 183 us (0.89)
  the two profiles are of different devices: /device:TPU:96 before, /device:TPU:64 now
where the time goes in v2:
time: 183 us
  blocking collectives  94.5 us (52%)
  waiting for transfers between devices  42.2 us (23%)
  starting transfers between devices  14.4 us (8%)
  between operations  14.2 us (8%)
  local copies, waits for them, and re-layouts  9.12 us (5%)
  Pallas kernels  7.61 us (4%)
    all_to_all x1, blocking collectives, body(): lax.all_to_all(summed, 'far', split_axis=0, concat_axis=0, tiled=True)  48.7 us
    all_to_all x1, blocking collectives, body(): lax.all_to_all(deliver, 'far', split_axis=0, concat_axis=0, tiled=True)  34.6 us
    all_to_all x2, waiting for transfers between devices, broadcast_gather(): lax.all_to_all(copies, axis, split_axis=0, concat_axis=0, tiled=True, axi...  24.6 us
    all_to_all x1, waiting for transfers between devices, body(): parts = lax.all_to_all(sent, 'dp', split_axis=0, concat_axis=0, tiled=True)  17 us
    all_to_all x1, blocking collectives, broadcast_gather(): lax.all_to_all(copies, axis, split_axis=0, concat_axis=0, tiled=True, axi...  11.2 us
    pallas_call x1, Pallas kernels, slot_step(): pl.pallas_call(slot_kernel, grid_spec=pltpu.PrefetchScalarGridSpec(num_sc...  7.61 us
    all_to_all x2, starting transfers between devices, broadcast_gather(): lax.all_to_all(copies, axis, split_axis=0, concat_axis=0, tiled=True, axi...  7.19 us
    all_to_all x1, starting transfers between devices, body(): parts = lax.all_to_all(sent, 'dp', split_axis=0, concat_axis=0, tiled=True)  7.17 us
  transfers between devices with their start and end apart: 4, of which 3 were waited for; matrix products, arithmetic and copies ran while one was open for 1% of the time, Pallas kernels for 0%

profile of v2, /device:TPU:64, one launch (start us, length us, event | category | flops | bytes accessed | tf_op | source)
XLA Modules:
  0.0 182.6 jit_solution(7275279536167715974)
XLA Ops:
  7.2 2.5 %copy.18 = bf16[16,4,4,2,8,128]{5,4,3,2,1,0:T(8,128)(2,1)} copy(bf16[16,4,4,2,8,128]{5,4,2,1,0,3:T(8,128)(2,1)} %bitcast.16) | data formatting | bytes 2097152 | tf_op jit(solution)/shard_map/transpose | solution.py:108
  9.6 7.2 %all-to-all-start = ((bf16[16,16,16,128]{3,2,1,0:T(8,128)(2,1)}), bf16[16,16,16,128]{3,2,1,0:T(8,128)(2,1)S(1)}, u32[]{:S(2)}, u32[]{:S(2)}) async-start(bf16[16,16,16,128]{3,2,1,0:T(8,128)(2,1)} %bitcast.5), calls=%async_computation | async-start | bytes 2097152 | tf_op jit(solution)/shard_map/all_to_all | solution.py:109
  16.9 0.7 all-gather.2.cloned.1.call-update
  17.6 17.0 %all-to-all-done = bf16[16,16,16,128]{3,2,1,0:T(8,128)(2,1)S(1)} async-done(((bf16[16,16,16,128]{3,2,1,0:T(8,128)(2,1)}), bf16[16,16,16,128]{3,2,1,0:T(8,128)(2,1)S(1)}, u32[]{:S(2)}, u32[]{:S(2)}) %all-to-all-start) | async-done | bytes 1048608 | tf_op jit(solution)/shard_map/all_to_all | solution.py:109
  34.5 0.1 reduce_sum.22
  34.7 48.7 %all_to_all.30 = bf16[16,16,128]{2,1,0:T(8,128)(2,1)S(1)} all-to-all(bf16[16,16,128]{2,1,0:T(8,128)(2,1)S(1)} %reduce_sum.22), channel_id=1, replica_groups=mesh['dp'=16,'far'=16,'near'=4] {'far'}, dimensions={0} | all-to-all | bytes 131072 | tf_op jit(solution)/shard_map/all_to_all | solution.py:112
  83.3 0.7 broadcast_in_dim.12
  84.1 3.4 %all-to-all-start.2 = ((bf16[4,16,16,128]{3,2,1,0:T(8,128)(2,1)}), bf16[4,16,16,128]{3,2,1,0:T(8,128)(2,1)S(1)}, u32[]{:S(2)}, u32[]{:S(2)}) async-start(bf16[4,16,16,128]{3,2,1,0:T(8,128)(2,1)} %broadcast_in_dim.12), calls=%async_computation.2 | async-start | bytes 524288 | tf_op jit(solution)/shard_map/all_to_all | solution.py:20
  87.5 0.2 convert_reduce_fusion
  87.7 0.2 reshape.27
  87.9 0.1 eq.44
  88.0 5.5 %all-to-all-done.2 = bf16[4,16,16,128]{3,2,1,0:T(8,128)(2,1)S(1)} async-done(((bf16[4,16,16,128]{3,2,1,0:T(8,128)(2,1)}), bf16[4,16,16,128]{3,2,1,0:T(8,128)(2,1)S(1)}, u32[]{:S(2)}, u32[]{:S(2)}) %all-to-all-start.2) | async-done | bytes 262176 | tf_op jit(solution)/shard_map/all_to_all | solution.py:20
  93.5 0.1 reshape_reshape.3
  93.6 0.2 convolution_convert_fusion
  93.8 0.1 reshape.30
  93.9 34.6 %all_to_all.31 = bf16[16,40,128]{2,1,0:T(8,128)(2,1)S(1)} all-to-all(bf16[16,40,128]{2,1,0:T(8,128)(2,1)S(1)} %reshape.30), channel_id=1, replica_groups=mesh['dp'=16,'far'=16,'near'=4] {'far'}, dimensions={0} | all-to-all | bytes 327680 | tf_op jit(solution)/shard_map/all_to_all | solution.py:127
  128.6 11.2 %all_to_all.32 = bf16[4,5,32,512]{3,2,1,0:T(8,128)(2,1)S(1)} all-to-all(bf16[4,5,32,512]{3,2,1,0:T(8,128)(2,1)S(1)} %broadcast_in_dim.14), channel_id=1, replica_groups={{0,256,512,768},{64,320,576,832},{128,384,640,896},{192,448,704,960},{1..., dimensions={0} | all-to-all | bytes 1310720 | tf_op jit(solution)/shard_map/all_to_all | solution.py:20
  139.8 1.8 broadcast_in_dim.15
  141.6 3.8 %all-to-all-start.5 = ((bf16[4,4,5,32,512]{4,3,2,1,0:T(8,128)(2,1)}), bf16[4,4,5,32,512]{4,3,2,1,0:T(8,128)(2,1)S(1)}, u32[]{:S(2)}, u32[]{:S(2)}) async-start(bf16[4,4,5,32,512]{4,3,2,1,0:T(8,128)(2,1)} %broadcast_in_dim.15), calls=%async_computation.5 | async-start | bytes 5242880 | tf_op jit(solution)/shard_map/all_to_all | solution.py:20
  145.5 0.1 pad_add_fusion.where
  145.6 19.1 %all-to-all-done.5.recv = bf16[4,4,5,32,512]{4,3,2,1,0:T(8,128)(2,1)S(1)} async-done(((bf16[4,4,5,32,512]{4,3,2,1,0:T(8,128)(2,1)}), bf16[4,4,5,32,512]{4,3,2,1,0:T(8,128)(2,1)S(1)}, u32[]{:S(2)}, u32[]{:S(2)}) %all-to-all-start.5) | async-done | bytes 2621472 | tf_op jit(solution)/shard_map/all_to_all | solution.py:20
  164.7 1.7 copy-done
  166.4 1.7 copy-done.1
  168.2 7.6 %shard_map.94 = (bf16[5,512,512]{2,1,0:T(8,128)(2,1)}, f32[5,32,512]{2,1,0:T(8,128)}, f32[5,32,512]{2,1,0:T(8,128)}) custom-call(s32[2]{0:T(128)S(1)} %pad_add_fusion.where, bf16[4,4,5,32,512]{4,3,2,1,0:T(8,128)(2,1)S(1)} %all-to-all-done.5.recv, bf16[5,512,512]{2,1,0:T(8,128)(2,1)S(1)} %copy-done.1, bf16[5,512,512]{2,1,0:T(8,128)(2,1)S(1)} %copy-done, ...), custom_call_target="tpu_custom_call" | custom-call | flops 4697620480 | bytes 13107200 | tf_op jit(solution)/shard_map/pallas_call | solution.py:67
  (18 shorter events, 0.2 us)
Async XLA Ops:
  9.6 77.9 %copy-start.5 = (s32[128]{0:T(128)S(1)}, s32[128]{0:T(128)}, u32[]{:S(2)}) copy-start(s32[128]{0:T(128)} %param.8) | copy-start | bytes 1540
  9.6 24.9 %all-to-all-start = ((bf16[16,16,16,128]{3,2,1,0:T(8,128)(2,1)}), bf16[16,16,16,128]{3,2,1,0:T(8,128)(2,1)S(1)}, u32[]{:S(2)}, u32[]{:S(2)}) async-start(bf16[16,16,16,128]{3,2,1,0:T(8,128)(2,1)} %bitcast.5), calls=%async_computation | async-start | bytes 2097152 | tf_op jit(solution)/shard_map/all_to_all | solution.py:109
  16.8 123.0 %all-gather.2.cloned.1.call-start = ((), (), s32[]{:S(2)}) async-start(), calls=%async_computation.6 | async-start | bytes 2785280 | tf_op jit(solution)/shard_map/all_gather | solution.py:105
  84.1 9.4 %all-to-all-start.2 = ((bf16[4,16,16,128]{3,2,1,0:T(8,128)(2,1)}), bf16[4,16,16,128]{3,2,1,0:T(8,128)(2,1)S(1)}, u32[]{:S(2)}, u32[]{:S(2)}) async-start(bf16[4,16,16,128]{3,2,1,0:T(8,128)(2,1)} %broadcast_in_dim.12), calls=%async_computation.2 | async-start | bytes 524288 | tf_op jit(solution)/shard_map/all_to_all | solution.py:20
  141.6 3.8 %copy-start.4 = (f32[5,512]{1,0:T(8,128)S(1)}, f32[5,512]{1,0:T(8,128)}, u32[]{:S(2)}) copy-start(f32[5,512]{1,0:T(8,128)} %param.11) | copy-start | bytes 30724
  141.6 23.1 %copy-start.2 = (f32[5,32,512]{2,1,0:T(8,128)S(1)}, f32[5,32,512]{2,1,0:T(8,128)}, u32[]{:S(2)}) copy-start(f32[5,32,512]{2,1,0:T(8,128)} %left.1) | copy-start | bytes 983044
  141.6 23.1 %copy-start.3 = (f32[5,32,512]{2,1,0:T(8,128)S(1)}, f32[5,32,512]{2,1,0:T(8,128)}, u32[]{:S(2)}) copy-start(f32[5,32,512]{2,1,0:T(8,128)} %right.1) | copy-start | bytes 983044
  141.6 23.1 %all-to-all-start.5 = ((bf16[4,4,5,32,512]{4,3,2,1,0:T(8,128)(2,1)}), bf16[4,4,5,32,512]{4,3,2,1,0:T(8,128)(2,1)S(1)}, u32[]{:S(2)}, u32[]{:S(2)}) async-start(bf16[4,4,5,32,512]{4,3,2,1,0:T(8,128)(2,1)} %broadcast_in_dim.15), calls=%async_computation.5 | async-start | bytes 5242880 | tf_op jit(solution)/shard_map/all_to_all | solution.py:20
  164.7 1.7 copy-start
  166.4 1.7 copy-start.1
Sparse Core Ops, SparseCore 0:
  21.9 89.1 all-gather.1

commit v3 on v2

v3 whole, which is shorter than its diff:
```python
import jax
import jax.numpy as jnp
from jax import lax
from jax.experimental import pallas as pl
from jax.experimental.pallas import tpu as pltpu
from jax.sharding import Mesh, PartitionSpec as P

decay_rate = 0.9
epsilon = 1e-06
CORES = 2
SIDE = 4
ALL = ("dp", "z", "core")
EVEN = ((0, 1), (2, 3))
ODD = ((1, 2), (0, 3))


def broadcast_gather(x, axis, groups=None):
    n = lax.axis_size(axis) if groups is None else len(groups[0])
    copies = jnp.broadcast_to(x[None], (n,) + x.shape)
    return lax.all_to_all(
        copies, axis, split_axis=0, concat_axis=0, tiled=True, axis_index_groups=groups
    )


def quads(n_opt, parity):
    groups = []
    for opt in range(n_opt):
        pairs = EVEN if opt % CORES == parity else ODD
        for across in pairs:
            for along in pairs:
                groups.append([(x * SIDE + y) * n_opt + opt for x in across for y in along])
    return groups


def contract(a, b, dim_a, dim_b):
    return lax.dot_general(
        a, b, (((dim_a,), (dim_b,)), ((), ())), preferred_element_type=jnp.float32
    )


def slot_kernel(where, recv, root, basis, factor, left, right, update, left_new, right_new, g, gram):
    my_dp, core = where[0], where[1]
    rows = left.shape[1]
    flip_x = my_dp // SIDE // 2 == 0
    flip_y = my_dp % SIDE // 2 == 0
    for d in range(SIDE * SIDE):
        x, y = d // SIDE, d % SIDE
        outer_x, outer_y = int(x in (0, 3)), int(y in (0, 3))
        odd_x = jnp.where(flip_x, 1 - outer_x, outer_x)
        odd_y = jnp.where(flip_y, 1 - outer_y, outer_y)
        high = x // 2 * 2 + y // 2
        first = jnp.where(core == 0, high, odd_x * 2 + odd_y)
        second = jnp.where(core == 0, x % 2 * 2 + y % 2, high)
        g[d * rows : (d + 1) * rows, :] = recv[first, second, 0]
    block = g[...]
    applied = contract(root[0], block, 1, 0).astype(jnp.bfloat16)
    own = g[pl.ds(pl.multiple_of(my_dp * rows, rows), rows), :]
    left_new[0] = decay_rate * left[0] + (1.0 - decay_rate) * contract(own, block, 1, 1)
    group = 128 // rows
    lanes = pl.ds(pl.multiple_of(my_dp // group * 128, 128), 128)
    gram[...] = contract(g[:, lanes], block, 0, 0)
    mine = gram[pl.ds(pl.multiple_of(my_dp % group * rows, rows), rows), :]
    right_new[0] = decay_rate * right[0] + (1.0 - decay_rate) * mine
    scaled = (contract(applied, basis[0], 1, 0) * factor[0]).astype(jnp.bfloat16)
    update[0] = contract(scaled, basis[0], 1, 1).astype(jnp.bfloat16)


def slot_step(where, recv, root, basis, factor, left, right):
    cap, width, _ = basis.shape
    rows = left.shape[1]
    whole = pl.BlockSpec((1, width, width), lambda s, w: (s, 0, 0))
    slab = pl.BlockSpec((1, rows, width), lambda s, w: (s, 0, 0))
    return pl.pallas_call(
        slot_kernel,
        grid_spec=pltpu.PrefetchScalarGridSpec(
            num_scalar_prefetch=1,
            grid=(cap,),
            in_specs=[
                pl.BlockSpec((4, 4, 1, rows, width), lambda s, w: (0, 0, s, 0, 0)),
                whole,
                whole,
                pl.BlockSpec((1, 1, width), lambda s, w: (s, 0, 0)),
                slab,
                slab,
            ],
            out_specs=[whole, slab, slab],
            scratch_shapes=[
                pltpu.VMEM((width, width), jnp.bfloat16),
                pltpu.VMEM((128, width), jnp.float32),
            ],
        ),
        out_shape=[
            jax.ShapeDtypeStruct(basis.shape, jnp.bfloat16),
            jax.ShapeDtypeStruct(left.shape, jnp.float32),
            jax.ShapeDtypeStruct(right.shape, jnp.float32),
        ],
        compiler_params=pltpu.CompilerParams(vmem_limit_bytes=56 * 1024 * 1024),
        cost_estimate=pl.CostEstimate(
            flops=7 * cap * width**3, bytes_accessed=10 * cap * width**2, transcendentals=0
        ),
    )(where, recv, root, basis, factor, left, right)


def body(gradients, owner_map, left_root, right_basis, right_eigen, left_stat, right_stat):
    n_dp, n_z = lax.axis_size("dp"), lax.axis_size("z")
    _, blocks, width, _ = gradients.shape
    cap, rows, _ = left_stat.shape
    my_dp, my_core = lax.axis_index("dp"), lax.axis_index("core")
    row_tiles, col_tiles = rows // 8, width // 128

    root = lax.all_gather(left_root, "dp", axis=1, tiled=True)

    sent = gradients.reshape(blocks, n_dp, rows, width).transpose(1, 0, 2, 3)
    parts = lax.all_to_all(sent, "dp", split_axis=0, concat_axis=0, tiled=True)
    summed = jnp.sum(parts.astype(jnp.float32), axis=0).astype(jnp.bfloat16)

    summed = summed.reshape(blocks, row_tiles, 2, 4, col_tiles, 128)
    pieces = summed.transpose(1, 4, 2, 0, 3, 5).reshape(n_z, blocks * 4, 128)
    spread = lax.all_to_all(pieces, "z", split_axis=0, concat_axis=0, tiled=True)
    swapped = lax.ppermute(spread, "core", [(0, 1), (1, 0)])
    held = jnp.concatenate([t.reshape(n_z * blocks, 4 * 128) for t in (spread, swapped)])

    same = owner_map[:, None] == owner_map[None, :]
    order = jnp.arange(owner_map.shape[0], dtype=jnp.int32)
    slot = jnp.sum((same & (order[None, :] < order[:, None])).astype(jnp.int32), axis=1)
    place = jnp.where(owner_map % CORES == my_core, owner_map // CORES * cap + slot, -1)
    place = place.reshape(n_z, CORES, blocks)
    first, second = place[:, 0].reshape(-1), place[:, 1].reshape(-1)
    place = jnp.concatenate(
        [jnp.where(my_core == 0, first, second), jnp.where(my_core == 0, second, first)]
    )
    pick = (jnp.arange(n_z * cap, dtype=jnp.int32)[:, None] == place[None, :]).astype(jnp.bfloat16)
    chosen = jnp.dot(pick, held, preferred_element_type=jnp.float32).astype(jnp.bfloat16)
    deliver = chosen.reshape(n_z, cap, 4, 128)
    arrived = lax.all_to_all(deliver, "z", split_axis=0, concat_axis=0, tiled=True)

    owned = arrived.reshape(row_tiles, col_tiles, 2, cap, 4, 128)
    owned = owned.transpose(3, 0, 2, 4, 1, 5).reshape(cap, rows, width)
    n_opt = n_z * CORES
    factor = (right_eigen + epsilon) ** (-0.25)
    where = jnp.stack([my_dp, my_core]).astype(jnp.int32)
    line = broadcast_gather(owned, ALL, quads(n_opt, 0))
    line, root, factor, where = lax.optimization_barrier((line, root, factor, where))
    recv = broadcast_gather(line, ALL, quads(n_opt, 1))

    update, left_new, right_new = slot_step(
        where, recv, root, right_basis, factor[:, None, :], left_stat, right_stat
    )
    return (update, left_new, right_new)


def solution(mesh):
    n_dp, n_opt = mesh.devices.shape
    inner = Mesh(mesh.devices.reshape(n_dp, n_opt // CORES, CORES), ALL)
    opt = ("z", "core")
    in_specs = (
        P("dp", opt, None, None),
        P(),
        P(opt, "dp", None),
        P(opt, None, None),
        P(opt, None),
        P(opt, "dp", None),
        P(opt, "dp", None),
    )
    out_specs = (P(opt, None, None), P(opt, "dp", None), P(opt, "dp", None))
    return jax.shard_map(body, mesh=inner, in_specs=in_specs, out_specs=out_specs, check_vma=False)
```

time: 183 us -> 183 us (level)
  the two profiles are of different devices: /device:TPU:64 before, /device:TPU:1 now
where the time goes in v3:
time: 183 us; the launch traced here: 180 us
  blocking collectives  55.2 us (30%)
  waiting for transfers between devices  47.6 us (26%)
  starting transfers between devices  45 us (25%)
  between operations  14.2 us (8%)
  Pallas kernels  9.61 us (5%)
  local copies, waits for them, and re-layouts  7.49 us (4%)
    all_to_all x1, blocking collectives, body(): lax.all_to_all(deliver, 'z', split_axis=0, concat_axis=0, tiled=True)  36.1 us
    all_to_all x1, starting transfers between devices, body(): lax.all_to_all(pieces, 'z', split_axis=0, concat_axis=0, tiled=True)  32.6 us
    all_to_all x2, waiting for transfers between devices, broadcast_gather(): lax.all_to_all(copies, axis, split_axis=0, concat_axis=0, tiled=True, axi...  23.4 us
    all_to_all x1, waiting for transfers between devices, body(): lax.all_to_all(pieces, 'z', split_axis=0, concat_axis=0, tiled=True)  22.8 us
    all_to_all x1, blocking collectives, body(): parts = lax.all_to_all(sent, 'dp', split_axis=0, concat_axis=0, tiled=True)  19.1 us
    pallas_call x1, Pallas kernels, slot_step(): pl.pallas_call(slot_kernel, grid_spec=pltpu.PrefetchScalarGridSpec(num_sc...  9.61 us
    all_to_all x2, starting transfers between devices, broadcast_gather(): lax.all_to_all(copies, axis, split_axis=0, concat_axis=0, tiled=True, axi...  7.14 us
    ppermute x1, starting transfers between devices, body(): swapped = lax.ppermute(spread, 'core', [(0, 1), (1, 0)])  5.3 us
  transfers between devices with their start and end apart: 5, of which 4 were waited for; matrix products, arithmetic and copies ran while one was open for 3% of the time, Pallas kernels for 0%

profile of v3, /device:TPU:1, one launch (start us, length us, event | category | flops | bytes accessed | tf_op | source)
XLA Modules:
  0.0 180.4 jit_solution(6714945492943682945)
XLA Ops:
  7.2 0.7 all-gather.2.cloned.1.call-update
  7.9 1.3 copy.19
  9.2 19.1 %all_to_all.25 = bf16[16,2,32,512]{3,2,1,0:T(8,128)(2,1)S(1)} all-to-all(bf16[16,2,32,512]{3,2,1,0:T(8,128)(2,1)S(1)} %copy.19), channel_id=1, replica_groups=mesh['dp'=16,'z'=32,'core'=2] {'dp'}, dimensions={0} | all-to-all | bytes 2097152 | tf_op jit(solution)/shard_map/all_to_all | solution.py:114
  28.4 0.1 reduce_sum.22
  28.5 0.7 copy.20
  29.2 32.6 %all-to-all-start.1 = ((bf16[32,8,128]{2,1,0:T(8,128)(2,1)}), bf16[32,8,128]{2,1,0:T(8,128)(2,1)S(1)}, u32[]{:S(2)}, u32[]{:S(2)}) async-start(bf16[32,8,128]{2,1,0:T(8,128)(2,1)} %bitcast.3), calls=%async_computation.1 | async-start | bytes 131072 | tf_op jit(solution)/shard_map/all_to_all | solution.py:119
  61.8 0.2 convert_reduce_fusion
  62.0 0.2 reshape.39
  62.4 0.1 select_n.41
  62.5 22.8 %all-to-all-done.1 = bf16[32,8,128]{2,1,0:T(8,128)(2,1)S(1)} async-done(((bf16[32,8,128]{2,1,0:T(8,128)(2,1)}), bf16[32,8,128]{2,1,0:T(8,128)(2,1)S(1)}, u32[]{:S(2)}, u32[]{:S(2)}) %all-to-all-start.1) | async-done | bytes 65568 | tf_op jit(solution)/shard_map/all_to_all | solution.py:119
  85.2 5.3 %collective-permute-start = (bf16[32,8,128]{2,1,0:T(8,128)(2,1)S(1)}, bf16[32,8,128]{2,1,0:T(8,128)(2,1)S(1)}, u32[]{:S(2)}, u32[]{:S(2)}) collective-permute-start(bf16[32,8,128]{2,1,0:T(8,128)(2,1)S(1)} %all-to-all-done.1), channel_id=1, source_target_pairs={{0,1},{1,0},{2,3},{3,2},{4,5},{5,4},{6,7},{7,6},{8,9},{9,8},{10,11... | collective-permute-start | bytes 196616 | tf_op jit(solution)/shard_map/ppermute | solution.py:120
  90.7 0.8 collective-permute-done
  91.5 0.2 convolution_convert_fusion
  91.7 36.1 %all_to_all.26 = bf16[32,5,4,128]{3,2,1,0:T(4,128)(2,1)S(1)} all-to-all(bf16[32,5,4,128]{3,2,1,0:T(4,128)(2,1)S(1)} %reshape.45), channel_id=1, replica_groups=mesh['dp'=16,'z'=32,'core'=2] {'z'}, dimensions={0} | all-to-all | bytes 327680 | tf_op jit(solution)/shard_map/all_to_all | solution.py:135
  127.9 0.9 broadcast_in_dim.11
  128.8 3.5 %all-to-all-start.3 = ((bf16[4,5,32,512]{3,2,1,0:T(8,128)(2,1)}), bf16[4,5,32,512]{3,2,1,0:T(8,128)(2,1)S(1)}, u32[]{:S(2)}, u32[]{:S(2)}) async-start(bf16[4,5,32,512]{3,2,1,0:T(8,128)(2,1)} %broadcast_in_dim.11), calls=%async_computation.3 | async-start | bytes 1310720 | tf_op jit(solution)/shard_map/all_to_all | solution.py:20
  132.3 0.6 pad_add_fusion.1.where
  133.0 7.0 %all-to-all-done.3 = bf16[4,5,32,512]{3,2,1,0:T(8,128)(2,1)S(1)} async-done(((bf16[4,5,32,512]{3,2,1,0:T(8,128)(2,1)}), bf16[4,5,32,512]{3,2,1,0:T(8,128)(2,1)S(1)}, u32[]{:S(2)}, u32[]{:S(2)}) %all-to-all-start.3) | async-done | bytes 655392 | tf_op jit(solution)/shard_map/all_to_all | solution.py:20
  140.0 1.8 %broadcast_in_dim.12 = bf16[4,4,5,32,512]{4,3,2,1,0:T(8,128)(2,1)} broadcast(bf16[4,5,32,512]{3,2,1,0:T(8,128)(2,1)S(1)} %all-to-all-done.3), dimensions={1,2,3,4} | broadcast | bytes 3276800 | tf_op jit(solution)/shard_map/broadcast_in_dim | solution.py:19
  141.8 3.7 %all-to-all-start.4 = ((bf16[4,4,5,32,512]{4,3,2,1,0:T(8,128)(2,1)}), bf16[4,4,5,32,512]{4,3,2,1,0:T(8,128)(2,1)S(1)}, u32[]{:S(2)}, u32[]{:S(2)}) async-start(bf16[4,4,5,32,512]{4,3,2,1,0:T(8,128)(2,1)} %broadcast_in_dim.12), calls=%async_computation.4 | async-start | bytes 5242880 | tf_op jit(solution)/shard_map/all_to_all | solution.py:20
  145.5 0.6 broadcast_in_dim.13.factor
  146.1 16.4 %all-to-all-done.4.recv = bf16[4,4,5,32,512]{4,3,2,1,0:T(8,128)(2,1)S(1)} async-done(((bf16[4,4,5,32,512]{4,3,2,1,0:T(8,128)(2,1)}), bf16[4,4,5,32,512]{4,3,2,1,0:T(8,128)(2,1)S(1)}, u32[]{:S(2)}, u32[]{:S(2)}) %all-to-all-start.4) | async-done | bytes 2621472 | tf_op jit(solution)/shard_map/all_to_all | solution.py:20
  162.5 1.5 copy-done
  164.0 9.6 %shard_map.94 = (bf16[5,512,512]{2,1,0:T(8,128)(2,1)}, f32[5,32,512]{2,1,0:T(8,128)}, f32[5,32,512]{2,1,0:T(8,128)}) custom-call(s32[2]{0:T(128)} %pad_add_fusion.1.where, bf16[4,4,5,32,512]{4,3,2,1,0:T(8,128)(2,1)} %copy-done, bf16[5,512,512]{2,1,0:T(8,128)(2,1)} %all-gather.2.cloned.1.call-done.root, bf16[5,512,512]{2,1,0:T(8,128)(2,1)} %basis.1, ...), custom_call_target="tpu_custom_call" | custom-call | flops 4697620480 | bytes 13107200 | tf_op jit(solution)/shard_map/pallas_call | solution.py:73
  (18 shorter events, 0.7 us)
Async XLA Ops:
  7.2 132.8 %all-gather.2.cloned.1.call-start = ((), (), s32[]{:S(2)}) async-start(), calls=%async_computation.5 | async-start | bytes 2785280 | tf_op jit(solution)/shard_map/all_gather | solution.py:111
  7.9 53.9 %copy-start.2 = (s32[128]{0:T(128)S(1)}, s32[128]{0:T(128)}, u32[]{:S(2)}) copy-start(s32[128]{0:T(128)} %param.8) | copy-start | bytes 1540
  28.4 104.6 %copy-start.1 = (f32[5,512]{1,0:T(8,128)S(1)}, f32[5,512]{1,0:T(8,128)}, u32[]{:S(2)}) copy-start(f32[5,512]{1,0:T(8,128)} %param.11) | copy-start | bytes 30724
  29.2 56.0 %all-to-all-start.1 = ((bf16[32,8,128]{2,1,0:T(8,128)(2,1)}), bf16[32,8,128]{2,1,0:T(8,128)(2,1)S(1)}, u32[]{:S(2)}, u32[]{:S(2)}) async-start(bf16[32,8,128]{2,1,0:T(8,128)(2,1)} %bitcast.3), calls=%async_computation.1 | async-start | bytes 131072 | tf_op jit(solution)/shard_map/all_to_all | solution.py:119
  85.2 6.2 %collective-permute-start = (bf16[32,8,128]{2,1,0:T(8,128)(2,1)S(1)}, bf16[32,8,128]{2,1,0:T(8,128)(2,1)S(1)}, u32[]{:S(2)}, u32[]{:S(2)}) collective-permute-start(bf16[32,8,128]{2,1,0:T(8,128)(2,1)S(1)} %all-to-all-done.1), channel_id=1, source_target_pairs={{0,1},{1,0},{2,3},{3,2},{4,5},{5,4},{6,7},{7,6},{8,9},{9,8},{10,11... | collective-permute-start | bytes 196616 | tf_op jit(solution)/shard_map/ppermute | solution.py:120
  128.8 11.2 %all-to-all-start.3 = ((bf16[4,5,32,512]{3,2,1,0:T(8,128)(2,1)}), bf16[4,5,32,512]{3,2,1,0:T(8,128)(2,1)S(1)}, u32[]{:S(2)}, u32[]{:S(2)}) async-start(bf16[4,5,32,512]{3,2,1,0:T(8,128)(2,1)} %broadcast_in_dim.11), calls=%async_computation.3 | async-start | bytes 1310720 | tf_op jit(solution)/shard_map/all_to_all | solution.py:20
  141.8 20.6 %all-to-all-start.4 = ((bf16[4,4,5,32,512]{4,3,2,1,0:T(8,128)(2,1)}), bf16[4,4,5,32,512]{4,3,2,1,0:T(8,128)(2,1)S(1)}, u32[]{:S(2)}, u32[]{:S(2)}) async-start(bf16[4,4,5,32,512]{4,3,2,1,0:T(8,128)(2,1)} %broadcast_in_dim.12), calls=%async_computation.4 | async-start | bytes 5242880 | tf_op jit(solution)/shard_map/all_to_all | solution.py:20
  162.5 1.5 copy-start
Sparse Core Ops, SparseCore 0:
  12.2 90.1 all-gather.1

commit v4 on v3

--- a/solution.py
+++ b/solution.py
@@ -22,14 +22,28 @@
     )
 
 
-def quads(n_opt, parity):
+def quads(n_opt):
     groups = []
     for opt in range(n_opt):
-        pairs = EVEN if opt % CORES == parity else ODD
+        pairs = EVEN if opt % CORES == 0 else ODD
         for across in pairs:
             for along in pairs:
                 groups.append([(x * SIDE + y) * n_opt + opt for x in across for y in along])
     return groups
+
+
+def swap_corner(x, across, along):
+    def partner(v, core, moved):
+        return v if not moved else (SIDE - 1 - v if core == 0 else v ^ 1)
+
+    n_opt = lax.axis_size("z") * CORES
+    pairs = []
+    for source in range(SIDE * SIDE * n_opt):
+        d, opt = divmod(source, n_opt)
+        px = partner(d // SIDE, opt % CORES, across)
+        py = partner(d % SIDE, opt % CORES, along)
+        pairs.append((source, (px * SIDE + py) * n_opt + opt))
+    return lax.ppermute(x, ALL, pairs)
 
 
 def contract(a, b, dim_a, dim_b):
@@ -38,20 +52,24 @@
     )
 
 
-def slot_kernel(where, recv, root, basis, factor, left, right, update, left_new, right_new, g, gram):
+def slot_kernel(where, own4, along4, across4, corner4, root, basis, factor, left, right, update, left_new, right_new, g, gram):
     my_dp, core = where[0], where[1]
     rows = left.shape[1]
-    flip_x = my_dp // SIDE // 2 == 0
-    flip_y = my_dp % SIDE // 2 == 0
-    for d in range(SIDE * SIDE):
-        x, y = d // SIDE, d % SIDE
-        outer_x, outer_y = int(x in (0, 3)), int(y in (0, 3))
-        odd_x = jnp.where(flip_x, 1 - outer_x, outer_x)
-        odd_y = jnp.where(flip_y, 1 - outer_y, outer_y)
-        high = x // 2 * 2 + y // 2
-        first = jnp.where(core == 0, high, odd_x * 2 + odd_y)
-        second = jnp.where(core == 0, x % 2 * 2 + y % 2, high)
-        g[d * rows : (d + 1) * rows, :] = recv[first, second, 0]
+    my_x, my_y = my_dp // SIDE, my_dp % SIDE
+
+    def spot(mine, moved, member):
+        half = jnp.where(mine >= 2, 1, 0)
+        outer = jnp.where((mine == 0) | (mine == SIDE - 1), 1, 0)
+        if moved:
+            half, outer = 1 - half, 1 - outer
+        return jnp.where(core == 0, half * 2 + member, 2 + outer if member else 1 - outer)
+
+    for step, rows4 in enumerate((own4, along4, across4, corner4)):
+        for member in range(SIDE):
+            x = spot(my_x, step // 2, member // 2)
+            y = spot(my_y, step % 2, member % 2)
+            first = pl.multiple_of((x * SIDE + y) * rows, rows)
+            g[pl.ds(first, rows), :] = rows4[member, 0]
     block = g[...]
     applied = contract(root[0], block, 1, 0).astype(jnp.bfloat16)
     own = g[pl.ds(pl.multiple_of(my_dp * rows, rows), rows), :]
@@ -65,9 +83,10 @@
     update[0] = contract(scaled, basis[0], 1, 1).astype(jnp.bfloat16)
 
 
-def slot_step(where, recv, root, basis, factor, left, right):
+def slot_step(where, squares, root, basis, factor, left, right):
     cap, width, _ = basis.shape
     rows = left.shape[1]
+    square = pl.BlockSpec((SIDE, 1, rows, width), lambda s, w: (0, s, 0, 0))
     whole = pl.BlockSpec((1, width, width), lambda s, w: (s, 0, 0))
     slab = pl.BlockSpec((1, rows, width), lambda s, w: (s, 0, 0))
     return pl.pallas_call(
@@ -76,7 +95,10 @@
             num_scalar_prefetch=1,
             grid=(cap,),
             in_specs=[
-                pl.BlockSpec((4, 4, 1, rows, width), lambda s, w: (0, 0, s, 0, 0)),
+                square,
+                square,
+                square,
+                square,
                 whole,
                 whole,
                 pl.BlockSpec((1, 1, width), lambda s, w: (s, 0, 0)),
@@ -94,11 +116,11 @@
             jax.ShapeDtypeStruct(left.shape, jnp.float32),
             jax.ShapeDtypeStruct(right.shape, jnp.float32),
         ],
-        compiler_params=pltpu.CompilerParams(vmem_limit_bytes=56 * 1024 * 1024),
+        compiler_params=pltpu.CompilerParams(vmem_limit_bytes=48 * 1024 * 1024),
         cost_estimate=pl.CostEstimate(
             flops=7 * cap * width**3, bytes_accessed=10 * cap * width**2, transcendentals=0
         ),
-    )(where, recv, root, basis, factor, left, right)
+    )(where, *squares, root, basis, factor, left, right)
 
 
 def body(gradients, owner_map, left_root, right_basis, right_eigen, left_stat, right_stat):
@@ -139,12 +161,12 @@
     n_opt = n_z * CORES
     factor = (right_eigen + epsilon) ** (-0.25)
     where = jnp.stack([my_dp, my_core]).astype(jnp.int32)
-    line = broadcast_gather(owned, ALL, quads(n_opt, 0))
+    line = broadcast_gather(owned, ALL, quads(n_opt))
     line, root, factor, where = lax.optimization_barrier((line, root, factor, where))
-    recv = broadcast_gather(line, ALL, quads(n_opt, 1))
+    squares = [line] + [swap_corner(line, a, b) for a, b in ((False, True), (True, False), (True, True))]
 
     update, left_new, right_new = slot_step(
-        where, recv, root, right_basis, factor[:, None, :], left_stat, right_stat
+        where, squares, root, right_basis, factor[:, None, :], left_stat, right_stat
     )
     return (update, left_new, right_new)
 

time: 183 us -> 180 us (0.984)
  starting transfers between devices: 45 us -> 49.8 us
  waiting for transfers between devices: 47.6 us -> 42.9 us
  local copies, waits for them, and re-layouts: 7.49 us -> 5.3 us
    all_to_all x2 -> x1, waiting for transfers between devices: 23.4 us -> 7.56 us  [broadcast_gather(): lax.all_to_all(copies, axis, split_axis=0, concat_axis=0, tiled=True, axi...]
    ppermute x0 -> x3, waiting for transfers between devices: none -> 11.1 us  [swap_corner(): return lax.ppermute(x, ALL, pairs)]
    ppermute x0 -> x3, starting transfers between devices: none -> 8.36 us  [swap_corner(): return lax.ppermute(x, ALL, pairs)]
    all_to_all x2 -> x1, starting transfers between devices: 7.14 us -> 3.48 us  [broadcast_gather(): lax.all_to_all(copies, axis, split_axis=0, concat_axis=0, tiled=True, axi...]
  transfers between devices with their start and end apart: 5 -> 7, of which waited for: 4 -> 6; matrix products, arithmetic and copies ran while one was open for 3% -> 2% of each run, Pallas kernels for 0% -> 0%
where the time goes in v4:
time: 180 us; the launch traced here: 177 us
  blocking collectives  55.2 us (31%)
  starting transfers between devices  49.8 us (28%)
  waiting for transfers between devices  42.9 us (24%)
  between operations  14.2 us (8%)
  Pallas kernels  8.98 us (5%)
  local copies, waits for them, and re-layouts  5.3 us (3%)
    all_to_all x1, blocking collectives, body(): lax.all_to_all(deliver, 'z', split_axis=0, concat_axis=0, tiled=True)  36.1 us
    all_to_all x1, starting transfers between devices, body(): lax.all_to_all(pieces, 'z', split_axis=0, concat_axis=0, tiled=True)  32.6 us
    all_to_all x1, waiting for transfers between devices, body(): lax.all_to_all(pieces, 'z', split_axis=0, concat_axis=0, tiled=True)  22.8 us
    all_to_all x1, blocking collectives, body(): parts = lax.all_to_all(sent, 'dp', split_axis=0, concat_axis=0, tiled=True)  19.1 us
    ppermute x3, waiting for transfers between devices, swap_corner(): return lax.ppermute(x, ALL, pairs)  11.1 us
    pallas_call x1, Pallas kernels, slot_step(): pl.pallas_call(slot_kernel, grid_spec=pltpu.PrefetchScalarGridSpec(num_sc...  8.98 us
    ppermute x3, starting transfers between devices, swap_corner(): return lax.ppermute(x, ALL, pairs)  8.36 us
    all_to_all x1, waiting for transfers between devices, broadcast_gather(): lax.all_to_all(copies, axis, split_axis=0, concat_axis=0, tiled=True, axi...  7.56 us
  transfers between devices with their start and end apart: 7, of which 6 were waited for; matrix products, arithmetic and copies ran while one was open for 2% of the time, Pallas kernels for 0%

profile of v4, /device:TPU:1, one launch (start us, length us, event | category | flops | bytes accessed | tf_op | source)
XLA Modules:
  0.0 177.1 jit_solution(14752163619909732659)
XLA Ops:
  7.2 0.7 all-gather.2.cloned.1.call-update
  7.9 1.3 copy.19
  9.2 19.1 %all_to_all.20 = bf16[16,2,32,512]{3,2,1,0:T(8,128)(2,1)S(1)} all-to-all(bf16[16,2,32,512]{3,2,1,0:T(8,128)(2,1)S(1)} %copy.19), channel_id=1, replica_groups=mesh['dp'=16,'z'=32,'core'=2] {'dp'}, dimensions={0} | all-to-all | bytes 2097152 | tf_op jit(solution)/shard_map/all_to_all | solution.py:136
  28.4 0.1 reduce_sum.22
  28.5 0.7 copy.20
  29.2 32.6 %all-to-all-start.1 = ((bf16[32,8,128]{2,1,0:T(8,128)(2,1)}), bf16[32,8,128]{2,1,0:T(8,128)(2,1)S(1)}, u32[]{:S(2)}, u32[]{:S(2)}) async-start(bf16[32,8,128]{2,1,0:T(8,128)(2,1)} %bitcast.3), calls=%async_computation.1 | async-start | bytes 131072 | tf_op jit(solution)/shard_map/all_to_all | solution.py:141
  61.8 0.2 convert_reduce_fusion
  62.0 0.2 reshape.38
  62.5 22.8 %all-to-all-done.1 = bf16[32,8,128]{2,1,0:T(8,128)(2,1)S(1)} async-done(((bf16[32,8,128]{2,1,0:T(8,128)(2,1)}), bf16[32,8,128]{2,1,0:T(8,128)(2,1)S(1)}, u32[]{:S(2)}, u32[]{:S(2)}) %all-to-all-start.1) | async-done | bytes 65568 | tf_op jit(solution)/shard_map/all_to_all | solution.py:141
  85.2 5.3 %collective-permute-start = (bf16[32,8,128]{2,1,0:T(8,128)(2,1)S(1)}, bf16[32,8,128]{2,1,0:T(8,128)(2,1)S(1)}, u32[]{:S(2)}, u32[]{:S(2)}) collective-permute-start(bf16[32,8,128]{2,1,0:T(8,128)(2,1)S(1)} %all-to-all-done.1), channel_id=1, source_target_pairs={{0,1},{1,0},{2,3},{3,2},{4,5},{5,4},{6,7},{7,6},{8,9},{9,8},{10,11... | collective-permute-start | bytes 196616 | tf_op jit(solution)/shard_map/ppermute | solution.py:142
  90.7 0.8 collective-permute-done
  91.5 0.2 convolution_convert_fusion
  91.7 36.1 %all_to_all.21 = bf16[32,5,4,128]{3,2,1,0:T(4,128)(2,1)S(1)} all-to-all(bf16[32,5,4,128]{3,2,1,0:T(4,128)(2,1)S(1)} %reshape.44), channel_id=1, replica_groups=mesh['dp'=16,'z'=32,'core'=2] {'z'}, dimensions={0} | all-to-all | bytes 327680 | tf_op jit(solution)/shard_map/all_to_all | solution.py:157
  127.9 0.9 broadcast_in_dim.9
  128.9 3.5 %all-to-all-start.3 = ((bf16[4,5,32,512]{3,2,1,0:T(8,128)(2,1)}), bf16[4,5,32,512]{3,2,1,0:T(8,128)(2,1)S(1)}, u32[]{:S(2)}, u32[]{:S(2)}) async-start(bf16[4,5,32,512]{3,2,1,0:T(8,128)(2,1)} %broadcast_in_dim.9), calls=%async_computation.3 | async-start | bytes 1310720 | tf_op jit(solution)/shard_map/all_to_all | solution.py:20
  132.4 7.6 %all-to-all-done.3.own4 = bf16[4,5,32,512]{3,2,1,0:T(8,128)(2,1)S(1)} async-done(((bf16[4,5,32,512]{3,2,1,0:T(8,128)(2,1)}), bf16[4,5,32,512]{3,2,1,0:T(8,128)(2,1)S(1)}, u32[]{:S(2)}, u32[]{:S(2)}) %all-to-all-start.3) | async-done | bytes 655392 | tf_op jit(solution)/shard_map/all_to_all | solution.py:20
  140.0 1.9 %collective-permute-start.3 = (bf16[4,5,32,512]{3,2,1,0:T(8,128)(2,1)S(1)}, bf16[4,5,32,512]{3,2,1,0:T(8,128)(2,1)S(1)}, u32[]{:S(2)}, u32[]{:S(2)}) collective-permute-start(bf16[4,5,32,512]{3,2,1,0:T(8,128)(2,1)S(1)} %all-to-all-done.3.own4), channel_id=1, source_target_pairs={{0,960},{1,321},{2,962},{3,323},{4,964},{5,325},{6,966},{7,327},{8... | collective-permute-start | bytes 1966088 | tf_op jit(solution)/shard_map/ppermute | solution.py:46
  141.9 3.4 %collective-permute-start.2 = (bf16[4,5,32,512]{3,2,1,0:T(8,128)(2,1)S(1)}, bf16[4,5,32,512]{3,2,1,0:T(8,128)(2,1)S(1)}, u32[]{:S(2)}, u32[]{:S(2)}) collective-permute-start(bf16[4,5,32,512]{3,2,1,0:T(8,128)(2,1)S(1)} %all-to-all-done.3.own4), channel_id=1, source_target_pairs={{0,768},{1,257},{2,770},{3,259},{4,772},{5,261},{6,774},{7,263},{8... | collective-permute-start | bytes 1966088 | tf_op jit(solution)/shard_map/ppermute | solution.py:46
  145.3 3.1 %collective-permute-start.1 = (bf16[4,5,32,512]{3,2,1,0:T(8,128)(2,1)S(1)}, bf16[4,5,32,512]{3,2,1,0:T(8,128)(2,1)S(1)}, u32[]{:S(2)}, u32[]{:S(2)}) collective-permute-start(bf16[4,5,32,512]{3,2,1,0:T(8,128)(2,1)S(1)} %all-to-all-done.3.own4), channel_id=1, source_target_pairs={{0,192},{1,65},{2,194},{3,67},{4,196},{5,69},{6,198},{7,71},{8,200... | collective-permute-start | bytes 1966088 | tf_op jit(solution)/shard_map/ppermute | solution.py:46
  148.4 4.2 %collective-permute-done.3.corner4 = bf16[4,5,32,512]{3,2,1,0:T(8,128)(2,1)S(1)} collective-permute-done((bf16[4,5,32,512]{3,2,1,0:T(8,128)(2,1)S(1)}, bf16[4,5,32,512]{3,2,1,0:T(8,128)(2,1)S(1)}, u32[]{:S(2)}, u32[]{:S(2)}) %collective-permute-start.3) | collective-permute-done | bytes 655392 | tf_op jit(solution)/shard_map/ppermute | solution.py:46
  152.6 6.1 %collective-permute-done.2.across4 = bf16[4,5,32,512]{3,2,1,0:T(8,128)(2,1)S(1)} collective-permute-done((bf16[4,5,32,512]{3,2,1,0:T(8,128)(2,1)S(1)}, bf16[4,5,32,512]{3,2,1,0:T(8,128)(2,1)S(1)}, u32[]{:S(2)}, u32[]{:S(2)}) %collective-permute-start.2) | collective-permute-done | bytes 655392 | tf_op jit(solution)/shard_map/ppermute | solution.py:46
  158.7 0.8 collective-permute-done.1.along4
  159.6 1.7 copy-done
  161.3 9.0 %shard_map.94 = (bf16[5,512,512]{2,1,0:T(8,128)(2,1)}, f32[5,32,512]{2,1,0:T(8,128)}, f32[5,32,512]{2,1,0:T(8,128)}) custom-call(s32[2]{0:T(128)S(1)} %pad_add_fusion.1.where, bf16[4,5,32,512]{3,2,1,0:T(8,128)(2,1)S(1)} %all-to-all-done.3.own4, bf16[4,5,32,512]{3,2,1,0:T(8,128)(2,1)S(1)} %collective-permute-done.1.along4, ...), custom_call_target="tpu_custom_call" | custom-call | flops 4697620480 | bytes 13107200 | tf_op jit(solution)/shard_map/pallas_call | solution.py:92
  (25 shorter events, 0.9 us)
Async XLA Ops:
  7.2 132.8 %all-gather.2.cloned.1.call-start = ((), (), s32[]{:S(2)}) async-start(), calls=%async_computation.4 | async-start | bytes 2785280 | tf_op jit(solution)/shard_map/all_gather | solution.py:133
  7.9 53.9 %copy-start.4 = (s32[128]{0:T(128)S(1)}, s32[128]{0:T(128)}, u32[]{:S(2)}) copy-start(s32[128]{0:T(128)} %param.8) | copy-start | bytes 1540
  28.4 104.1 %copy-start.3 = (f32[5,512]{1,0:T(8,128)S(1)}, f32[5,512]{1,0:T(8,128)}, u32[]{:S(2)}) copy-start(f32[5,512]{1,0:T(8,128)} %param.11) | copy-start | bytes 30724
  28.4 131.2 %copy-start.1 = (f32[5,32,512]{2,1,0:T(8,128)S(1)}, f32[5,32,512]{2,1,0:T(8,128)}, u32[]{:S(2)}) copy-start(f32[5,32,512]{2,1,0:T(8,128)} %left.1) | copy-start | bytes 983044
  28.4 131.2 %copy-start.2 = (f32[5,32,512]{2,1,0:T(8,128)S(1)}, f32[5,32,512]{2,1,0:T(8,128)}, u32[]{:S(2)}) copy-start(f32[5,32,512]{2,1,0:T(8,128)} %right.1) | copy-start | bytes 983044
  29.2 56.0 %all-to-all-start.1 = ((bf16[32,8,128]{2,1,0:T(8,128)(2,1)}), bf16[32,8,128]{2,1,0:T(8,128)(2,1)S(1)}, u32[]{:S(2)}, u32[]{:S(2)}) async-start(bf16[32,8,128]{2,1,0:T(8,128)(2,1)} %bitcast.3), calls=%async_computation.1 | async-start | bytes 131072 | tf_op jit(solution)/shard_map/all_to_all | solution.py:141
  85.2 6.2 %collective-permute-start = (bf16[32,8,128]{2,1,0:T(8,128)(2,1)S(1)}, bf16[32,8,128]{2,1,0:T(8,128)(2,1)S(1)}, u32[]{:S(2)}, u32[]{:S(2)}) collective-permute-start(bf16[32,8,128]{2,1,0:T(8,128)(2,1)S(1)} %all-to-all-done.1), channel_id=1, source_target_pairs={{0,1},{1,0},{2,3},{3,2},{4,5},{5,4},{6,7},{7,6},{8,9},{9,8},{10,11... | collective-permute-start | bytes 196616 | tf_op jit(solution)/shard_map/ppermute | solution.py:142
  128.9 11.2 %all-to-all-start.3 = ((bf16[4,5,32,512]{3,2,1,0:T(8,128)(2,1)}), bf16[4,5,32,512]{3,2,1,0:T(8,128)(2,1)S(1)}, u32[]{:S(2)}, u32[]{:S(2)}) async-start(bf16[4,5,32,512]{3,2,1,0:T(8,128)(2,1)} %broadcast_in_dim.9), calls=%async_computation.3 | async-start | bytes 1310720 | tf_op jit(solution)/shard_map/all_to_all | solution.py:20
  140.0 12.6 %collective-permute-start.3 = (bf16[4,5,32,512]{3,2,1,0:T(8,128)(2,1)S(1)}, bf16[4,5,32,512]{3,2,1,0:T(8,128)(2,1)S(1)}, u32[]{:S(2)}, u32[]{:S(2)}) collective-permute-start(bf16[4,5,32,512]{3,2,1,0:T(8,128)(2,1)S(1)} %all-to-all-done.3.own4), channel_id=1, source_target_pairs={{0,960},{1,321},{2,962},{3,323},{4,964},{5,325},{6,966},{7,327},{8... | collective-permute-start | bytes 1966088 | tf_op jit(solution)/shard_map/ppermute | solution.py:46
  141.9 16.8 %collective-permute-start.2 = (bf16[4,5,32,512]{3,2,1,0:T(8,128)(2,1)S(1)}, bf16[4,5,32,512]{3,2,1,0:T(8,128)(2,1)S(1)}, u32[]{:S(2)}, u32[]{:S(2)}) collective-permute-start(bf16[4,5,32,512]{3,2,1,0:T(8,128)(2,1)S(1)} %all-to-all-done.3.own4), channel_id=1, source_target_pairs={{0,768},{1,257},{2,770},{3,259},{4,772},{5,261},{6,774},{7,263},{8... | collective-permute-start | bytes 1966088 | tf_op jit(solution)/shard_map/ppermute | solution.py:46
  145.3 14.2 %collective-permute-start.1 = (bf16[4,5,32,512]{3,2,1,0:T(8,128)(2,1)S(1)}, bf16[4,5,32,512]{3,2,1,0:T(8,128)(2,1)S(1)}, u32[]{:S(2)}, u32[]{:S(2)}) collective-permute-start(bf16[4,5,32,512]{3,2,1,0:T(8,128)(2,1)S(1)} %all-to-all-done.3.own4), channel_id=1, source_target_pairs={{0,192},{1,65},{2,194},{3,67},{4,196},{5,69},{6,198},{7,71},{8,200... | collective-permute-start | bytes 1966088 | tf_op jit(solution)/shard_map/ppermute | solution.py:46
  159.5 1.7 copy-start
Sparse Core Ops, SparseCore 0:
  12.2 90.1 all-gather.1

commit v5 on v4

--- a/solution.py
+++ b/solution.py
@@ -52,7 +52,7 @@
     )
 
 
-def slot_kernel(where, own4, along4, across4, corner4, root, basis, factor, left, right, update, left_new, right_new, g, gram):
+def slot_kernel(where, own4, along4, across4, corner4, root, middle, left, right, update, left_new, right_new, g, gram):
     my_dp, core = where[0], where[1]
     rows = left.shape[1]
     my_x, my_y = my_dp // SIDE, my_dp % SIDE
@@ -79,12 +79,35 @@
     gram[...] = contract(g[:, lanes], block, 0, 0)
     mine = gram[pl.ds(pl.multiple_of(my_dp % group * rows, rows), rows), :]
     right_new[0] = decay_rate * right[0] + (1.0 - decay_rate) * mine
-    scaled = (contract(applied, basis[0], 1, 0) * factor[0]).astype(jnp.bfloat16)
-    update[0] = contract(scaled, basis[0], 1, 1).astype(jnp.bfloat16)
-
-
-def slot_step(where, squares, root, basis, factor, left, right):
+    update[0] = contract(applied, middle[0], 1, 0).astype(jnp.bfloat16)
+
+
+def middle_kernel(basis, factor, middle):
+    scaled = basis[0].astype(jnp.float32) * factor[0]
+    high = scaled.astype(jnp.bfloat16)
+    low = (scaled - high.astype(jnp.float32)).astype(jnp.bfloat16)
+    product = contract(high, basis[0], 1, 1) + contract(low, basis[0], 1, 1)
+    middle[0] = product.astype(jnp.bfloat16)
+
+
+def middle_step(basis, factor):
     cap, width, _ = basis.shape
+    whole = pl.BlockSpec((1, width, width), lambda s: (s, 0, 0))
+    return pl.pallas_call(
+        middle_kernel,
+        grid=(cap,),
+        in_specs=[whole, pl.BlockSpec((1, 1, width), lambda s: (s, 0, 0))],
+        out_specs=whole,
+        out_shape=jax.ShapeDtypeStruct(basis.shape, jnp.bfloat16),
+        compiler_params=pltpu.CompilerParams(vmem_limit_bytes=58 * 1024 * 1024),
+        cost_estimate=pl.CostEstimate(
+            flops=4 * cap * width**3, bytes_accessed=4 * cap * width**2, transcendentals=0
+        ),
+    )(basis, factor)
+
+
+def slot_step(where, squares, root, middle, left, right):
+    cap, width, _ = middle.shape
     rows = left.shape[1]
     square = pl.BlockSpec((SIDE, 1, rows, width), lambda s, w: (0, s, 0, 0))
     whole = pl.BlockSpec((1, width, width), lambda s, w: (s, 0, 0))
@@ -101,7 +124,6 @@
                 square,
                 whole,
                 whole,
-                pl.BlockSpec((1, 1, width), lambda s, w: (s, 0, 0)),
                 slab,
                 slab,
             ],
@@ -112,15 +134,15 @@
             ],
         ),
         out_shape=[
-            jax.ShapeDtypeStruct(basis.shape, jnp.bfloat16),
+            jax.ShapeDtypeStruct(middle.shape, jnp.bfloat16),
             jax.ShapeDtypeStruct(left.shape, jnp.float32),
             jax.ShapeDtypeStruct(right.shape, jnp.float32),
         ],
-        compiler_params=pltpu.CompilerParams(vmem_limit_bytes=48 * 1024 * 1024),
+        compiler_params=pltpu.CompilerParams(vmem_limit_bytes=58 * 1024 * 1024),
         cost_estimate=pl.CostEstimate(
-            flops=7 * cap * width**3, bytes_accessed=10 * cap * width**2, transcendentals=0
+            flops=5 * cap * width**3, bytes_accessed=10 * cap * width**2, transcendentals=0
         ),
-    )(where, *squares, root, basis, factor, left, right)
+    )(where, *squares, root, middle, left, right)
 
 
 def body(gradients, owner_map, left_root, right_basis, right_eigen, left_stat, right_stat):
@@ -138,7 +160,11 @@
 
     summed = summed.reshape(blocks, row_tiles, 2, 4, col_tiles, 128)
     pieces = summed.transpose(1, 4, 2, 0, 3, 5).reshape(n_z, blocks * 4, 128)
+    pieces, right_basis = lax.optimization_barrier((pieces, right_basis))
+    factor = (right_eigen + epsilon) ** (-0.25)
+    middle = middle_step(right_basis, factor[:, None, :])
     spread = lax.all_to_all(pieces, "z", split_axis=0, concat_axis=0, tiled=True)
+    spread, middle = lax.optimization_barrier((spread, middle))
     swapped = lax.ppermute(spread, "core", [(0, 1), (1, 0)])
     held = jnp.concatenate([t.reshape(n_z * blocks, 4 * 128) for t in (spread, swapped)])
 
@@ -159,14 +185,13 @@
     owned = arrived.reshape(row_tiles, col_tiles, 2, cap, 4, 128)
     owned = owned.transpose(3, 0, 2, 4, 1, 5).reshape(cap, rows, width)
     n_opt = n_z * CORES
-    factor = (right_eigen + epsilon) ** (-0.25)
     where = jnp.stack([my_dp, my_core]).astype(jnp.int32)
     line = broadcast_gather(owned, ALL, quads(n_opt))
-    line, root, factor, where = lax.optimization_barrier((line, root, factor, where))
+    line, root, where = lax.optimization_barrier((line, root, where))
     squares = [line] + [swap_corner(line, a, b) for a, b in ((False, True), (True, False), (True, True))]
 
     update, left_new, right_new = slot_step(
-        where, squares, root, right_basis, factor[:, None, :], left_stat, right_stat
+        where, squares, root, middle, left_stat, right_stat
     )
     return (update, left_new, right_new)
 

time: 180 us -> 182 us (1.011)
  blocking collectives: 55.2 us -> 36.8 us
  starting transfers between devices: 49.8 us -> 58.2 us
  Pallas kernels: 8.98 us -> 15.7 us
  waiting for transfers between devices: 42.9 us -> 46.8 us
    all_to_all x1 -> x0, blocking collectives: 19.1 us -> none  [body(): parts = lax.all_to_all(sent, 'dp', split_axis=0, concat_axis=0, tiled=True)]
    all_to_all x0 -> x1, waiting for transfers between devices: none -> 10.9 us  [body(): parts = lax.all_to_all(sent, 'dp', split_axis=0, concat_axis=0, tiled=True)]
    all_to_all x0 -> x1, starting transfers between devices: none -> 7.58 us  [body(): parts = lax.all_to_all(sent, 'dp', split_axis=0, concat_axis=0, tiled=True)]
    pallas_call x0 -> x1, Pallas kernels: none -> 6.6 us  [middle_step(): pl.pallas_call(middle_kernel, grid=(cap,), in_specs=[whole, pl.BlockSpec(...]
    all_to_all x1, waiting for transfers between devices: 22.8 us -> 16.3 us  [body(): lax.all_to_all(pieces, 'z', split_axis=0, concat_axis=0, tiled=True)]
  transfers between devices with their start and end apart: 7 -> 8, of which waited for: 6 -> 7; matrix products, arithmetic and copies ran while one was open for 2% -> 4% of each run, Pallas kernels for 0% -> 4%
where the time goes in v5:
time: 182 us; the launch traced here: 179 us
  starting transfers between devices  58.2 us (32%)
  waiting for transfers between devices  46.8 us (26%)
  blocking collectives  36.8 us (20%)
  Pallas kernels  15.7 us (9%)
  between operations  14.2 us (8%)
  local copies, waits for them, and re-layouts  6.01 us (3%)
    all_to_all x1, blocking collectives, body(): lax.all_to_all(deliver, 'z', split_axis=0, concat_axis=0, tiled=True)  36.8 us
    all_to_all x1, starting transfers between devices, body(): lax.all_to_all(pieces, 'z', split_axis=0, concat_axis=0, tiled=True)  32.2 us
    all_to_all x1, waiting for transfers between devices, body(): lax.all_to_all(pieces, 'z', split_axis=0, concat_axis=0, tiled=True)  16.3 us
    ppermute x3, waiting for transfers between devices, swap_corner(): return lax.ppermute(x, ALL, pairs)  11.1 us
    all_to_all x1, waiting for transfers between devices, body(): parts = lax.all_to_all(sent, 'dp', split_axis=0, concat_axis=0, tiled=True)  10.9 us
    pallas_call x1, Pallas kernels, slot_step(): pl.pallas_call(slot_kernel, grid_spec=pltpu.PrefetchScalarGridSpec(num_sc...  9.14 us
    ppermute x3, starting transfers between devices, swap_corner(): return lax.ppermute(x, ALL, pairs)  8.36 us
    all_to_all x1, starting transfers between devices, body(): parts = lax.all_to_all(sent, 'dp', split_axis=0, concat_axis=0, tiled=True)  7.58 us
  transfers between devices with their start and end apart: 8, of which 7 were waited for; matrix products, arithmetic and copies ran while one was open for 4% of the time, Pallas kernels for 4%

profile of v5, /device:TPU:1, one launch (start us, length us, event | category | flops | bytes accessed | tf_op | source)
XLA Modules:
  0.0 179.1 jit_solution(9049560185693689352)
XLA Ops:
  7.2 0.7 all-gather.2.cloned.1.call-update
  7.9 2.3 %copy.19 = bf16[16,2,32,512]{3,2,1,0:T(8,128)(2,1)} copy(bf16[16,2,32,512]{3,2,0,1:T(8,128)(2,1)} %bitcast.11) | data formatting | bytes 2097152 | tf_op jit(solution)/shard_map/transpose | solution.py:157
  10.2 7.6 %all-to-all-start = ((bf16[16,2,32,512]{3,2,1,0:T(8,128)(2,1)}), bf16[16,2,32,512]{3,2,1,0:T(8,128)(2,1)S(1)}, u32[]{:S(2)}, u32[]{:S(2)}) async-start(bf16[16,2,32,512]{3,2,1,0:T(8,128)(2,1)} %copy.19), calls=%async_computation | async-start | bytes 2097152 | tf_op jit(solution)/shard_map/all_to_all | solution.py:158
  17.9 0.6 broadcast_in_dim.8.factor
  18.6 10.9 %all-to-all-done = bf16[16,2,32,512]{3,2,1,0:T(8,128)(2,1)S(1)} async-done(((bf16[16,2,32,512]{3,2,1,0:T(8,128)(2,1)}), bf16[16,2,32,512]{3,2,1,0:T(8,128)(2,1)S(1)}, u32[]{:S(2)}, u32[]{:S(2)}) %all-to-all-start) | async-done | bytes 1048608 | tf_op jit(solution)/shard_map/all_to_all | solution.py:158
  29.7 0.7 copy.20
  30.4 32.2 %all-to-all-start.1 = ((bf16[32,8,128]{2,1,0:T(8,128)(2,1)}), bf16[32,8,128]{2,1,0:T(8,128)(2,1)S(1)}, u32[]{:S(2)}, u32[]{:S(2)}) async-start(bf16[32,8,128]{2,1,0:T(8,128)(2,1)} %bitcast.3), calls=%async_computation.1 | async-start | bytes 131072 | tf_op jit(solution)/shard_map/all_to_all | solution.py:166
  63.1 6.6 %shard_map.94.middle = bf16[5,512,512]{2,1,0:T(8,128)(2,1)} custom-call(bf16[5,512,512]{2,1,0:T(8,128)(2,1)} %basis, f32[5,1,512]{2,1,0:T(1,128)} %broadcast_in_dim.8.factor), custom_call_target="tpu_custom_call" | custom-call | flops 2684354560 | bytes 5242880 | tf_op jit(solution)/shard_map/pallas_call | solution.py:96
  69.7 16.3 %all-to-all-done.1 = bf16[32,8,128]{2,1,0:T(8,128)(2,1)S(1)} async-done(((bf16[32,8,128]{2,1,0:T(8,128)(2,1)}), bf16[32,8,128]{2,1,0:T(8,128)(2,1)S(1)}, u32[]{:S(2)}, u32[]{:S(2)}) %all-to-all-start.1) | async-done | bytes 65568 | tf_op jit(solution)/shard_map/all_to_all | solution.py:166
  86.0 6.5 %collective-permute-start = (bf16[32,8,128]{2,1,0:T(8,128)(2,1)S(1)}, bf16[32,8,128]{2,1,0:T(8,128)(2,1)S(1)}, u32[]{:S(2)}, u32[]{:S(2)}) collective-permute-start(bf16[32,8,128]{2,1,0:T(8,128)(2,1)S(1)} %all-to-all-done.1), channel_id=1, source_target_pairs={{0,1},{1,0},{2,3},{3,2},{4,5},{5,4},{6,7},{7,6},{8,9},{9,8},{10,11... | collective-permute-start | bytes 196616 | tf_op jit(solution)/shard_map/ppermute | solution.py:168
  92.6 0.8 collective-permute-done
  93.7 36.8 %all_to_all.20 = bf16[32,5,4,128]{3,2,1,0:T(4,128)(2,1)S(1)} all-to-all(bf16[32,5,4,128]{3,2,1,0:T(4,128)(2,1)S(1)} %reshape.44), channel_id=1, replica_groups=mesh['dp'=16,'z'=32,'core'=2] {'z'}, dimensions={0} | all-to-all | bytes 327680 | tf_op jit(solution)/shard_map/all_to_all | solution.py:183
  130.6 0.9 broadcast_in_dim.10
  131.5 3.5 %all-to-all-start.3 = ((bf16[4,5,32,512]{3,2,1,0:T(8,128)(2,1)}), bf16[4,5,32,512]{3,2,1,0:T(8,128)(2,1)S(1)}, u32[]{:S(2)}, u32[]{:S(2)}) async-start(bf16[4,5,32,512]{3,2,1,0:T(8,128)(2,1)} %broadcast_in_dim.10), calls=%async_computation.3 | async-start | bytes 1310720 | tf_op jit(solution)/shard_map/all_to_all | solution.py:20
  135.0 0.7 pad_add_fusion.1.where
  135.7 7.0 %all-to-all-done.3.own4 = bf16[4,5,32,512]{3,2,1,0:T(8,128)(2,1)S(1)} async-done(((bf16[4,5,32,512]{3,2,1,0:T(8,128)(2,1)}), bf16[4,5,32,512]{3,2,1,0:T(8,128)(2,1)S(1)}, u32[]{:S(2)}, u32[]{:S(2)}) %all-to-all-start.3) | async-done | bytes 655392 | tf_op jit(solution)/shard_map/all_to_all | solution.py:20
  142.7 1.9 %collective-permute-start.3 = (bf16[4,5,32,512]{3,2,1,0:T(8,128)(2,1)S(1)}, bf16[4,5,32,512]{3,2,1,0:T(8,128)(2,1)S(1)}, u32[]{:S(2)}, u32[]{:S(2)}) collective-permute-start(bf16[4,5,32,512]{3,2,1,0:T(8,128)(2,1)S(1)} %all-to-all-done.3.own4), channel_id=1, source_target_pairs={{0,960},{1,321},{2,962},{3,323},{4,964},{5,325},{6,966},{7,327},{8... | collective-permute-start | bytes 1966088 | tf_op jit(solution)/shard_map/ppermute | solution.py:46
  144.6 3.1 %collective-permute-start.2 = (bf16[4,5,32,512]{3,2,1,0:T(8,128)(2,1)S(1)}, bf16[4,5,32,512]{3,2,1,0:T(8,128)(2,1)S(1)}, u32[]{:S(2)}, u32[]{:S(2)}) collective-permute-start(bf16[4,5,32,512]{3,2,1,0:T(8,128)(2,1)S(1)} %all-to-all-done.3.own4), channel_id=1, source_target_pairs={{0,768},{1,257},{2,770},{3,259},{4,772},{5,261},{6,774},{7,263},{8... | collective-permute-start | bytes 1966088 | tf_op jit(solution)/shard_map/ppermute | solution.py:46
  147.8 3.3 %collective-permute-start.1 = (bf16[4,5,32,512]{3,2,1,0:T(8,128)(2,1)S(1)}, bf16[4,5,32,512]{3,2,1,0:T(8,128)(2,1)S(1)}, u32[]{:S(2)}, u32[]{:S(2)}) collective-permute-start(bf16[4,5,32,512]{3,2,1,0:T(8,128)(2,1)S(1)} %all-to-all-done.3.own4), channel_id=1, source_target_pairs={{0,192},{1,65},{2,194},{3,67},{4,196},{5,69},{6,198},{7,71},{8,200... | collective-permute-start | bytes 1966088 | tf_op jit(solution)/shard_map/ppermute | solution.py:46
  151.1 4.2 %collective-permute-done.3.corner4 = bf16[4,5,32,512]{3,2,1,0:T(8,128)(2,1)S(1)} collective-permute-done((bf16[4,5,32,512]{3,2,1,0:T(8,128)(2,1)S(1)}, bf16[4,5,32,512]{3,2,1,0:T(8,128)(2,1)S(1)}, u32[]{:S(2)}, u32[]{:S(2)}) %collective-permute-start.3) | collective-permute-done | bytes 655392 | tf_op jit(solution)/shard_map/ppermute | solution.py:46
  155.2 5.9 %collective-permute-done.2.across4 = bf16[4,5,32,512]{3,2,1,0:T(8,128)(2,1)S(1)} collective-permute-done((bf16[4,5,32,512]{3,2,1,0:T(8,128)(2,1)S(1)}, bf16[4,5,32,512]{3,2,1,0:T(8,128)(2,1)S(1)}, u32[]{:S(2)}, u32[]{:S(2)}) %collective-permute-start.2) | collective-permute-done | bytes 655392 | tf_op jit(solution)/shard_map/ppermute | solution.py:46
  161.1 1.1 collective-permute-done.1.along4
  162.2 0.8 copy-done.5
  163.1 9.1 %shard_map.95 = (bf16[5,512,512]{2,1,0:T(8,128)(2,1)}, f32[5,32,512]{2,1,0:T(8,128)}, f32[5,32,512]{2,1,0:T(8,128)}) custom-call(s32[2]{0:T(128)} %pad_add_fusion.1.where, bf16[4,5,32,512]{3,2,1,0:T(8,128)(2,1)} %copy-done, bf16[4,5,32,512]{3,2,1,0:T(8,128)(2,1)} %copy-done.5, bf16[4,5,32,512]{3,2,1,0:T(8,128)(2,1)} %copy-done.4, ...), custom_call_target="tpu_custom_call" | custom-call | flops 3355443200 | bytes 13107200 | tf_op jit(solution)/shard_map/pallas_call | solution.py:115
  (29 shorter events, 1.4 us)
Async XLA Ops:
  7.2 10.7 %copy-start.1 = (f32[5,512]{1,0:T(8,128)S(1)}, f32[5,512]{1,0:T(8,128)}, u32[]{:S(2)}) copy-start(f32[5,512]{1,0:T(8,128)} %param.11) | copy-start | bytes 30724
  7.2 11.3 %copy-start.2 = (s32[128]{0:T(128)S(1)}, s32[128]{0:T(128)}, u32[]{:S(2)}) copy-start(s32[128]{0:T(128)} %param.8) | copy-start | bytes 1540
  7.2 135.5 %all-gather.2.cloned.1.call-start = ((), (), s32[]{:S(2)}) async-start(), calls=%async_computation.4 | async-start | bytes 2785280 | tf_op jit(solution)/shard_map/all_gather | solution.py:155
  10.2 19.3 %all-to-all-start = ((bf16[16,2,32,512]{3,2,1,0:T(8,128)(2,1)}), bf16[16,2,32,512]{3,2,1,0:T(8,128)(2,1)S(1)}, u32[]{:S(2)}, u32[]{:S(2)}) async-start(bf16[16,2,32,512]{3,2,1,0:T(8,128)(2,1)} %copy.19), calls=%async_computation | async-start | bytes 2097152 | tf_op jit(solution)/shard_map/all_to_all | solution.py:158
  30.4 55.6 %all-to-all-start.1 = ((bf16[32,8,128]{2,1,0:T(8,128)(2,1)}), bf16[32,8,128]{2,1,0:T(8,128)(2,1)S(1)}, u32[]{:S(2)}, u32[]{:S(2)}) async-start(bf16[32,8,128]{2,1,0:T(8,128)(2,1)} %bitcast.3), calls=%async_computation.1 | async-start | bytes 131072 | tf_op jit(solution)/shard_map/all_to_all | solution.py:166
  86.0 7.4 %collective-permute-start = (bf16[32,8,128]{2,1,0:T(8,128)(2,1)S(1)}, bf16[32,8,128]{2,1,0:T(8,128)(2,1)S(1)}, u32[]{:S(2)}, u32[]{:S(2)}) collective-permute-start(bf16[32,8,128]{2,1,0:T(8,128)(2,1)S(1)} %all-to-all-done.1), channel_id=1, source_target_pairs={{0,1},{1,0},{2,3},{3,2},{4,5},{5,4},{6,7},{7,6},{8,9},{9,8},{10,11... | collective-permute-start | bytes 196616 | tf_op jit(solution)/shard_map/ppermute | solution.py:168
  131.5 11.2 %all-to-all-start.3 = ((bf16[4,5,32,512]{3,2,1,0:T(8,128)(2,1)}), bf16[4,5,32,512]{3,2,1,0:T(8,128)(2,1)S(1)}, u32[]{:S(2)}, u32[]{:S(2)}) async-start(bf16[4,5,32,512]{3,2,1,0:T(8,128)(2,1)} %broadcast_in_dim.10), calls=%async_computation.3 | async-start | bytes 1310720 | tf_op jit(solution)/shard_map/all_to_all | solution.py:20
  142.7 19.5 %copy-start = (bf16[4,5,32,512]{3,2,1,0:T(8,128)(2,1)}, bf16[4,5,32,512]{3,2,1,0:T(8,128)(2,1)S(1)}, u32[]{:S(2)}) copy-start(bf16[4,5,32,512]{3,2,1,0:T(8,128)(2,1)S(1)} %all-to-all-done.3.own4) | copy-start | bytes 1966084
  142.7 12.6 %collective-permute-start.3 = (bf16[4,5,32,512]{3,2,1,0:T(8,128)(2,1)S(1)}, bf16[4,5,32,512]{3,2,1,0:T(8,128)(2,1)S(1)}, u32[]{:S(2)}, u32[]{:S(2)}) collective-permute-start(bf16[4,5,32,512]{3,2,1,0:T(8,128)(2,1)S(1)} %all-to-all-done.3.own4), channel_id=1, source_target_pairs={{0,960},{1,321},{2,962},{3,323},{4,964},{5,325},{6,966},{7,327},{8... | collective-permute-start | bytes 1966088 | tf_op jit(solution)/shard_map/ppermute | solution.py:46
  144.6 16.5 %collective-permute-start.2 = (bf16[4,5,32,512]{3,2,1,0:T(8,128)(2,1)S(1)}, bf16[4,5,32,512]{3,2,1,0:T(8,128)(2,1)S(1)}, u32[]{:S(2)}, u32[]{:S(2)}) collective-permute-start(bf16[4,5,32,512]{3,2,1,0:T(8,128)(2,1)S(1)} %all-to-all-done.3.own4), channel_id=1, source_target_pairs={{0,768},{1,257},{2,770},{3,259},{4,772},{5,261},{6,774},{7,263},{8... | collective-permute-start | bytes 1966088 | tf_op jit(solution)/shard_map/ppermute | solution.py:46
  147.8 14.5 %collective-permute-start.1 = (bf16[4,5,32,512]{3,2,1,0:T(8,128)(2,1)S(1)}, bf16[4,5,32,512]{3,2,1,0:T(8,128)(2,1)S(1)}, u32[]{:S(2)}, u32[]{:S(2)}) collective-permute-start(bf16[4,5,32,512]{3,2,1,0:T(8,128)(2,1)S(1)} %all-to-all-done.3.own4), channel_id=1, source_target_pairs={{0,192},{1,65},{2,194},{3,67},{4,196},{5,69},{6,198},{7,71},{8,200... | collective-permute-start | bytes 1966088 | tf_op jit(solution)/shard_map/ppermute | solution.py:46
  155.2 7.0 %copy-start.3 = (bf16[4,5,32,512]{3,2,1,0:T(8,128)(2,1)}, bf16[4,5,32,512]{3,2,1,0:T(8,128)(2,1)S(1)}, u32[]{:S(2)}) copy-start(bf16[4,5,32,512]{3,2,1,0:T(8,128)(2,1)S(1)} %collective-permute-done.3.corner4) | copy-start | bytes 1966084
  161.1 1.1 copy-start.4
  162.2 0.9 copy-start.5
Sparse Core Ops, SparseCore 0:
  12.3 90.1 all-gather.1

commit v6 on v5

--- a/solution.py
+++ b/solution.py
@@ -52,9 +52,13 @@
     )
 
 
-def slot_kernel(where, own4, along4, across4, corner4, root, middle, left, right, update, left_new, right_new, g, gram):
+def slot_kernel(
+    where, own4, along4, across4, corner4, root, middle, left, right,
+    update, left_new, right_new,
+    g, gram, update_out, left_out, right_out, update_sem, left_sem, right_sem
+):
     my_dp, core = where[0], where[1]
-    rows = left.shape[1]
+    cap, rows, _ = left.shape
     my_x, my_y = my_dp // SIDE, my_dp % SIDE
 
     def spot(mine, moved, member):
@@ -64,22 +68,41 @@
             half, outer = 1 - half, 1 - outer
         return jnp.where(core == 0, half * 2 + member, 2 + outer if member else 1 - outer)
 
-    for step, rows4 in enumerate((own4, along4, across4, corner4)):
-        for member in range(SIDE):
-            x = spot(my_x, step // 2, member // 2)
-            y = spot(my_y, step % 2, member % 2)
-            first = pl.multiple_of((x * SIDE + y) * rows, rows)
-            g[pl.ds(first, rows), :] = rows4[member, 0]
-    block = g[...]
-    applied = contract(root[0], block, 1, 0).astype(jnp.bfloat16)
-    own = g[pl.ds(pl.multiple_of(my_dp * rows, rows), rows), :]
-    left_new[0] = decay_rate * left[0] + (1.0 - decay_rate) * contract(own, block, 1, 1)
+    spots = {
+        (step, member): pl.multiple_of(
+            (spot(my_x, step // 2, member // 2) * SIDE + spot(my_y, step % 2, member % 2)) * rows,
+            rows,
+        )
+        for step in range(SIDE)
+        for member in range(SIDE)
+    }
     group = 128 // rows
+    own_rows = pl.ds(pl.multiple_of(my_dp * rows, rows), rows)
     lanes = pl.ds(pl.multiple_of(my_dp // group * 128, 128), 128)
-    gram[...] = contract(g[:, lanes], block, 0, 0)
-    mine = gram[pl.ds(pl.multiple_of(my_dp % group * rows, rows), rows), :]
-    right_new[0] = decay_rate * right[0] + (1.0 - decay_rate) * mine
-    update[0] = contract(applied, middle[0], 1, 0).astype(jnp.bfloat16)
+    gram_rows = pl.ds(pl.multiple_of(my_dp % group * rows, rows), rows)
+    results = []
+
+    def send(source, target, sem, s):
+        copy = pltpu.make_async_copy(source.at[s], target.at[s], sem.at[s])
+        copy.start()
+        results.append(copy)
+
+    for s in range(cap):
+        for step, rows4 in enumerate((own4, along4, across4, corner4)):
+            for member in range(SIDE):
+                g[s, pl.ds(spots[step, member], rows), :] = rows4[member, s]
+        block = g[s]
+        left_gram = contract(g[s, own_rows, :], block, 1, 1)
+        left_out[s] = decay_rate * left[s] + (1.0 - decay_rate) * left_gram
+        send(left_out, left_new, left_sem, s)
+        gram[s] = contract(g[s, :, lanes], block, 0, 0)
+        right_out[s] = decay_rate * right[s] + (1.0 - decay_rate) * gram[s, gram_rows, :]
+        send(right_out, right_new, right_sem, s)
+        applied = contract(root[s], block, 1, 0).astype(jnp.bfloat16)
+        update_out[s] = contract(applied, middle[s], 1, 0).astype(jnp.bfloat16)
+        send(update_out, update, update_sem, s)
+    for copy in results:
+        copy.wait()
 
 
 def middle_kernel(basis, factor, middle):
@@ -106,39 +129,47 @@
     )(basis, factor)
 
 
+def stage_kernel(source, target, sem):
+    copy = pltpu.make_async_copy(source, target, sem)
+    copy.start()
+    copy.wait()
+
+
+def stage(x):
+    return pl.pallas_call(
+        stage_kernel,
+        in_specs=[pl.BlockSpec(memory_space=pl.ANY)],
+        out_specs=pl.BlockSpec(memory_space=pltpu.VMEM),
+        scratch_shapes=[pltpu.SemaphoreType.DMA],
+        out_shape=jax.ShapeDtypeStruct(x.shape, x.dtype),
+        compiler_params=pltpu.CompilerParams(vmem_limit_bytes=32 * 1024 * 1024),
+        cost_estimate=pl.CostEstimate(flops=0, bytes_accessed=4 * x.size, transcendentals=0),
+    )(x)
+
+
 def slot_step(where, squares, root, middle, left, right):
     cap, width, _ = middle.shape
     rows = left.shape[1]
-    square = pl.BlockSpec((SIDE, 1, rows, width), lambda s, w: (0, s, 0, 0))
-    whole = pl.BlockSpec((1, width, width), lambda s, w: (s, 0, 0))
-    slab = pl.BlockSpec((1, rows, width), lambda s, w: (s, 0, 0))
+    near = pl.BlockSpec(memory_space=pltpu.VMEM)
+    away = pl.BlockSpec(memory_space=pl.ANY)
     return pl.pallas_call(
         slot_kernel,
-        grid_spec=pltpu.PrefetchScalarGridSpec(
-            num_scalar_prefetch=1,
-            grid=(cap,),
-            in_specs=[
-                square,
-                square,
-                square,
-                square,
-                whole,
-                whole,
-                slab,
-                slab,
-            ],
-            out_specs=[whole, slab, slab],
-            scratch_shapes=[
-                pltpu.VMEM((width, width), jnp.bfloat16),
-                pltpu.VMEM((128, width), jnp.float32),
-            ],
-        ),
+        in_specs=[pl.BlockSpec(memory_space=pltpu.SMEM)] + [near] * 8,
+        out_specs=[away] * 3,
+        scratch_shapes=[
+            pltpu.VMEM((cap, width, width), jnp.bfloat16),
+            pltpu.VMEM((cap, 128, width), jnp.float32),
+            pltpu.VMEM((cap, width, width), jnp.bfloat16),
+            pltpu.VMEM(left.shape, jnp.float32),
+            pltpu.VMEM(right.shape, jnp.float32),
+        ]
+        + [pltpu.SemaphoreType.DMA((cap,))] * 3,
         out_shape=[
             jax.ShapeDtypeStruct(middle.shape, jnp.bfloat16),
             jax.ShapeDtypeStruct(left.shape, jnp.float32),
             jax.ShapeDtypeStruct(right.shape, jnp.float32),
         ],
-        compiler_params=pltpu.CompilerParams(vmem_limit_bytes=58 * 1024 * 1024),
+        compiler_params=pltpu.CompilerParams(vmem_limit_bytes=32 * 1024 * 1024),
         cost_estimate=pl.CostEstimate(
             flops=5 * cap * width**3, bytes_accessed=10 * cap * width**2, transcendentals=0
         ),
@@ -160,11 +191,14 @@
 
     summed = summed.reshape(blocks, row_tiles, 2, 4, col_tiles, 128)
     pieces = summed.transpose(1, 4, 2, 0, 3, 5).reshape(n_z, blocks * 4, 128)
-    pieces, right_basis = lax.optimization_barrier((pieces, right_basis))
+    pieces, right_basis, right_eigen, owner_map, my_dp, my_core = lax.optimization_barrier(
+        (pieces, right_basis, right_eigen, owner_map, my_dp, my_core)
+    )
+    where = jnp.stack([my_dp, my_core]).astype(jnp.int32)
     factor = (right_eigen + epsilon) ** (-0.25)
     middle = middle_step(right_basis, factor[:, None, :])
     spread = lax.all_to_all(pieces, "z", split_axis=0, concat_axis=0, tiled=True)
-    spread, middle = lax.optimization_barrier((spread, middle))
+    spread, middle, where = lax.optimization_barrier((spread, middle, where))
     swapped = lax.ppermute(spread, "core", [(0, 1), (1, 0)])
     held = jnp.concatenate([t.reshape(n_z * blocks, 4 * 128) for t in (spread, swapped)])
 
@@ -185,13 +219,12 @@
     owned = arrived.reshape(row_tiles, col_tiles, 2, cap, 4, 128)
     owned = owned.transpose(3, 0, 2, 4, 1, 5).reshape(cap, rows, width)
     n_opt = n_z * CORES
-    where = jnp.stack([my_dp, my_core]).astype(jnp.int32)
     line = broadcast_gather(owned, ALL, quads(n_opt))
-    line, root, where = lax.optimization_barrier((line, root, where))
+    line, root = lax.optimization_barrier((line, root))
     squares = [line] + [swap_corner(line, a, b) for a, b in ((False, True), (True, False), (True, True))]
 
     update, left_new, right_new = slot_step(
-        where, squares, root, middle, left_stat, right_stat
+        where, squares, stage(root), middle, left_stat, right_stat
     )
     return (update, left_new, right_new)
 

time: 182 us -> 177 us (0.973)
  blocking collectives: 36.8 us -> 49.3 us
  waiting for transfers between devices: 46.8 us -> 37.8 us
  starting transfers between devices: 58.2 us -> 54.7 us
  Pallas kernels: 15.7 us -> 12.3 us
    all_to_all x0 -> x1, blocking collectives: none -> 11.6 us  [broadcast_gather(): lax.all_to_all(copies, axis, split_axis=0, concat_axis=0, tiled=True, axi...]
    all_to_all x1 -> x0, waiting for transfers between devices: 6.99 us -> none  [broadcast_gather(): lax.all_to_all(copies, axis, split_axis=0, concat_axis=0, tiled=True, axi...]
    all_to_all x1 -> x0, starting transfers between devices: 3.48 us -> none  [broadcast_gather(): lax.all_to_all(copies, axis, split_axis=0, concat_axis=0, tiled=True, axi...]
    pallas_call x1 -> x2, Pallas kernels: 9.14 us -> 5.71 us  [the longest x1 5.53 us: slot_step(): pl.pallas_call(slot_kernel, in_specs=[pl.BlockSpec(memory_space=pltpu.SME...]
    ppermute x3, waiting for transfers between devices: 11.1 us -> 9.21 us  [swap_corner(): return lax.ppermute(x, ALL, pairs)]
  transfers between devices with their start and end apart: 8 -> 7, of which waited for: 7 -> 6; matrix products, arithmetic and copies ran while one was open for 4% -> 3% of each run, Pallas kernels for 4% -> 4%
where the time goes in v6:
time: 177 us; the launch traced here: 175 us
  starting transfers between devices  54.7 us (31%)
  blocking collectives  49.3 us (28%)
  waiting for transfers between devices  37.8 us (21%)
  between operations  14.3 us (8%)
  Pallas kernels  12.3 us (7%)
  local copies, waits for them, and re-layouts  6.07 us (3%)
    all_to_all x1, blocking collectives, body(): lax.all_to_all(deliver, 'z', split_axis=0, concat_axis=0, tiled=True)  37.7 us
    all_to_all x1, starting transfers between devices, body(): lax.all_to_all(pieces, 'z', split_axis=0, concat_axis=0, tiled=True)  32.2 us
    all_to_all x1, waiting for transfers between devices, body(): lax.all_to_all(pieces, 'z', split_axis=0, concat_axis=0, tiled=True)  15.4 us
    all_to_all x1, waiting for transfers between devices, body(): parts = lax.all_to_all(sent, 'dp', split_axis=0, concat_axis=0, tiled=True)  11.7 us
    all_to_all x1, blocking collectives, broadcast_gather(): lax.all_to_all(copies, axis, split_axis=0, concat_axis=0, tiled=True, axi...  11.6 us
    ppermute x3, waiting for transfers between devices, swap_corner(): return lax.ppermute(x, ALL, pairs)  9.21 us
    ppermute x3, starting transfers between devices, swap_corner(): return lax.ppermute(x, ALL, pairs)  8.36 us
    all_to_all x1, starting transfers between devices, body(): parts = lax.all_to_all(sent, 'dp', split_axis=0, concat_axis=0, tiled=True)  7.58 us
  transfers between devices with their start and end apart: 7, of which 6 were waited for; matrix products, arithmetic and copies ran while one was open for 3% of the time, Pallas kernels for 4%

profile of v6, /device:TPU:1, one launch (start us, length us, event | category | flops | bytes accessed | tf_op | source)
XLA Modules:
  0.0 175.2 jit_solution(9105947551433058892)
XLA Ops:
  7.2 0.7 all-gather.2.cloned.1.call-update
  7.9 2.3 %copy.19 = bf16[16,2,32,512]{3,2,1,0:T(8,128)(2,1)} copy(bf16[16,2,32,512]{3,2,0,1:T(8,128)(2,1)} %bitcast.11) | data formatting | bytes 2097152 | tf_op jit(solution)/shard_map/transpose | solution.py:188
  10.2 7.6 %all-to-all-start = ((bf16[16,2,32,512]{3,2,1,0:T(8,128)(2,1)}), bf16[16,2,32,512]{3,2,1,0:T(8,128)(2,1)S(1)}, u32[]{:S(2)}, u32[]{:S(2)}) async-start(bf16[16,2,32,512]{3,2,1,0:T(8,128)(2,1)} %copy.19), calls=%async_computation | async-start | bytes 2097152 | tf_op jit(solution)/shard_map/all_to_all | solution.py:189
  17.8 11.7 %all-to-all-done = bf16[16,2,32,512]{3,2,1,0:T(8,128)(2,1)S(1)} async-done(((bf16[16,2,32,512]{3,2,1,0:T(8,128)(2,1)}), bf16[16,2,32,512]{3,2,1,0:T(8,128)(2,1)S(1)}, u32[]{:S(2)}, u32[]{:S(2)}) %all-to-all-start) | async-done | bytes 1048608 | tf_op jit(solution)/shard_map/all_to_all | solution.py:189
  29.8 0.7 copy.20
  30.4 32.2 %all-to-all-start.1 = ((bf16[32,8,128]{2,1,0:T(8,128)(2,1)}), bf16[32,8,128]{2,1,0:T(8,128)(2,1)S(1)}, u32[]{:S(2)}, u32[]{:S(2)}) async-start(bf16[32,8,128]{2,1,0:T(8,128)(2,1)} %bitcast.3), calls=%async_computation.1 | async-start | bytes 131072 | tf_op jit(solution)/shard_map/all_to_all | solution.py:200
  62.6 0.2 convert_reduce_fusion
  62.9 0.6 broadcast_in_dim.8.factor
  64.0 6.6 %shard_map.94.middle = bf16[5,512,512]{2,1,0:T(8,128)(2,1)} custom-call(bf16[5,512,512]{2,1,0:T(8,128)(2,1)} %basis, f32[5,1,512]{2,1,0:T(1,128)} %broadcast_in_dim.8.factor), custom_call_target="tpu_custom_call" | custom-call | flops 2684354560 | bytes 5242880 | tf_op jit(solution)/shard_map/pallas_call | solution.py:119
  70.6 15.4 %all-to-all-done.1 = bf16[32,8,128]{2,1,0:T(8,128)(2,1)S(1)} async-done(((bf16[32,8,128]{2,1,0:T(8,128)(2,1)}), bf16[32,8,128]{2,1,0:T(8,128)(2,1)S(1)}, u32[]{:S(2)}, u32[]{:S(2)}) %all-to-all-start.1) | async-done | bytes 65568 | tf_op jit(solution)/shard_map/all_to_all | solution.py:200
  86.0 6.5 %collective-permute-start = (bf16[32,8,128]{2,1,0:T(8,128)(2,1)S(1)}, bf16[32,8,128]{2,1,0:T(8,128)(2,1)S(1)}, u32[]{:S(2)}, u32[]{:S(2)}) collective-permute-start(bf16[32,8,128]{2,1,0:T(8,128)(2,1)S(1)} %all-to-all-done.1), channel_id=1, source_target_pairs={{0,1},{1,0},{2,3},{3,2},{4,5},{5,4},{6,7},{7,6},{8,9},{9,8},{10,11... | collective-permute-start | bytes 196616 | tf_op jit(solution)/shard_map/ppermute | solution.py:202
  92.6 0.8 collective-permute-done
  93.5 0.2 convolution_convert_fusion
  93.7 37.7 %all_to_all.20 = bf16[32,5,4,128]{3,2,1,0:T(4,128)(2,1)S(1)} all-to-all(bf16[32,5,4,128]{3,2,1,0:T(4,128)(2,1)S(1)} %reshape.44), channel_id=1, replica_groups=mesh['dp'=16,'z'=32,'core'=2] {'z'}, dimensions={0} | all-to-all | bytes 327680 | tf_op jit(solution)/shard_map/all_to_all | solution.py:217
  131.6 11.6 %all_to_all.21.own4 = bf16[4,5,32,512]{3,2,1,0:T(8,128)(2,1)S(1)} all-to-all(bf16[4,5,32,512]{3,2,1,0:T(8,128)(2,1)S(1)} %broadcast_in_dim.10), channel_id=1, replica_groups={{0,64,256,320},{128,192,384,448},{512,576,768,832},{640,704,896,960},{3..., dimensions={0} | all-to-all | bytes 1310720 | tf_op jit(solution)/shard_map/all_to_all | solution.py:20
  143.3 1.9 %collective-permute-start.3 = (bf16[4,5,32,512]{3,2,1,0:T(8,128)(2,1)S(1)}, bf16[4,5,32,512]{3,2,1,0:T(8,128)(2,1)S(1)}, u32[]{:S(2)}, u32[]{:S(2)}) collective-permute-start(bf16[4,5,32,512]{3,2,1,0:T(8,128)(2,1)S(1)} %all_to_all.21.own4), channel_id=1, source_target_pairs={{0,960},{1,321},{2,962},{3,323},{4,964},{5,325},{6,966},{7,327},{8... | collective-permute-start | bytes 1966088 | tf_op jit(solution)/shard_map/ppermute | solution.py:46
  145.2 2.2 %collective-permute-start.2 = (bf16[4,5,32,512]{3,2,1,0:T(8,128)(2,1)S(1)}, bf16[4,5,32,512]{3,2,1,0:T(8,128)(2,1)S(1)}, u32[]{:S(2)}, u32[]{:S(2)}) collective-permute-start(bf16[4,5,32,512]{3,2,1,0:T(8,128)(2,1)S(1)} %all_to_all.21.own4), channel_id=1, source_target_pairs={{0,768},{1,257},{2,770},{3,259},{4,772},{5,261},{6,774},{7,263},{8... | collective-permute-start | bytes 1966088 | tf_op jit(solution)/shard_map/ppermute | solution.py:46
  147.4 4.3 %collective-permute-start.1 = (bf16[4,5,32,512]{3,2,1,0:T(8,128)(2,1)S(1)}, bf16[4,5,32,512]{3,2,1,0:T(8,128)(2,1)S(1)}, u32[]{:S(2)}, u32[]{:S(2)}) collective-permute-start(bf16[4,5,32,512]{3,2,1,0:T(8,128)(2,1)S(1)} %all_to_all.21.own4), channel_id=1, source_target_pairs={{0,192},{1,65},{2,194},{3,67},{4,196},{5,69},{6,198},{7,71},{8,200... | collective-permute-start | bytes 1966088 | tf_op jit(solution)/shard_map/ppermute | solution.py:46
  151.7 1.7 copy-done
  153.4 0.2 shard_map.95.root
  153.6 2.2 %collective-permute-done.3.corner4 = bf16[4,5,32,512]{3,2,1,0:T(8,128)(2,1)S(1)} collective-permute-done((bf16[4,5,32,512]{3,2,1,0:T(8,128)(2,1)S(1)}, bf16[4,5,32,512]{3,2,1,0:T(8,128)(2,1)S(1)}, u32[]{:S(2)}, u32[]{:S(2)}) %collective-permute-start.3) | collective-permute-done | bytes 655392 | tf_op jit(solution)/shard_map/ppermute | solution.py:46
  155.8 4.9 %collective-permute-done.2.across4 = bf16[4,5,32,512]{3,2,1,0:T(8,128)(2,1)S(1)} collective-permute-done((bf16[4,5,32,512]{3,2,1,0:T(8,128)(2,1)S(1)}, bf16[4,5,32,512]{3,2,1,0:T(8,128)(2,1)S(1)}, u32[]{:S(2)}, u32[]{:S(2)}) %collective-permute-start.2) | collective-permute-done | bytes 655392 | tf_op jit(solution)/shard_map/ppermute | solution.py:46
  160.7 2.1 %collective-permute-done.1.along4 = bf16[4,5,32,512]{3,2,1,0:T(8,128)(2,1)S(1)} collective-permute-done((bf16[4,5,32,512]{3,2,1,0:T(8,128)(2,1)S(1)}, bf16[4,5,32,512]{3,2,1,0:T(8,128)(2,1)S(1)}, u32[]{:S(2)}, u32[]{:S(2)}) %collective-permute-start.1) | collective-permute-done | bytes 655392 | tf_op jit(solution)/shard_map/ppermute | solution.py:46
  162.8 5.5 %shard_map.96 = (bf16[5,512,512]{2,1,0:T(8,128)(2,1)}, f32[5,32,512]{2,1,0:T(8,128)}, f32[5,32,512]{2,1,0:T(8,128)}) custom-call(s32[2]{0:T(128)S(1)} %pad_add_fusion.where, bf16[4,5,32,512]{3,2,1,0:T(8,128)(2,1)S(1)} %all_to_all.21.own4, bf16[4,5,32,512]{3,2,1,0:T(8,128)(2,1)S(1)} %collective-permute-done.1.along4, ...), custom_call_target="tpu_custom_call" | custom-call | flops 3355443200 | bytes 13107200 | tf_op jit(solution)/shard_map/pallas_call | solution.py:155
  (29 shorter events, 1.2 us)
Async XLA Ops:
  7.2 136.1 %all-gather.2.cloned.1.call-start = ((), (), s32[]{:S(2)}) async-start(), calls=%async_computation.4 | async-start | bytes 2785280 | tf_op jit(solution)/shard_map/all_gather | solution.py:186
  7.9 54.7 %copy-start.5 = (s32[128]{0:T(128)S(1)}, s32[128]{0:T(128)}, u32[]{:S(2)}) copy-start(s32[128]{0:T(128)} %param.8) | copy-start | bytes 1540
  7.9 54.9 %copy-start.4 = (f32[5,512]{1,0:T(8,128)S(1)}, f32[5,512]{1,0:T(8,128)}, u32[]{:S(2)}) copy-start(f32[5,512]{1,0:T(8,128)} %param.11) | copy-start | bytes 30724
  10.2 19.3 %all-to-all-start = ((bf16[16,2,32,512]{3,2,1,0:T(8,128)(2,1)}), bf16[16,2,32,512]{3,2,1,0:T(8,128)(2,1)S(1)}, u32[]{:S(2)}, u32[]{:S(2)}) async-start(bf16[16,2,32,512]{3,2,1,0:T(8,128)(2,1)} %copy.19), calls=%async_computation | async-start | bytes 2097152 | tf_op jit(solution)/shard_map/all_to_all | solution.py:189
  30.4 55.6 %all-to-all-start.1 = ((bf16[32,8,128]{2,1,0:T(8,128)(2,1)}), bf16[32,8,128]{2,1,0:T(8,128)(2,1)S(1)}, u32[]{:S(2)}, u32[]{:S(2)}) async-start(bf16[32,8,128]{2,1,0:T(8,128)(2,1)} %bitcast.3), calls=%async_computation.1 | async-start | bytes 131072 | tf_op jit(solution)/shard_map/all_to_all | solution.py:200
  86.0 7.4 %collective-permute-start = (bf16[32,8,128]{2,1,0:T(8,128)(2,1)S(1)}, bf16[32,8,128]{2,1,0:T(8,128)(2,1)S(1)}, u32[]{:S(2)}, u32[]{:S(2)}) collective-permute-start(bf16[32,8,128]{2,1,0:T(8,128)(2,1)S(1)} %all-to-all-done.1), channel_id=1, source_target_pairs={{0,1},{1,0},{2,3},{3,2},{4,5},{5,4},{6,7},{7,6},{8,9},{9,8},{10,11... | collective-permute-start | bytes 196616 | tf_op jit(solution)/shard_map/ppermute | solution.py:202
  131.6 31.2 %copy-start.1 = (f32[5,32,512]{2,1,0:T(8,128)S(1)}, f32[5,32,512]{2,1,0:T(8,128)}, u32[]{:S(2)}) copy-start(f32[5,32,512]{2,1,0:T(8,128)} %left.1) | copy-start | bytes 983044
  131.6 31.2 %copy-start.2 = (f32[5,32,512]{2,1,0:T(8,128)S(1)}, f32[5,32,512]{2,1,0:T(8,128)}, u32[]{:S(2)}) copy-start(f32[5,32,512]{2,1,0:T(8,128)} %right.1) | copy-start | bytes 983044
  143.3 12.6 %collective-permute-start.3 = (bf16[4,5,32,512]{3,2,1,0:T(8,128)(2,1)S(1)}, bf16[4,5,32,512]{3,2,1,0:T(8,128)(2,1)S(1)}, u32[]{:S(2)}, u32[]{:S(2)}) collective-permute-start(bf16[4,5,32,512]{3,2,1,0:T(8,128)(2,1)S(1)} %all_to_all.21.own4), channel_id=1, source_target_pairs={{0,960},{1,321},{2,962},{3,323},{4,964},{5,325},{6,966},{7,327},{8... | collective-permute-start | bytes 1966088 | tf_op jit(solution)/shard_map/ppermute | solution.py:46
  145.2 15.5 %collective-permute-start.2 = (bf16[4,5,32,512]{3,2,1,0:T(8,128)(2,1)S(1)}, bf16[4,5,32,512]{3,2,1,0:T(8,128)(2,1)S(1)}, u32[]{:S(2)}, u32[]{:S(2)}) collective-permute-start(bf16[4,5,32,512]{3,2,1,0:T(8,128)(2,1)S(1)} %all_to_all.21.own4), channel_id=1, source_target_pairs={{0,768},{1,257},{2,770},{3,259},{4,772},{5,261},{6,774},{7,263},{8... | collective-permute-start | bytes 1966088 | tf_op jit(solution)/shard_map/ppermute | solution.py:46
  147.4 15.5 %collective-permute-start.1 = (bf16[4,5,32,512]{3,2,1,0:T(8,128)(2,1)S(1)}, bf16[4,5,32,512]{3,2,1,0:T(8,128)(2,1)S(1)}, u32[]{:S(2)}, u32[]{:S(2)}) collective-permute-start(bf16[4,5,32,512]{3,2,1,0:T(8,128)(2,1)S(1)} %all_to_all.21.own4), channel_id=1, source_target_pairs={{0,192},{1,65},{2,194},{3,67},{4,196},{5,69},{6,198},{7,71},{8,200... | collective-permute-start | bytes 1966088 | tf_op jit(solution)/shard_map/ppermute | solution.py:46
  151.7 1.7 copy-start
  153.4 9.4 %copy-start.3 = (bf16[5,512,512]{2,1,0:T(8,128)(2,1)S(1)}, bf16[5,512,512]{2,1,0:T(8,128)(2,1)}, u32[]{:S(2)}) copy-start(bf16[5,512,512]{2,1,0:T(8,128)(2,1)} %shard_map.94.middle) | copy-start | bytes 7864324
Sparse Core Ops, SparseCore 0:
  12.2 90.1 all-gather.1

commit v7 on v6

--- a/solution.py
+++ b/solution.py
@@ -186,19 +186,19 @@
     root = lax.all_gather(left_root, "dp", axis=1, tiled=True)
 
     sent = gradients.reshape(blocks, n_dp, rows, width).transpose(1, 0, 2, 3)
+    sent, my_dp, my_core = lax.optimization_barrier((sent, my_dp, my_core))
     parts = lax.all_to_all(sent, "dp", split_axis=0, concat_axis=0, tiled=True)
     summed = jnp.sum(parts.astype(jnp.float32), axis=0).astype(jnp.bfloat16)
 
     summed = summed.reshape(blocks, row_tiles, 2, 4, col_tiles, 128)
     pieces = summed.transpose(1, 4, 2, 0, 3, 5).reshape(n_z, blocks * 4, 128)
-    pieces, right_basis, right_eigen, owner_map, my_dp, my_core = lax.optimization_barrier(
-        (pieces, right_basis, right_eigen, owner_map, my_dp, my_core)
+    pieces, right_eigen, owner_map, my_dp, my_core = lax.optimization_barrier(
+        (pieces, right_eigen, owner_map, my_dp, my_core)
     )
     where = jnp.stack([my_dp, my_core]).astype(jnp.int32)
-    factor = (right_eigen + epsilon) ** (-0.25)
-    middle = middle_step(right_basis, factor[:, None, :])
+    factor = ((right_eigen + epsilon) ** (-0.25))[:, None, :]
     spread = lax.all_to_all(pieces, "z", split_axis=0, concat_axis=0, tiled=True)
-    spread, middle, where = lax.optimization_barrier((spread, middle, where))
+    spread, where, factor = lax.optimization_barrier((spread, where, factor))
     swapped = lax.ppermute(spread, "core", [(0, 1), (1, 0)])
     held = jnp.concatenate([t.reshape(n_z * blocks, 4 * 128) for t in (spread, swapped)])
 
@@ -214,7 +214,10 @@
     pick = (jnp.arange(n_z * cap, dtype=jnp.int32)[:, None] == place[None, :]).astype(jnp.bfloat16)
     chosen = jnp.dot(pick, held, preferred_element_type=jnp.float32).astype(jnp.bfloat16)
     deliver = chosen.reshape(n_z, cap, 4, 128)
+    deliver, right_basis, factor = lax.optimization_barrier((deliver, right_basis, factor))
+    middle = middle_step(right_basis, factor)
     arrived = lax.all_to_all(deliver, "z", split_axis=0, concat_axis=0, tiled=True)
+    arrived, middle = lax.optimization_barrier((arrived, middle))
 
     owned = arrived.reshape(row_tiles, col_tiles, 2, cap, 4, 128)
     owned = owned.transpose(3, 0, 2, 4, 1, 5).reshape(cap, rows, width)

time: 177 us -> 175 us (0.989)
  waiting for transfers between devices: 37.8 us -> 59.2 us
  blocking collectives: 49.3 us -> 30.8 us
  starting transfers between devices: 54.7 us -> 50.1 us
    all_to_all x1, blocking collectives: 37.7 us -> 19.1 us  [body(): parts = lax.all_to_all(sent, 'dp', split_axis=0, concat_axis=0, tiled=True)]
    all_to_all x1, waiting for transfers between devices: 11.7 us -> 26.5 us  [body(): lax.all_to_all(deliver, 'z', split_axis=0, concat_axis=0, tiled=True)]
    all_to_all x1, waiting for transfers between devices: 15.4 us -> 22 us  [body(): lax.all_to_all(pieces, 'z', split_axis=0, concat_axis=0, tiled=True)]
    all_to_all x1, starting transfers between devices: 7.58 us -> 3.86 us  [body(): lax.all_to_all(deliver, 'z', split_axis=0, concat_axis=0, tiled=True)]
    transpose x1 -> x0, local copies, waits for them, and re-layouts: 2.32 us -> none  [body(): sent = gradients.reshape(blocks, n_dp, rows, width).transpose(1, 0, 2, 3)]
where the time goes in v7:
time: 175 us; the launch traced here: 173 us
  waiting for transfers between devices  59.2 us (34%)
  starting transfers between devices  50.1 us (29%)
  blocking collectives  30.8 us (18%)
  between operations  14.2 us (8%)
  Pallas kernels  12.3 us (7%)
  local copies, waits for them, and re-layouts  5.74 us (3%)
    all_to_all x1, starting transfers between devices, body(): lax.all_to_all(pieces, 'z', split_axis=0, concat_axis=0, tiled=True)  32.6 us
    all_to_all x1, waiting for transfers between devices, body(): lax.all_to_all(deliver, 'z', split_axis=0, concat_axis=0, tiled=True)  26.5 us
    all_to_all x1, waiting for transfers between devices, body(): lax.all_to_all(pieces, 'z', split_axis=0, concat_axis=0, tiled=True)  22 us
    all_to_all x1, blocking collectives, body(): parts = lax.all_to_all(sent, 'dp', split_axis=0, concat_axis=0, tiled=True)  19.1 us
    all_to_all x1, blocking collectives, broadcast_gather(): lax.all_to_all(copies, axis, split_axis=0, concat_axis=0, tiled=True, axi...  11.6 us
    ppermute x3, waiting for transfers between devices, swap_corner(): return lax.ppermute(x, ALL, pairs)  9.21 us
    ppermute x3, starting transfers between devices, swap_corner(): return lax.ppermute(x, ALL, pairs)  8.36 us
    pallas_call x1, Pallas kernels, middle_step(): pl.pallas_call(middle_kernel, grid=(cap,), in_specs=[whole, pl.BlockSpec(...  6.59 us
  transfers between devices with their start and end apart: 7, of which 6 were waited for; matrix products, arithmetic and copies ran while one was open for 3% of the time, Pallas kernels for 4%

profile of v7, /device:TPU:1, one launch (start us, length us, event | category | flops | bytes accessed | tf_op | source)
XLA Modules:
  0.0 173.2 jit_solution(5370636910669463080)
XLA Ops:
  7.2 0.7 all-gather.2.cloned.1.call-update
  7.9 1.3 copy.19
  9.2 19.1 %all_to_all.20 = bf16[16,2,32,512]{3,2,1,0:T(8,128)(2,1)S(1)} all-to-all(bf16[16,2,32,512]{3,2,1,0:T(8,128)(2,1)S(1)} %copy.19), channel_id=1, replica_groups=mesh['dp'=16,'z'=32,'core'=2] {'dp'}, dimensions={0} | all-to-all | bytes 2097152 | tf_op jit(solution)/shard_map/all_to_all | solution.py:190
  28.6 0.7 copy.20
  29.2 32.6 %all-to-all-start.1 = ((bf16[32,8,128]{2,1,0:T(8,128)(2,1)}), bf16[32,8,128]{2,1,0:T(8,128)(2,1)S(1)}, u32[]{:S(2)}, u32[]{:S(2)}) async-start(bf16[32,8,128]{2,1,0:T(8,128)(2,1)} %bitcast.3), calls=%async_computation.1 | async-start | bytes 131072 | tf_op jit(solution)/shard_map/all_to_all | solution.py:200
  62.0 0.6 broadcast_in_dim.8.factor
  63.2 22.0 %all-to-all-done.1 = bf16[32,8,128]{2,1,0:T(8,128)(2,1)S(1)} async-done(((bf16[32,8,128]{2,1,0:T(8,128)(2,1)}), bf16[32,8,128]{2,1,0:T(8,128)(2,1)S(1)}, u32[]{:S(2)}, u32[]{:S(2)}) %all-to-all-start.1) | async-done | bytes 65568 | tf_op jit(solution)/shard_map/all_to_all | solution.py:200
  85.2 5.3 %collective-permute-start = (bf16[32,8,128]{2,1,0:T(8,128)(2,1)S(1)}, bf16[32,8,128]{2,1,0:T(8,128)(2,1)S(1)}, u32[]{:S(2)}, u32[]{:S(2)}) collective-permute-start(bf16[32,8,128]{2,1,0:T(8,128)(2,1)S(1)} %all-to-all-done.1), channel_id=1, source_target_pairs={{0,1},{1,0},{2,3},{3,2},{4,5},{5,4},{6,7},{7,6},{8,9},{9,8},{10,11... | collective-permute-start | bytes 196616 | tf_op jit(solution)/shard_map/ppermute | solution.py:202
  90.7 0.8 collective-permute-done
  91.5 0.2 convolution_convert_fusion
  91.7 0.7 reshape.44
  92.4 3.9 %all-to-all-start.2 = ((bf16[32,5,4,128]{3,2,1,0:T(4,128)(2,1)}), bf16[32,5,4,128]{3,2,1,0:T(4,128)(2,1)S(1)}, u32[]{:S(2)}, u32[]{:S(2)}) async-start(bf16[32,5,4,128]{3,2,1,0:T(4,128)(2,1)} %reshape.44), calls=%async_computation.2 | async-start | bytes 327680 | tf_op jit(solution)/shard_map/all_to_all | solution.py:219
  96.3 6.6 %shard_map.94.middle = bf16[5,512,512]{2,1,0:T(8,128)(2,1)} custom-call(bf16[5,512,512]{2,1,0:T(8,128)(2,1)} %basis, f32[5,1,512]{2,1,0:T(1,128)} %broadcast_in_dim.8.factor), custom_call_target="tpu_custom_call" | custom-call | flops 2684354560 | bytes 5242880 | tf_op jit(solution)/shard_map/pallas_call | solution.py:119
  102.9 26.5 %all-to-all-done.2 = bf16[32,5,4,128]{3,2,1,0:T(4,128)(2,1)S(1)} async-done(((bf16[32,5,4,128]{3,2,1,0:T(4,128)(2,1)}), bf16[32,5,4,128]{3,2,1,0:T(4,128)(2,1)S(1)}, u32[]{:S(2)}, u32[]{:S(2)}) %all-to-all-start.2) | async-done | bytes 163872 | tf_op jit(solution)/shard_map/all_to_all | solution.py:219
  129.6 11.6 %all_to_all.21.own4 = bf16[4,5,32,512]{3,2,1,0:T(8,128)(2,1)S(1)} all-to-all(bf16[4,5,32,512]{3,2,1,0:T(8,128)(2,1)S(1)} %broadcast_in_dim.10), channel_id=1, replica_groups={{0,64,256,320},{128,192,384,448},{512,576,768,832},{640,704,896,960},{3..., dimensions={0} | all-to-all | bytes 1310720 | tf_op jit(solution)/shard_map/all_to_all | solution.py:20
  141.2 1.9 %collective-permute-start.3 = (bf16[4,5,32,512]{3,2,1,0:T(8,128)(2,1)S(1)}, bf16[4,5,32,512]{3,2,1,0:T(8,128)(2,1)S(1)}, u32[]{:S(2)}, u32[]{:S(2)}) collective-permute-start(bf16[4,5,32,512]{3,2,1,0:T(8,128)(2,1)S(1)} %all_to_all.21.own4), channel_id=1, source_target_pairs={{0,960},{1,321},{2,962},{3,323},{4,964},{5,325},{6,966},{7,327},{8... | collective-permute-start | bytes 1966088 | tf_op jit(solution)/shard_map/ppermute | solution.py:46
  143.2 2.4 %collective-permute-start.2 = (bf16[4,5,32,512]{3,2,1,0:T(8,128)(2,1)S(1)}, bf16[4,5,32,512]{3,2,1,0:T(8,128)(2,1)S(1)}, u32[]{:S(2)}, u32[]{:S(2)}) collective-permute-start(bf16[4,5,32,512]{3,2,1,0:T(8,128)(2,1)S(1)} %all_to_all.21.own4), channel_id=1, source_target_pairs={{0,768},{1,257},{2,770},{3,259},{4,772},{5,261},{6,774},{7,263},{8... | collective-permute-start | bytes 1966088 | tf_op jit(solution)/shard_map/ppermute | solution.py:46
  145.6 4.1 %collective-permute-start.1 = (bf16[4,5,32,512]{3,2,1,0:T(8,128)(2,1)S(1)}, bf16[4,5,32,512]{3,2,1,0:T(8,128)(2,1)S(1)}, u32[]{:S(2)}, u32[]{:S(2)}) collective-permute-start(bf16[4,5,32,512]{3,2,1,0:T(8,128)(2,1)S(1)} %all_to_all.21.own4), channel_id=1, source_target_pairs={{0,192},{1,65},{2,194},{3,67},{4,196},{5,69},{6,198},{7,71},{8,200... | collective-permute-start | bytes 1966088 | tf_op jit(solution)/shard_map/ppermute | solution.py:46
  149.6 1.7 copy-done
  151.4 0.2 shard_map.95.root
  151.6 2.2 %collective-permute-done.3.corner4 = bf16[4,5,32,512]{3,2,1,0:T(8,128)(2,1)S(1)} collective-permute-done((bf16[4,5,32,512]{3,2,1,0:T(8,128)(2,1)S(1)}, bf16[4,5,32,512]{3,2,1,0:T(8,128)(2,1)S(1)}, u32[]{:S(2)}, u32[]{:S(2)}) %collective-permute-start.3) | collective-permute-done | bytes 655392 | tf_op jit(solution)/shard_map/ppermute | solution.py:46
  153.8 5.1 %collective-permute-done.2.across4 = bf16[4,5,32,512]{3,2,1,0:T(8,128)(2,1)S(1)} collective-permute-done((bf16[4,5,32,512]{3,2,1,0:T(8,128)(2,1)S(1)}, bf16[4,5,32,512]{3,2,1,0:T(8,128)(2,1)S(1)}, u32[]{:S(2)}, u32[]{:S(2)}) %collective-permute-start.2) | collective-permute-done | bytes 655392 | tf_op jit(solution)/shard_map/ppermute | solution.py:46
  158.9 1.9 %collective-permute-done.1.along4 = bf16[4,5,32,512]{3,2,1,0:T(8,128)(2,1)S(1)} collective-permute-done((bf16[4,5,32,512]{3,2,1,0:T(8,128)(2,1)S(1)}, bf16[4,5,32,512]{3,2,1,0:T(8,128)(2,1)S(1)}, u32[]{:S(2)}, u32[]{:S(2)}) %collective-permute-start.1) | collective-permute-done | bytes 655392 | tf_op jit(solution)/shard_map/ppermute | solution.py:46
  160.8 5.5 %shard_map.96 = (bf16[5,512,512]{2,1,0:T(8,128)(2,1)}, f32[5,32,512]{2,1,0:T(8,128)}, f32[5,32,512]{2,1,0:T(8,128)}) custom-call(s32[2]{0:T(128)S(1)} %pad_add_fusion.where, bf16[4,5,32,512]{3,2,1,0:T(8,128)(2,1)S(1)} %all_to_all.21.own4, bf16[4,5,32,512]{3,2,1,0:T(8,128)(2,1)S(1)} %collective-permute-done.1.along4, ...), custom_call_target="tpu_custom_call" | custom-call | flops 3355443200 | bytes 13107200 | tf_op jit(solution)/shard_map/pallas_call | solution.py:155
  (29 shorter events, 1.4 us)
Async XLA Ops:
  7.2 134.1 %all-gather.2.cloned.1.call-start = ((), (), s32[]{:S(2)}) async-start(), calls=%async_computation.4 | async-start | bytes 2785280 | tf_op jit(solution)/shard_map/all_gather | solution.py:186
  7.9 53.9 %copy-start.4 = (f32[5,512]{1,0:T(8,128)S(1)}, f32[5,512]{1,0:T(8,128)}, u32[]{:S(2)}) copy-start(f32[5,512]{1,0:T(8,128)} %param.11) | copy-start | bytes 30724
  7.9 53.9 %copy-start.5 = (s32[128]{0:T(128)S(1)}, s32[128]{0:T(128)}, u32[]{:S(2)}) copy-start(s32[128]{0:T(128)} %param.8) | copy-start | bytes 1540
  29.2 56.0 %all-to-all-start.1 = ((bf16[32,8,128]{2,1,0:T(8,128)(2,1)}), bf16[32,8,128]{2,1,0:T(8,128)(2,1)S(1)}, u32[]{:S(2)}, u32[]{:S(2)}) async-start(bf16[32,8,128]{2,1,0:T(8,128)(2,1)} %bitcast.3), calls=%async_computation.1 | async-start | bytes 131072 | tf_op jit(solution)/shard_map/all_to_all | solution.py:200
  85.2 6.2 %collective-permute-start = (bf16[32,8,128]{2,1,0:T(8,128)(2,1)S(1)}, bf16[32,8,128]{2,1,0:T(8,128)(2,1)S(1)}, u32[]{:S(2)}, u32[]{:S(2)}) collective-permute-start(bf16[32,8,128]{2,1,0:T(8,128)(2,1)S(1)} %all-to-all-done.1), channel_id=1, source_target_pairs={{0,1},{1,0},{2,3},{3,2},{4,5},{5,4},{6,7},{7,6},{8,9},{9,8},{10,11... | collective-permute-start | bytes 196616 | tf_op jit(solution)/shard_map/ppermute | solution.py:202
  92.4 37.0 %all-to-all-start.2 = ((bf16[32,5,4,128]{3,2,1,0:T(4,128)(2,1)}), bf16[32,5,4,128]{3,2,1,0:T(4,128)(2,1)S(1)}, u32[]{:S(2)}, u32[]{:S(2)}) async-start(bf16[32,5,4,128]{3,2,1,0:T(4,128)(2,1)} %reshape.44), calls=%async_computation.2 | async-start | bytes 327680 | tf_op jit(solution)/shard_map/all_to_all | solution.py:219
  129.6 31.2 %copy-start.1 = (f32[5,32,512]{2,1,0:T(8,128)S(1)}, f32[5,32,512]{2,1,0:T(8,128)}, u32[]{:S(2)}) copy-start(f32[5,32,512]{2,1,0:T(8,128)} %left.1) | copy-start | bytes 983044
  129.6 31.2 %copy-start.2 = (f32[5,32,512]{2,1,0:T(8,128)S(1)}, f32[5,32,512]{2,1,0:T(8,128)}, u32[]{:S(2)}) copy-start(f32[5,32,512]{2,1,0:T(8,128)} %right.1) | copy-start | bytes 983044
  141.2 12.6 %collective-permute-start.3 = (bf16[4,5,32,512]{3,2,1,0:T(8,128)(2,1)S(1)}, bf16[4,5,32,512]{3,2,1,0:T(8,128)(2,1)S(1)}, u32[]{:S(2)}, u32[]{:S(2)}) collective-permute-start(bf16[4,5,32,512]{3,2,1,0:T(8,128)(2,1)S(1)} %all_to_all.21.own4), channel_id=1, source_target_pairs={{0,960},{1,321},{2,962},{3,323},{4,964},{5,325},{6,966},{7,327},{8... | collective-permute-start | bytes 1966088 | tf_op jit(solution)/shard_map/ppermute | solution.py:46
  143.2 15.8 %collective-permute-start.2 = (bf16[4,5,32,512]{3,2,1,0:T(8,128)(2,1)S(1)}, bf16[4,5,32,512]{3,2,1,0:T(8,128)(2,1)S(1)}, u32[]{:S(2)}, u32[]{:S(2)}) collective-permute-start(bf16[4,5,32,512]{3,2,1,0:T(8,128)(2,1)S(1)} %all_to_all.21.own4), channel_id=1, source_target_pairs={{0,768},{1,257},{2,770},{3,259},{4,772},{5,261},{6,774},{7,263},{8... | collective-permute-start | bytes 1966088 | tf_op jit(solution)/shard_map/ppermute | solution.py:46
  145.6 15.2 %collective-permute-start.1 = (bf16[4,5,32,512]{3,2,1,0:T(8,128)(2,1)S(1)}, bf16[4,5,32,512]{3,2,1,0:T(8,128)(2,1)S(1)}, u32[]{:S(2)}, u32[]{:S(2)}) collective-permute-start(bf16[4,5,32,512]{3,2,1,0:T(8,128)(2,1)S(1)} %all_to_all.21.own4), channel_id=1, source_target_pairs={{0,192},{1,65},{2,194},{3,67},{4,196},{5,69},{6,198},{7,71},{8,200... | collective-permute-start | bytes 1966088 | tf_op jit(solution)/shard_map/ppermute | solution.py:46
  149.6 1.7 %copy-start = (bf16[5,512,512]{2,1,0:T(8,128)(2,1)S(1)}, bf16[5,512,512]{2,1,0:T(8,128)(2,1)}, u32[]{:S(2)}) copy-start(bf16[5,512,512]{2,1,0:T(8,128)(2,1)} %all-gather.2.cloned.1.call-done.source) | copy-start | bytes 7864324
  151.4 9.4 %copy-start.3 = (bf16[5,512,512]{2,1,0:T(8,128)(2,1)S(1)}, bf16[5,512,512]{2,1,0:T(8,128)(2,1)}, u32[]{:S(2)}) copy-start(bf16[5,512,512]{2,1,0:T(8,128)(2,1)} %shard_map.94.middle) | copy-start | bytes 7864324
Sparse Core Ops, SparseCore 0:
  12.2 90.1 all-gather.1

commit v8 on v7

--- a/solution.py
+++ b/solution.py
@@ -12,6 +12,7 @@
 ALL = ("dp", "z", "core")
 EVEN = ((0, 1), (2, 3))
 ODD = ((1, 2), (0, 3))
+MOVES = ((False, True), (True, False), (True, True))
 
 
 def broadcast_gather(x, axis, groups=None):
@@ -32,9 +33,9 @@
     return groups
 
 
-def swap_corner(x, across, along):
+def swap_corner(x, across, along, parity):
     def partner(v, core, moved):
-        return v if not moved else (SIDE - 1 - v if core == 0 else v ^ 1)
+        return v if not moved else (SIDE - 1 - v if core == parity else v ^ 1)
 
     n_opt = lax.axis_size("z") * CORES
     pairs = []
@@ -129,22 +130,38 @@
     )(basis, factor)
 
 
-def stage_kernel(source, target, sem):
-    copy = pltpu.make_async_copy(source, target, sem)
-    copy.start()
-    copy.wait()
-
-
-def stage(x):
+def stage_kernel(where, own4, along4, across4, corner4, whole):
+    my_dp, core = where[0], where[1]
+    cap, rows = own4.shape[1], own4.shape[2]
+
+    def moved(v, parity):
+        return jnp.where(core == parity, SIDE - 1 - v, v + 1 - 2 * (v % 2))
+
+    for outer, rows4 in enumerate((own4, along4, across4, corner4)):
+        x, y = my_dp // SIDE, my_dp % SIDE
+        x = moved(x, 0) if outer // 2 else x
+        y = moved(y, 0) if outer % 2 else y
+        for inner in range(SIDE):
+            row = moved(x, 1) if inner // 2 else x
+            column = moved(y, 1) if inner % 2 else y
+            first = pl.multiple_of((row * SIDE + column) * rows, rows)
+            for s in range(cap):
+                whole[s, pl.ds(first, rows), :] = rows4[inner, s]
+
+
+def stage(where, squares):
+    _, cap, rows, width = squares[0].shape
+    near = pl.BlockSpec(memory_space=pltpu.VMEM)
     return pl.pallas_call(
         stage_kernel,
-        in_specs=[pl.BlockSpec(memory_space=pl.ANY)],
-        out_specs=pl.BlockSpec(memory_space=pltpu.VMEM),
-        scratch_shapes=[pltpu.SemaphoreType.DMA],
-        out_shape=jax.ShapeDtypeStruct(x.shape, x.dtype),
+        in_specs=[pl.BlockSpec(memory_space=pltpu.SMEM)] + [near] * 4,
+        out_specs=near,
+        out_shape=jax.ShapeDtypeStruct((cap, width, width), jnp.bfloat16),
         compiler_params=pltpu.CompilerParams(vmem_limit_bytes=32 * 1024 * 1024),
-        cost_estimate=pl.CostEstimate(flops=0, bytes_accessed=4 * x.size, transcendentals=0),
-    )(x)
+        cost_estimate=pl.CostEstimate(
+            flops=0, bytes_accessed=4 * cap * width**2, transcendentals=0
+        ),
+    )(where, *squares)
 
 
 def slot_step(where, squares, root, middle, left, right):
@@ -183,8 +200,6 @@
     my_dp, my_core = lax.axis_index("dp"), lax.axis_index("core")
     row_tiles, col_tiles = rows // 8, width // 128
 
-    root = lax.all_gather(left_root, "dp", axis=1, tiled=True)
-
     sent = gradients.reshape(blocks, n_dp, rows, width).transpose(1, 0, 2, 3)
     sent, my_dp, my_core = lax.optimization_barrier((sent, my_dp, my_core))
     parts = lax.all_to_all(sent, "dp", split_axis=0, concat_axis=0, tiled=True)
@@ -192,9 +207,10 @@
 
     summed = summed.reshape(blocks, row_tiles, 2, 4, col_tiles, 128)
     pieces = summed.transpose(1, 4, 2, 0, 3, 5).reshape(n_z, blocks * 4, 128)
-    pieces, right_eigen, owner_map, my_dp, my_core = lax.optimization_barrier(
-        (pieces, right_eigen, owner_map, my_dp, my_core)
-    )
+    pieces, right_eigen, owner_map, my_dp, my_core, left_root = lax.optimization_barrier(
+        (pieces, right_eigen, owner_map, my_dp, my_core, left_root)
+    )
+    root4 = jnp.stack([left_root] + [swap_corner(left_root, a, b, 1) for a, b in MOVES])
     where = jnp.stack([my_dp, my_core]).astype(jnp.int32)
     factor = ((right_eigen + epsilon) ** (-0.25))[:, None, :]
     spread = lax.all_to_all(pieces, "z", split_axis=0, concat_axis=0, tiled=True)
@@ -214,8 +230,11 @@
     pick = (jnp.arange(n_z * cap, dtype=jnp.int32)[:, None] == place[None, :]).astype(jnp.bfloat16)
     chosen = jnp.dot(pick, held, preferred_element_type=jnp.float32).astype(jnp.bfloat16)
     deliver = chosen.reshape(n_z, cap, 4, 128)
-    deliver, right_basis, factor = lax.optimization_barrier((deliver, right_basis, factor))
+    deliver, right_basis, factor, root4 = lax.optimization_barrier(
+        (deliver, right_basis, factor, root4)
+    )
     middle = middle_step(right_basis, factor)
+    roots = [root4] + [swap_corner(root4, a, b, 0) for a, b in MOVES]
     arrived = lax.all_to_all(deliver, "z", split_axis=0, concat_axis=0, tiled=True)
     arrived, middle = lax.optimization_barrier((arrived, middle))
 
@@ -223,11 +242,11 @@
     owned = owned.transpose(3, 0, 2, 4, 1, 5).reshape(cap, rows, width)
     n_opt = n_z * CORES
     line = broadcast_gather(owned, ALL, quads(n_opt))
-    line, root = lax.optimization_barrier((line, root))
-    squares = [line] + [swap_corner(line, a, b) for a, b in ((False, True), (True, False), (True, True))]
+    line, *roots = lax.optimization_barrier((line, *roots))
+    squares = [line] + [swap_corner(line, a, b, 0) for a, b in MOVES]
 
     update, left_new, right_new = slot_step(
-        where, squares, stage(root), middle, left_stat, right_stat
+        where, squares, stage(where, roots), middle, left_stat, right_stat
     )
     return (update, left_new, right_new)
 

time: 175 us -> 173 us (0.989)
  starting transfers between devices: 50.1 us -> 71.9 us
  between operations: 14.2 us -> 0.93 us
  blocking collectives: 30.8 us -> 19.1 us
    ppermute x3 -> x9, starting transfers between devices: 8.36 us -> 27.8 us  [swap_corner(): return lax.ppermute(x, ALL, pairs)]
    all_to_all x1 -> x0, blocking collectives: 11.6 us -> none  [broadcast_gather(): lax.all_to_all(copies, axis, split_axis=0, concat_axis=0, tiled=True, axi...]
    all_to_all x1, waiting for transfers between devices: 26.5 us -> 18.1 us  [body(): lax.all_to_all(deliver, 'z', split_axis=0, concat_axis=0, tiled=True)]
    all_to_all x0 -> x1, waiting for transfers between devices: none -> 7.63 us  [broadcast_gather(): lax.all_to_all(copies, axis, split_axis=0, concat_axis=0, tiled=True, axi...]
    all_to_all x0 -> x1, starting transfers between devices: none -> 3.48 us  [broadcast_gather(): lax.all_to_all(copies, axis, split_axis=0, concat_axis=0, tiled=True, axi...]
    ppermute x3 -> x9, waiting for transfers between devices: 9.21 us -> 10.4 us  [swap_corner(): return lax.ppermute(x, ALL, pairs)]
  transfers between devices with their start and end apart: 7 -> 13, of which waited for: 6 -> 7; matrix products, arithmetic and copies ran while one was open for 3% -> 2% of each run, Pallas kernels for 4% -> 4%
where the time goes in v8:
time: 173 us; the launch traced here: 171 us
  starting transfers between devices  71.9 us (42%)
  waiting for transfers between devices  60.1 us (35%)
  blocking collectives  19.1 us (11%)
  Pallas kernels  12.8 us (7%)
  local copies, waits for them, and re-layouts  4.88 us (3%)
    all_to_all x1, starting transfers between devices, body(): lax.all_to_all(pieces, 'z', split_axis=0, concat_axis=0, tiled=True)  32.6 us
    ppermute x9, starting transfers between devices, swap_corner(): return lax.ppermute(x, ALL, pairs)  27.8 us
    all_to_all x1, waiting for transfers between devices, body(): lax.all_to_all(pieces, 'z', split_axis=0, concat_axis=0, tiled=True)  23.2 us
    all_to_all x1, blocking collectives, body(): parts = lax.all_to_all(sent, 'dp', split_axis=0, concat_axis=0, tiled=True)  19.1 us
    all_to_all x1, waiting for transfers between devices, body(): lax.all_to_all(deliver, 'z', split_axis=0, concat_axis=0, tiled=True)  18.1 us
    ppermute x9, waiting for transfers between devices, swap_corner(): return lax.ppermute(x, ALL, pairs)  10.4 us
    all_to_all x1, waiting for transfers between devices, broadcast_gather(): lax.all_to_all(copies, axis, split_axis=0, concat_axis=0, tiled=True, axi...  7.63 us
    pallas_call x1, Pallas kernels, middle_step(): pl.pallas_call(middle_kernel, grid=(cap,), in_specs=[whole, pl.BlockSpec(...  6.59 us
  transfers between devices with their start and end apart: 13, of which 7 were waited for; matrix products, arithmetic and copies ran while one was open for 2% of the time, Pallas kernels for 4%

profile of v8, /device:TPU:1, one launch (start us, length us, event | category | flops | bytes accessed | tf_op | source)
XLA Modules:
  0.0 170.6 jit_solution(2133692518726056648)
XLA Ops:
  0.7 1.3 copy.19
  2.0 19.1 %all_to_all.20 = bf16[16,2,32,512]{3,2,1,0:T(8,128)(2,1)S(1)} all-to-all(bf16[16,2,32,512]{3,2,1,0:T(8,128)(2,1)S(1)} %copy.19), channel_id=1, replica_groups=mesh['dp'=16,'z'=32,'core'=2] {'dp'}, dimensions={0} | all-to-all | bytes 2097152 | tf_op jit(solution)/shard_map/all_to_all | solution.py:205
  22.0 2.8 %collective-permute-start.3 = (bf16[5,32,512]{2,1,0:T(8,128)(2,1)S(1)}, bf16[5,32,512]{2,1,0:T(8,128)(2,1)S(1)}, u32[]{:S(2)}, u32[]{:S(2)}) collective-permute-start(bf16[5,32,512]{2,1,0:T(8,128)(2,1)S(1)} %copy-done.3), channel_id=1, source_target_pairs={{0,320},{1,961},{2,322},{3,963},{4,324},{5,965},{6,326},{7,967},{8... | collective-permute-start | bytes 491528 | tf_op jit(solution)/shard_map/ppermute | solution.py:47
  24.8 3.7 %collective-permute-start.2 = (bf16[5,32,512]{2,1,0:T(8,128)(2,1)S(1)}, bf16[5,32,512]{2,1,0:T(8,128)(2,1)S(1)}, u32[]{:S(2)}, u32[]{:S(2)}) collective-permute-start(bf16[5,32,512]{2,1,0:T(8,128)(2,1)S(1)} %copy-done.3), channel_id=1, source_target_pairs={{0,256},{1,769},{2,258},{3,771},{4,260},{5,773},{6,262},{7,775},{8... | collective-permute-start | bytes 491528 | tf_op jit(solution)/shard_map/ppermute | solution.py:47
  28.5 4.3 %collective-permute-start.1 = (bf16[5,32,512]{2,1,0:T(8,128)(2,1)S(1)}, bf16[5,32,512]{2,1,0:T(8,128)(2,1)S(1)}, u32[]{:S(2)}, u32[]{:S(2)}) collective-permute-start(bf16[5,32,512]{2,1,0:T(8,128)(2,1)S(1)} %copy-done.3), channel_id=1, source_target_pairs={{0,64},{1,193},{2,66},{3,195},{4,68},{5,197},{6,70},{7,199},{8,72}... | collective-permute-start | bytes 491528 | tf_op jit(solution)/shard_map/ppermute | solution.py:47
  33.0 32.6 %all-to-all-start.1 = ((bf16[32,8,128]{2,1,0:T(8,128)(2,1)}), bf16[32,8,128]{2,1,0:T(8,128)(2,1)S(1)}, u32[]{:S(2)}, u32[]{:S(2)}) async-start(bf16[32,8,128]{2,1,0:T(8,128)(2,1)} %bitcast.3), calls=%async_computation.1 | async-start | bytes 131072 | tf_op jit(solution)/shard_map/all_to_all | solution.py:216
  66.9 23.2 %all-to-all-done.1 = bf16[32,8,128]{2,1,0:T(8,128)(2,1)S(1)} async-done(((bf16[32,8,128]{2,1,0:T(8,128)(2,1)}), bf16[32,8,128]{2,1,0:T(8,128)(2,1)S(1)}, u32[]{:S(2)}, u32[]{:S(2)}) %all-to-all-start.1) | async-done | bytes 65568 | tf_op jit(solution)/shard_map/all_to_all | solution.py:216
  90.1 4.2 %collective-permute-start = (bf16[32,8,128]{2,1,0:T(8,128)(2,1)S(1)}, bf16[32,8,128]{2,1,0:T(8,128)(2,1)S(1)}, u32[]{:S(2)}, u32[]{:S(2)}) collective-permute-start(bf16[32,8,128]{2,1,0:T(8,128)(2,1)S(1)} %all-to-all-done.1), channel_id=1, source_target_pairs={{0,1},{1,0},{2,3},{3,2},{4,5},{5,4},{6,7},{7,6},{8,9},{9,8},{10,11... | collective-permute-start | bytes 196616 | tf_op jit(solution)/shard_map/ppermute | solution.py:218
  96.1 3.9 %all-to-all-start.2 = ((bf16[32,5,4,128]{3,2,1,0:T(4,128)(2,1)}), bf16[32,5,4,128]{3,2,1,0:T(4,128)(2,1)S(1)}, u32[]{:S(2)}, u32[]{:S(2)}) async-start(bf16[32,5,4,128]{3,2,1,0:T(4,128)(2,1)} %reshape.44), calls=%async_computation.2 | async-start | bytes 327680 | tf_op jit(solution)/shard_map/all_to_all | solution.py:238
  100.0 1.9 %collective-permute-start.6 = (bf16[4,5,32,512]{3,2,1,0:T(8,128)(2,1)S(1)}, bf16[4,5,32,512]{3,2,1,0:T(8,128)(2,1)S(1)}, u32[]{:S(2)}, u32[]{:S(2)}) collective-permute-start(bf16[4,5,32,512]{3,2,1,0:T(8,128)(2,1)S(1)} %pad_maximum_fusion.own4), channel_id=1, source_target_pairs={{0,960},{1,321},{2,962},{3,323},{4,964},{5,325},{6,966},{7,327},{8... | collective-permute-start | bytes 1966088 | tf_op jit(solution)/shard_map/ppermute | solution.py:47
  101.9 2.4 %collective-permute-start.5 = (bf16[4,5,32,512]{3,2,1,0:T(8,128)(2,1)S(1)}, bf16[4,5,32,512]{3,2,1,0:T(8,128)(2,1)S(1)}, u32[]{:S(2)}, u32[]{:S(2)}) collective-permute-start(bf16[4,5,32,512]{3,2,1,0:T(8,128)(2,1)S(1)} %pad_maximum_fusion.own4), channel_id=1, source_target_pairs={{0,768},{1,257},{2,770},{3,259},{4,772},{5,261},{6,774},{7,263},{8... | collective-permute-start | bytes 1966088 | tf_op jit(solution)/shard_map/ppermute | solution.py:47
  104.3 4.1 %collective-permute-start.4 = (bf16[4,5,32,512]{3,2,1,0:T(8,128)(2,1)S(1)}, bf16[4,5,32,512]{3,2,1,0:T(8,128)(2,1)S(1)}, u32[]{:S(2)}, u32[]{:S(2)}) collective-permute-start(bf16[4,5,32,512]{3,2,1,0:T(8,128)(2,1)S(1)} %pad_maximum_fusion.own4), channel_id=1, source_target_pairs={{0,192},{1,65},{2,194},{3,67},{4,196},{5,69},{6,198},{7,71},{8,200... | collective-permute-start | bytes 1966088 | tf_op jit(solution)/shard_map/ppermute | solution.py:47
  108.4 6.6 %shard_map.94.middle = bf16[5,512,512]{2,1,0:T(8,128)(2,1)} custom-call(bf16[5,512,512]{2,1,0:T(8,128)(2,1)} %basis, f32[5,1,512]{2,1,0:T(1,128)} %broadcast_in_dim.8.factor), custom_call_target="tpu_custom_call" | custom-call | flops 2684354560 | bytes 5242880 | tf_op jit(solution)/shard_map/pallas_call | solution.py:120
  115.0 18.1 %all-to-all-done.2 = bf16[32,5,4,128]{3,2,1,0:T(4,128)(2,1)S(1)} async-done(((bf16[32,5,4,128]{3,2,1,0:T(4,128)(2,1)}), bf16[32,5,4,128]{3,2,1,0:T(4,128)(2,1)S(1)}, u32[]{:S(2)}, u32[]{:S(2)}) %all-to-all-start.2) | async-done | bytes 163872 | tf_op jit(solution)/shard_map/all_to_all | solution.py:238
  133.2 0.9 broadcast_in_dim.10
  134.1 3.5 %all-to-all-start.3 = ((bf16[4,5,32,512]{3,2,1,0:T(8,128)(2,1)}), bf16[4,5,32,512]{3,2,1,0:T(8,128)(2,1)S(1)}, u32[]{:S(2)}, u32[]{:S(2)}) async-start(bf16[4,5,32,512]{3,2,1,0:T(8,128)(2,1)} %broadcast_in_dim.10), calls=%async_computation.3 | async-start | bytes 1310720 | tf_op jit(solution)/shard_map/all_to_all | solution.py:21
  137.7 7.6 %all-to-all-done.3.own4 = bf16[4,5,32,512]{3,2,1,0:T(8,128)(2,1)S(1)} async-done(((bf16[4,5,32,512]{3,2,1,0:T(8,128)(2,1)}), bf16[4,5,32,512]{3,2,1,0:T(8,128)(2,1)S(1)}, u32[]{:S(2)}, u32[]{:S(2)}) %all-to-all-start.3) | async-done | bytes 655392 | tf_op jit(solution)/shard_map/all_to_all | solution.py:21
  145.3 2.2 %collective-permute-start.9 = (bf16[4,5,32,512]{3,2,1,0:T(8,128)(2,1)S(1)}, bf16[4,5,32,512]{3,2,1,0:T(8,128)(2,1)S(1)}, u32[]{:S(2)}, u32[]{:S(2)}) collective-permute-start(bf16[4,5,32,512]{3,2,1,0:T(8,128)(2,1)S(1)} %all-to-all-done.3.own4), channel_id=1, source_target_pairs={{0,960},{1,321},{2,962},{3,323},{4,964},{5,325},{6,966},{7,327},{8... | collective-permute-start | bytes 1966088 | tf_op jit(solution)/shard_map/ppermute | solution.py:47
  147.5 2.2 %collective-permute-start.8 = (bf16[4,5,32,512]{3,2,1,0:T(8,128)(2,1)S(1)}, bf16[4,5,32,512]{3,2,1,0:T(8,128)(2,1)S(1)}, u32[]{:S(2)}, u32[]{:S(2)}) collective-permute-start(bf16[4,5,32,512]{3,2,1,0:T(8,128)(2,1)S(1)} %all-to-all-done.3.own4), channel_id=1, source_target_pairs={{0,768},{1,257},{2,770},{3,259},{4,772},{5,261},{6,774},{7,263},{8... | collective-permute-start | bytes 1966088 | tf_op jit(solution)/shard_map/ppermute | solution.py:47
  149.7 4.3 %collective-permute-start.7 = (bf16[4,5,32,512]{3,2,1,0:T(8,128)(2,1)S(1)}, bf16[4,5,32,512]{3,2,1,0:T(8,128)(2,1)S(1)}, u32[]{:S(2)}, u32[]{:S(2)}) collective-permute-start(bf16[4,5,32,512]{3,2,1,0:T(8,128)(2,1)S(1)} %all-to-all-done.3.own4), channel_id=1, source_target_pairs={{0,192},{1,65},{2,194},{3,67},{4,196},{5,69},{6,198},{7,71},{8,200... | collective-permute-start | bytes 1966088 | tf_op jit(solution)/shard_map/ppermute | solution.py:47
  154.7 3.4 %collective-permute-done.9.corner4 = bf16[4,5,32,512]{3,2,1,0:T(8,128)(2,1)S(1)} collective-permute-done((bf16[4,5,32,512]{3,2,1,0:T(8,128)(2,1)S(1)}, bf16[4,5,32,512]{3,2,1,0:T(8,128)(2,1)S(1)}, u32[]{:S(2)}, u32[]{:S(2)}) %collective-permute-start.9) | collective-permute-done | bytes 655392 | tf_op jit(solution)/shard_map/ppermute | solution.py:47
  158.1 4.9 %collective-permute-done.8.across4 = bf16[4,5,32,512]{3,2,1,0:T(8,128)(2,1)S(1)} collective-permute-done((bf16[4,5,32,512]{3,2,1,0:T(8,128)(2,1)S(1)}, bf16[4,5,32,512]{3,2,1,0:T(8,128)(2,1)S(1)}, u32[]{:S(2)}, u32[]{:S(2)}) %collective-permute-start.8) | collective-permute-done | bytes 655392 | tf_op jit(solution)/shard_map/ppermute | solution.py:47
  163.0 2.1 %collective-permute-done.7.along4 = bf16[4,5,32,512]{3,2,1,0:T(8,128)(2,1)S(1)} collective-permute-done((bf16[4,5,32,512]{3,2,1,0:T(8,128)(2,1)S(1)}, bf16[4,5,32,512]{3,2,1,0:T(8,128)(2,1)S(1)}, u32[]{:S(2)}, u32[]{:S(2)}) %collective-permute-start.7) | collective-permute-done | bytes 655392 | tf_op jit(solution)/shard_map/ppermute | solution.py:47
  165.1 5.5 %shard_map.96 = (bf16[5,512,512]{2,1,0:T(8,128)(2,1)}, f32[5,32,512]{2,1,0:T(8,128)}, f32[5,32,512]{2,1,0:T(8,128)}) custom-call(s32[2]{0:T(128)S(1)} %pad_add_fusion.where, bf16[4,5,32,512]{3,2,1,0:T(8,128)(2,1)S(1)} %all-to-all-done.3.own4, bf16[4,5,32,512]{3,2,1,0:T(8,128)(2,1)S(1)} %collective-permute-done.7.along4, ...), custom_call_target="tpu_custom_call" | custom-call | flops 3355443200 | bytes 13107200 | tf_op jit(solution)/shard_map/pallas_call | solution.py:172
  (40 shorter events, 4.9 us)
Async XLA Ops:
  0.6 21.4 %copy-start.3 = (bf16[5,32,512]{2,1,0:T(8,128)(2,1)S(1)}, bf16[5,32,512]{2,1,0:T(8,128)(2,1)}, u32[]{:S(2)}) copy-start(bf16[5,32,512]{2,1,0:T(8,128)(2,1)} %param.9) | copy-start | bytes 491524
  0.6 32.2 %copy-start.5 = (s32[128]{0:T(128)S(1)}, s32[128]{0:T(128)}, u32[]{:S(2)}) copy-start(s32[128]{0:T(128)} %param.8) | copy-start | bytes 1540
  0.7 65.2 %copy-start.4 = (f32[5,512]{1,0:T(8,128)S(1)}, f32[5,512]{1,0:T(8,128)}, u32[]{:S(2)}) copy-start(f32[5,512]{1,0:T(8,128)} %param.11) | copy-start | bytes 30724
  22.0 72.3 %collective-permute-start.3 = (bf16[5,32,512]{2,1,0:T(8,128)(2,1)S(1)}, bf16[5,32,512]{2,1,0:T(8,128)(2,1)S(1)}, u32[]{:S(2)}, u32[]{:S(2)}) collective-permute-start(bf16[5,32,512]{2,1,0:T(8,128)(2,1)S(1)} %copy-done.3), channel_id=1, source_target_pairs={{0,320},{1,961},{2,322},{3,963},{4,324},{5,965},{6,326},{7,967},{8... | collective-permute-start | bytes 491528 | tf_op jit(solution)/shard_map/ppermute | solution.py:47
  24.8 69.5 %collective-permute-start.2 = (bf16[5,32,512]{2,1,0:T(8,128)(2,1)S(1)}, bf16[5,32,512]{2,1,0:T(8,128)(2,1)S(1)}, u32[]{:S(2)}, u32[]{:S(2)}) collective-permute-start(bf16[5,32,512]{2,1,0:T(8,128)(2,1)S(1)} %copy-done.3), channel_id=1, source_target_pairs={{0,256},{1,769},{2,258},{3,771},{4,260},{5,773},{6,262},{7,775},{8... | collective-permute-start | bytes 491528 | tf_op jit(solution)/shard_map/ppermute | solution.py:47
  28.5 65.8 %collective-permute-start.1 = (bf16[5,32,512]{2,1,0:T(8,128)(2,1)S(1)}, bf16[5,32,512]{2,1,0:T(8,128)(2,1)S(1)}, u32[]{:S(2)}, u32[]{:S(2)}) collective-permute-start(bf16[5,32,512]{2,1,0:T(8,128)(2,1)S(1)} %copy-done.3), channel_id=1, source_target_pairs={{0,64},{1,193},{2,66},{3,195},{4,68},{5,197},{6,70},{7,199},{8,72}... | collective-permute-start | bytes 491528 | tf_op jit(solution)/shard_map/ppermute | solution.py:47
  33.0 57.1 %all-to-all-start.1 = ((bf16[32,8,128]{2,1,0:T(8,128)(2,1)}), bf16[32,8,128]{2,1,0:T(8,128)(2,1)S(1)}, u32[]{:S(2)}, u32[]{:S(2)}) async-start(bf16[32,8,128]{2,1,0:T(8,128)(2,1)} %bitcast.3), calls=%async_computation.1 | async-start | bytes 131072 | tf_op jit(solution)/shard_map/all_to_all | solution.py:216
  90.1 5.1 %collective-permute-start = (bf16[32,8,128]{2,1,0:T(8,128)(2,1)S(1)}, bf16[32,8,128]{2,1,0:T(8,128)(2,1)S(1)}, u32[]{:S(2)}, u32[]{:S(2)}) collective-permute-start(bf16[32,8,128]{2,1,0:T(8,128)(2,1)S(1)} %all-to-all-done.1), channel_id=1, source_target_pairs={{0,1},{1,0},{2,3},{3,2},{4,5},{5,4},{6,7},{7,6},{8,9},{9,8},{10,11... | collective-permute-start | bytes 196616 | tf_op jit(solution)/shard_map/ppermute | solution.py:218
  96.1 37.0 %all-to-all-start.2 = ((bf16[32,5,4,128]{3,2,1,0:T(4,128)(2,1)}), bf16[32,5,4,128]{3,2,1,0:T(4,128)(2,1)S(1)}, u32[]{:S(2)}, u32[]{:S(2)}) async-start(bf16[32,5,4,128]{3,2,1,0:T(4,128)(2,1)} %reshape.44), calls=%async_computation.2 | async-start | bytes 327680 | tf_op jit(solution)/shard_map/all_to_all | solution.py:238
  100.0 37.7 %collective-permute-start.6 = (bf16[4,5,32,512]{3,2,1,0:T(8,128)(2,1)S(1)}, bf16[4,5,32,512]{3,2,1,0:T(8,128)(2,1)S(1)}, u32[]{:S(2)}, u32[]{:S(2)}) collective-permute-start(bf16[4,5,32,512]{3,2,1,0:T(8,128)(2,1)S(1)} %pad_maximum_fusion.own4), channel_id=1, source_target_pairs={{0,960},{1,321},{2,962},{3,323},{4,964},{5,325},{6,966},{7,327},{8... | collective-permute-start | bytes 1966088 | tf_op jit(solution)/shard_map/ppermute | solution.py:47
  101.9 35.7 %collective-permute-start.5 = (bf16[4,5,32,512]{3,2,1,0:T(8,128)(2,1)S(1)}, bf16[4,5,32,512]{3,2,1,0:T(8,128)(2,1)S(1)}, u32[]{:S(2)}, u32[]{:S(2)}) collective-permute-start(bf16[4,5,32,512]{3,2,1,0:T(8,128)(2,1)S(1)} %pad_maximum_fusion.own4), channel_id=1, source_target_pairs={{0,768},{1,257},{2,770},{3,259},{4,772},{5,261},{6,774},{7,263},{8... | collective-permute-start | bytes 1966088 | tf_op jit(solution)/shard_map/ppermute | solution.py:47
  104.3 33.3 %collective-permute-start.4 = (bf16[4,5,32,512]{3,2,1,0:T(8,128)(2,1)S(1)}, bf16[4,5,32,512]{3,2,1,0:T(8,128)(2,1)S(1)}, u32[]{:S(2)}, u32[]{:S(2)}) collective-permute-start(bf16[4,5,32,512]{3,2,1,0:T(8,128)(2,1)S(1)} %pad_maximum_fusion.own4), channel_id=1, source_target_pairs={{0,192},{1,65},{2,194},{3,67},{4,196},{5,69},{6,198},{7,71},{8,200... | collective-permute-start | bytes 1966088 | tf_op jit(solution)/shard_map/ppermute | solution.py:47
  134.1 11.2 %all-to-all-start.3 = ((bf16[4,5,32,512]{3,2,1,0:T(8,128)(2,1)}), bf16[4,5,32,512]{3,2,1,0:T(8,128)(2,1)S(1)}, u32[]{:S(2)}, u32[]{:S(2)}) async-start(bf16[4,5,32,512]{3,2,1,0:T(8,128)(2,1)} %broadcast_in_dim.10), calls=%async_computation.3 | async-start | bytes 1310720 | tf_op jit(solution)/shard_map/all_to_all | solution.py:21
  145.3 19.8 %copy-start = (f32[5,32,512]{2,1,0:T(8,128)S(1)}, f32[5,32,512]{2,1,0:T(8,128)}, u32[]{:S(2)}) copy-start(f32[5,32,512]{2,1,0:T(8,128)} %left.1) | copy-start | bytes 983044
  145.3 19.8 %copy-start.1 = (f32[5,32,512]{2,1,0:T(8,128)S(1)}, f32[5,32,512]{2,1,0:T(8,128)}, u32[]{:S(2)}) copy-start(f32[5,32,512]{2,1,0:T(8,128)} %right.1) | copy-start | bytes 983044
  145.3 19.8 %copy-start.2 = (bf16[5,512,512]{2,1,0:T(8,128)(2,1)S(1)}, bf16[5,512,512]{2,1,0:T(8,128)(2,1)}, u32[]{:S(2)}) copy-start(bf16[5,512,512]{2,1,0:T(8,128)(2,1)} %shard_map.94.middle) | copy-start | bytes 7864324
  145.3 12.8 %collective-permute-start.9 = (bf16[4,5,32,512]{3,2,1,0:T(8,128)(2,1)S(1)}, bf16[4,5,32,512]{3,2,1,0:T(8,128)(2,1)S(1)}, u32[]{:S(2)}, u32[]{:S(2)}) collective-permute-start(bf16[4,5,32,512]{3,2,1,0:T(8,128)(2,1)S(1)} %all-to-all-done.3.own4), channel_id=1, source_target_pairs={{0,960},{1,321},{2,962},{3,323},{4,964},{5,325},{6,966},{7,327},{8... | collective-permute-start | bytes 1966088 | tf_op jit(solution)/shard_map/ppermute | solution.py:47
  147.5 15.5 %collective-permute-start.8 = (bf16[4,5,32,512]{3,2,1,0:T(8,128)(2,1)S(1)}, bf16[4,5,32,512]{3,2,1,0:T(8,128)(2,1)S(1)}, u32[]{:S(2)}, u32[]{:S(2)}) collective-permute-start(bf16[4,5,32,512]{3,2,1,0:T(8,128)(2,1)S(1)} %all-to-all-done.3.own4), channel_id=1, source_target_pairs={{0,768},{1,257},{2,770},{3,259},{4,772},{5,261},{6,774},{7,263},{8... | collective-permute-start | bytes 1966088 | tf_op jit(solution)/shard_map/ppermute | solution.py:47
  149.7 15.4 %collective-permute-start.7 = (bf16[4,5,32,512]{3,2,1,0:T(8,128)(2,1)S(1)}, bf16[4,5,32,512]{3,2,1,0:T(8,128)(2,1)S(1)}, u32[]{:S(2)}, u32[]{:S(2)}) collective-permute-start(bf16[4,5,32,512]{3,2,1,0:T(8,128)(2,1)S(1)} %all-to-all-done.3.own4), channel_id=1, source_target_pairs={{0,192},{1,65},{2,194},{3,67},{4,196},{5,69},{6,198},{7,71},{8,200... | collective-permute-start | bytes 1966088 | tf_op jit(solution)/shard_map/ppermute | solution.py:47

commit v9 on v8

--- a/solution.py
+++ b/solution.py
@@ -230,9 +230,7 @@
     pick = (jnp.arange(n_z * cap, dtype=jnp.int32)[:, None] == place[None, :]).astype(jnp.bfloat16)
     chosen = jnp.dot(pick, held, preferred_element_type=jnp.float32).astype(jnp.bfloat16)
     deliver = chosen.reshape(n_z, cap, 4, 128)
-    deliver, right_basis, factor, root4 = lax.optimization_barrier(
-        (deliver, right_basis, factor, root4)
-    )
+    deliver, right_basis, factor = lax.optimization_barrier((deliver, right_basis, factor))
     middle = middle_step(right_basis, factor)
     roots = [root4] + [swap_corner(root4, a, b, 0) for a, b in MOVES]
     arrived = lax.all_to_all(deliver, "z", split_axis=0, concat_axis=0, tiled=True)

time: 173 us -> 163 us (0.942)
  waiting for transfers between devices: 60.1 us -> 48 us
    all_to_all x1, waiting for transfers between devices: 18.1 us -> 3.52 us  [body(): lax.all_to_all(deliver, 'z', split_axis=0, concat_axis=0, tiled=True)]
    ppermute x9, waiting for transfers between devices: 10.4 us -> 14.1 us  [swap_corner(): return lax.ppermute(x, ALL, pairs)]
  transfers between devices with their start and end apart: 13 -> 13, of which waited for: 7 -> 8; matrix products, arithmetic and copies ran while one was open for 2% -> 2% of each run, Pallas kernels for 4% -> 5%
where the time goes in v9:
time: 163 us; the launch traced here: 160 us
  starting transfers between devices  73 us (45%)
  waiting for transfers between devices  48 us (29%)
  blocking collectives  19.3 us (12%)
  Pallas kernels  12.8 us (8%)
  local copies, waits for them, and re-layouts  4.86 us (3%)
    all_to_all x1, starting transfers between devices, body(): lax.all_to_all(pieces, 'z', split_axis=0, concat_axis=0, tiled=True)  32.6 us
    ppermute x9, starting transfers between devices, swap_corner(): return lax.ppermute(x, ALL, pairs)  27.8 us
    all_to_all x1, waiting for transfers between devices, body(): lax.all_to_all(pieces, 'z', split_axis=0, concat_axis=0, tiled=True)  22 us
    all_to_all x1, blocking collectives, body(): parts = lax.all_to_all(sent, 'dp', split_axis=0, concat_axis=0, tiled=True)  19.3 us
    ppermute x9, waiting for transfers between devices, swap_corner(): return lax.ppermute(x, ALL, pairs)  14.1 us
    all_to_all x1, waiting for transfers between devices, broadcast_gather(): lax.all_to_all(copies, axis, split_axis=0, concat_axis=0, tiled=True, axi...  7.63 us
    pallas_call x1, Pallas kernels, middle_step(): pl.pallas_call(middle_kernel, grid=(cap,), in_specs=[whole, pl.BlockSpec(...  6.59 us
    pallas_call x1, Pallas kernels, slot_step(): pl.pallas_call(slot_kernel, in_specs=[pl.BlockSpec(memory_space=pltpu.SME...  5.5 us
  transfers between devices with their start and end apart: 13, of which 8 were waited for; matrix products, arithmetic and copies ran while one was open for 2% of the time, Pallas kernels for 5%

profile of v9, /device:TPU:1, one launch (start us, length us, event | category | flops | bytes accessed | tf_op | source)
XLA Modules:
  0.0 159.8 jit_solution(690345380432736113)
XLA Ops:
  0.7 1.3 copy.19
  2.0 19.3 %all_to_all.20 = bf16[16,2,32,512]{3,2,1,0:T(8,128)(2,1)S(1)} all-to-all(bf16[16,2,32,512]{3,2,1,0:T(8,128)(2,1)S(1)} %copy.19), channel_id=1, replica_groups=mesh['dp'=16,'z'=32,'core'=2] {'dp'}, dimensions={0} | all-to-all | bytes 2097152 | tf_op jit(solution)/shard_map/all_to_all | solution.py:205
  22.1 32.6 %all-to-all-start.1 = ((bf16[32,8,128]{2,1,0:T(8,128)(2,1)}), bf16[32,8,128]{2,1,0:T(8,128)(2,1)S(1)}, u32[]{:S(2)}, u32[]{:S(2)}) async-start(bf16[32,8,128]{2,1,0:T(8,128)(2,1)} %bitcast.3), calls=%async_computation.1 | async-start | bytes 131072 | tf_op jit(solution)/shard_map/all_to_all | solution.py:216
  56.1 22.0 %all-to-all-done.1 = bf16[32,8,128]{2,1,0:T(8,128)(2,1)S(1)} async-done(((bf16[32,8,128]{2,1,0:T(8,128)(2,1)}), bf16[32,8,128]{2,1,0:T(8,128)(2,1)S(1)}, u32[]{:S(2)}, u32[]{:S(2)}) %all-to-all-start.1) | async-done | bytes 65568 | tf_op jit(solution)/shard_map/all_to_all | solution.py:216
  78.1 5.3 %collective-permute-start = (bf16[32,8,128]{2,1,0:T(8,128)(2,1)S(1)}, bf16[32,8,128]{2,1,0:T(8,128)(2,1)S(1)}, u32[]{:S(2)}, u32[]{:S(2)}) collective-permute-start(bf16[32,8,128]{2,1,0:T(8,128)(2,1)S(1)} %all-to-all-done.1), channel_id=1, source_target_pairs={{0,1},{1,0},{2,3},{3,2},{4,5},{5,4},{6,7},{7,6},{8,9},{9,8},{10,11... | collective-permute-start | bytes 196616 | tf_op jit(solution)/shard_map/ppermute | solution.py:218
  85.3 3.9 %all-to-all-start.2 = ((bf16[32,5,4,128]{3,2,1,0:T(4,128)(2,1)}), bf16[32,5,4,128]{3,2,1,0:T(4,128)(2,1)S(1)}, u32[]{:S(2)}, u32[]{:S(2)}) async-start(bf16[32,5,4,128]{3,2,1,0:T(4,128)(2,1)} %reshape.44), calls=%async_computation.2 | async-start | bytes 327680 | tf_op jit(solution)/shard_map/all_to_all | solution.py:236
  89.1 3.0 %collective-permute-start.3 = (bf16[5,32,512]{2,1,0:T(8,128)(2,1)S(1)}, bf16[5,32,512]{2,1,0:T(8,128)(2,1)S(1)}, u32[]{:S(2)}, u32[]{:S(2)}) collective-permute-start(bf16[5,32,512]{2,1,0:T(8,128)(2,1)S(1)} %copy-done.3), channel_id=1, source_target_pairs={{0,320},{1,961},{2,322},{3,963},{4,324},{5,965},{6,326},{7,967},{8... | collective-permute-start | bytes 491528 | tf_op jit(solution)/shard_map/ppermute | solution.py:47
  92.1 3.9 %collective-permute-start.2 = (bf16[5,32,512]{2,1,0:T(8,128)(2,1)S(1)}, bf16[5,32,512]{2,1,0:T(8,128)(2,1)S(1)}, u32[]{:S(2)}, u32[]{:S(2)}) collective-permute-start(bf16[5,32,512]{2,1,0:T(8,128)(2,1)S(1)} %copy-done.3), channel_id=1, source_target_pairs={{0,256},{1,769},{2,258},{3,771},{4,260},{5,773},{6,262},{7,775},{8... | collective-permute-start | bytes 491528 | tf_op jit(solution)/shard_map/ppermute | solution.py:47
  96.1 3.9 %collective-permute-start.1 = (bf16[5,32,512]{2,1,0:T(8,128)(2,1)S(1)}, bf16[5,32,512]{2,1,0:T(8,128)(2,1)S(1)}, u32[]{:S(2)}, u32[]{:S(2)}) collective-permute-start(bf16[5,32,512]{2,1,0:T(8,128)(2,1)S(1)} %copy-done.3), channel_id=1, source_target_pairs={{0,64},{1,193},{2,66},{3,195},{4,68},{5,197},{6,70},{7,199},{8,72}... | collective-permute-start | bytes 491528 | tf_op jit(solution)/shard_map/ppermute | solution.py:47
  100.0 3.7 %collective-permute-done.1 = bf16[5,32,512]{2,1,0:T(8,128)(2,1)S(1)} collective-permute-done((bf16[5,32,512]{2,1,0:T(8,128)(2,1)S(1)}, bf16[5,32,512]{2,1,0:T(8,128)(2,1)S(1)}, u32[]{:S(2)}, u32[]{:S(2)}) %collective-permute-start.1) | collective-permute-done | bytes 163872 | tf_op jit(solution)/shard_map/ppermute | solution.py:47
  103.7 1.9 %collective-permute-start.6 = (bf16[4,5,32,512]{3,2,1,0:T(8,128)(2,1)S(1)}, bf16[4,5,32,512]{3,2,1,0:T(8,128)(2,1)S(1)}, u32[]{:S(2)}, u32[]{:S(2)}) collective-permute-start(bf16[4,5,32,512]{3,2,1,0:T(8,128)(2,1)S(1)} %pad_maximum_fusion.own4), channel_id=1, source_target_pairs={{0,960},{1,321},{2,962},{3,323},{4,964},{5,325},{6,966},{7,327},{8... | collective-permute-start | bytes 1966088 | tf_op jit(solution)/shard_map/ppermute | solution.py:47
  105.7 2.0 %collective-permute-start.5 = (bf16[4,5,32,512]{3,2,1,0:T(8,128)(2,1)S(1)}, bf16[4,5,32,512]{3,2,1,0:T(8,128)(2,1)S(1)}, u32[]{:S(2)}, u32[]{:S(2)}) collective-permute-start(bf16[4,5,32,512]{3,2,1,0:T(8,128)(2,1)S(1)} %pad_maximum_fusion.own4), channel_id=1, source_target_pairs={{0,768},{1,257},{2,770},{3,259},{4,772},{5,261},{6,774},{7,263},{8... | collective-permute-start | bytes 1966088 | tf_op jit(solution)/shard_map/ppermute | solution.py:47
  107.7 4.4 %collective-permute-start.4 = (bf16[4,5,32,512]{3,2,1,0:T(8,128)(2,1)S(1)}, bf16[4,5,32,512]{3,2,1,0:T(8,128)(2,1)S(1)}, u32[]{:S(2)}, u32[]{:S(2)}) collective-permute-start(bf16[4,5,32,512]{3,2,1,0:T(8,128)(2,1)S(1)} %pad_maximum_fusion.own4), channel_id=1, source_target_pairs={{0,192},{1,65},{2,194},{3,67},{4,196},{5,69},{6,198},{7,71},{8,200... | collective-permute-start | bytes 1966088 | tf_op jit(solution)/shard_map/ppermute | solution.py:47
  112.1 6.6 %shard_map.94.middle = bf16[5,512,512]{2,1,0:T(8,128)(2,1)} custom-call(bf16[5,512,512]{2,1,0:T(8,128)(2,1)} %basis, f32[5,1,512]{2,1,0:T(1,128)} %broadcast_in_dim.8.factor), custom_call_target="tpu_custom_call" | custom-call | flops 2684354560 | bytes 5242880 | tf_op jit(solution)/shard_map/pallas_call | solution.py:120
  118.7 3.5 %all-to-all-done.2 = bf16[32,5,4,128]{3,2,1,0:T(4,128)(2,1)S(1)} async-done(((bf16[32,5,4,128]{3,2,1,0:T(4,128)(2,1)}), bf16[32,5,4,128]{3,2,1,0:T(4,128)(2,1)S(1)}, u32[]{:S(2)}, u32[]{:S(2)}) %all-to-all-start.2) | async-done | bytes 163872 | tf_op jit(solution)/shard_map/all_to_all | solution.py:236
  122.4 0.9 broadcast_in_dim.10
  123.3 3.5 %all-to-all-start.3 = ((bf16[4,5,32,512]{3,2,1,0:T(8,128)(2,1)}), bf16[4,5,32,512]{3,2,1,0:T(8,128)(2,1)S(1)}, u32[]{:S(2)}, u32[]{:S(2)}) async-start(bf16[4,5,32,512]{3,2,1,0:T(8,128)(2,1)} %broadcast_in_dim.10), calls=%async_computation.3 | async-start | bytes 1310720 | tf_op jit(solution)/shard_map/all_to_all | solution.py:21
  126.8 7.6 %all-to-all-done.3.own4 = bf16[4,5,32,512]{3,2,1,0:T(8,128)(2,1)S(1)} async-done(((bf16[4,5,32,512]{3,2,1,0:T(8,128)(2,1)}), bf16[4,5,32,512]{3,2,1,0:T(8,128)(2,1)S(1)}, u32[]{:S(2)}, u32[]{:S(2)}) %all-to-all-start.3) | async-done | bytes 655392 | tf_op jit(solution)/shard_map/all_to_all | solution.py:21
  134.5 2.2 %collective-permute-start.9 = (bf16[4,5,32,512]{3,2,1,0:T(8,128)(2,1)S(1)}, bf16[4,5,32,512]{3,2,1,0:T(8,128)(2,1)S(1)}, u32[]{:S(2)}, u32[]{:S(2)}) collective-permute-start(bf16[4,5,32,512]{3,2,1,0:T(8,128)(2,1)S(1)} %all-to-all-done.3.own4), channel_id=1, source_target_pairs={{0,960},{1,321},{2,962},{3,323},{4,964},{5,325},{6,966},{7,327},{8... | collective-permute-start | bytes 1966088 | tf_op jit(solution)/shard_map/ppermute | solution.py:47
  136.6 3.4 %collective-permute-start.8 = (bf16[4,5,32,512]{3,2,1,0:T(8,128)(2,1)S(1)}, bf16[4,5,32,512]{3,2,1,0:T(8,128)(2,1)S(1)}, u32[]{:S(2)}, u32[]{:S(2)}) collective-permute-start(bf16[4,5,32,512]{3,2,1,0:T(8,128)(2,1)S(1)} %all-to-all-done.3.own4), channel_id=1, source_target_pairs={{0,768},{1,257},{2,770},{3,259},{4,772},{5,261},{6,774},{7,263},{8... | collective-permute-start | bytes 1966088 | tf_op jit(solution)/shard_map/ppermute | solution.py:47
  140.0 3.1 %collective-permute-start.7 = (bf16[4,5,32,512]{3,2,1,0:T(8,128)(2,1)S(1)}, bf16[4,5,32,512]{3,2,1,0:T(8,128)(2,1)S(1)}, u32[]{:S(2)}, u32[]{:S(2)}) collective-permute-start(bf16[4,5,32,512]{3,2,1,0:T(8,128)(2,1)S(1)} %all-to-all-done.3.own4), channel_id=1, source_target_pairs={{0,192},{1,65},{2,194},{3,67},{4,196},{5,69},{6,198},{7,71},{8,200... | collective-permute-start | bytes 1966088 | tf_op jit(solution)/shard_map/ppermute | solution.py:47
  143.8 3.4 %collective-permute-done.9.corner4 = bf16[4,5,32,512]{3,2,1,0:T(8,128)(2,1)S(1)} collective-permute-done((bf16[4,5,32,512]{3,2,1,0:T(8,128)(2,1)S(1)}, bf16[4,5,32,512]{3,2,1,0:T(8,128)(2,1)S(1)}, u32[]{:S(2)}, u32[]{:S(2)}) %collective-permute-start.9) | collective-permute-done | bytes 655392 | tf_op jit(solution)/shard_map/ppermute | solution.py:47
  147.3 6.1 %collective-permute-done.8.across4 = bf16[4,5,32,512]{3,2,1,0:T(8,128)(2,1)S(1)} collective-permute-done((bf16[4,5,32,512]{3,2,1,0:T(8,128)(2,1)S(1)}, bf16[4,5,32,512]{3,2,1,0:T(8,128)(2,1)S(1)}, u32[]{:S(2)}, u32[]{:S(2)}) %collective-permute-start.8) | collective-permute-done | bytes 655392 | tf_op jit(solution)/shard_map/ppermute | solution.py:47
  154.3 5.5 %shard_map.96 = (bf16[5,512,512]{2,1,0:T(8,128)(2,1)}, f32[5,32,512]{2,1,0:T(8,128)}, f32[5,32,512]{2,1,0:T(8,128)}) custom-call(s32[2]{0:T(128)S(1)} %pad_add_fusion.where, bf16[4,5,32,512]{3,2,1,0:T(8,128)(2,1)S(1)} %all-to-all-done.3.own4, bf16[4,5,32,512]{3,2,1,0:T(8,128)(2,1)S(1)} %collective-permute-done.7.along4, ...), custom_call_target="tpu_custom_call" | custom-call | flops 3355443200 | bytes 13107200 | tf_op jit(solution)/shard_map/pallas_call | solution.py:172
  (40 shorter events, 5.8 us)
Async XLA Ops:
  0.6 54.0 %copy-start.4 = (f32[5,512]{1,0:T(8,128)S(1)}, f32[5,512]{1,0:T(8,128)}, u32[]{:S(2)}) copy-start(f32[5,512]{1,0:T(8,128)} %param.11) | copy-start | bytes 30724
  0.6 54.1 %copy-start.5 = (s32[128]{0:T(128)S(1)}, s32[128]{0:T(128)}, u32[]{:S(2)}) copy-start(s32[128]{0:T(128)} %param.8) | copy-start | bytes 1540
  2.0 87.2 %copy-start.3 = (bf16[5,32,512]{2,1,0:T(8,128)(2,1)S(1)}, bf16[5,32,512]{2,1,0:T(8,128)(2,1)}, u32[]{:S(2)}) copy-start(bf16[5,32,512]{2,1,0:T(8,128)(2,1)} %param.9) | copy-start | bytes 491524
  22.1 56.0 %all-to-all-start.1 = ((bf16[32,8,128]{2,1,0:T(8,128)(2,1)}), bf16[32,8,128]{2,1,0:T(8,128)(2,1)S(1)}, u32[]{:S(2)}, u32[]{:S(2)}) async-start(bf16[32,8,128]{2,1,0:T(8,128)(2,1)} %bitcast.3), calls=%async_computation.1 | async-start | bytes 131072 | tf_op jit(solution)/shard_map/all_to_all | solution.py:216
  78.1 6.2 %collective-permute-start = (bf16[32,8,128]{2,1,0:T(8,128)(2,1)S(1)}, bf16[32,8,128]{2,1,0:T(8,128)(2,1)S(1)}, u32[]{:S(2)}, u32[]{:S(2)}) collective-permute-start(bf16[32,8,128]{2,1,0:T(8,128)(2,1)S(1)} %all-to-all-done.1), channel_id=1, source_target_pairs={{0,1},{1,0},{2,3},{3,2},{4,5},{5,4},{6,7},{7,6},{8,9},{9,8},{10,11... | collective-permute-start | bytes 196616 | tf_op jit(solution)/shard_map/ppermute | solution.py:218
  85.3 37.0 %all-to-all-start.2 = ((bf16[32,5,4,128]{3,2,1,0:T(4,128)(2,1)}), bf16[32,5,4,128]{3,2,1,0:T(4,128)(2,1)S(1)}, u32[]{:S(2)}, u32[]{:S(2)}) async-start(bf16[32,5,4,128]{3,2,1,0:T(4,128)(2,1)} %reshape.44), calls=%async_computation.2 | async-start | bytes 327680 | tf_op jit(solution)/shard_map/all_to_all | solution.py:236
  89.1 10.8 %collective-permute-start.3 = (bf16[5,32,512]{2,1,0:T(8,128)(2,1)S(1)}, bf16[5,32,512]{2,1,0:T(8,128)(2,1)S(1)}, u32[]{:S(2)}, u32[]{:S(2)}) collective-permute-start(bf16[5,32,512]{2,1,0:T(8,128)(2,1)S(1)} %copy-done.3), channel_id=1, source_target_pairs={{0,320},{1,961},{2,322},{3,963},{4,324},{5,965},{6,326},{7,967},{8... | collective-permute-start | bytes 491528 | tf_op jit(solution)/shard_map/ppermute | solution.py:47
  92.1 7.8 %collective-permute-start.2 = (bf16[5,32,512]{2,1,0:T(8,128)(2,1)S(1)}, bf16[5,32,512]{2,1,0:T(8,128)(2,1)S(1)}, u32[]{:S(2)}, u32[]{:S(2)}) collective-permute-start(bf16[5,32,512]{2,1,0:T(8,128)(2,1)S(1)} %copy-done.3), channel_id=1, source_target_pairs={{0,256},{1,769},{2,258},{3,771},{4,260},{5,773},{6,262},{7,775},{8... | collective-permute-start | bytes 491528 | tf_op jit(solution)/shard_map/ppermute | solution.py:47
  96.1 7.6 %collective-permute-start.1 = (bf16[5,32,512]{2,1,0:T(8,128)(2,1)S(1)}, bf16[5,32,512]{2,1,0:T(8,128)(2,1)S(1)}, u32[]{:S(2)}, u32[]{:S(2)}) collective-permute-start(bf16[5,32,512]{2,1,0:T(8,128)(2,1)S(1)} %copy-done.3), channel_id=1, source_target_pairs={{0,64},{1,193},{2,66},{3,195},{4,68},{5,197},{6,70},{7,199},{8,72}... | collective-permute-start | bytes 491528 | tf_op jit(solution)/shard_map/ppermute | solution.py:47
  103.7 23.1 %collective-permute-start.6 = (bf16[4,5,32,512]{3,2,1,0:T(8,128)(2,1)S(1)}, bf16[4,5,32,512]{3,2,1,0:T(8,128)(2,1)S(1)}, u32[]{:S(2)}, u32[]{:S(2)}) collective-permute-start(bf16[4,5,32,512]{3,2,1,0:T(8,128)(2,1)S(1)} %pad_maximum_fusion.own4), channel_id=1, source_target_pairs={{0,960},{1,321},{2,962},{3,323},{4,964},{5,325},{6,966},{7,327},{8... | collective-permute-start | bytes 1966088 | tf_op jit(solution)/shard_map/ppermute | solution.py:47
  105.7 21.1 %collective-permute-start.5 = (bf16[4,5,32,512]{3,2,1,0:T(8,128)(2,1)S(1)}, bf16[4,5,32,512]{3,2,1,0:T(8,128)(2,1)S(1)}, u32[]{:S(2)}, u32[]{:S(2)}) collective-permute-start(bf16[4,5,32,512]{3,2,1,0:T(8,128)(2,1)S(1)} %pad_maximum_fusion.own4), channel_id=1, source_target_pairs={{0,768},{1,257},{2,770},{3,259},{4,772},{5,261},{6,774},{7,263},{8... | collective-permute-start | bytes 1966088 | tf_op jit(solution)/shard_map/ppermute | solution.py:47
  107.7 19.1 %collective-permute-start.4 = (bf16[4,5,32,512]{3,2,1,0:T(8,128)(2,1)S(1)}, bf16[4,5,32,512]{3,2,1,0:T(8,128)(2,1)S(1)}, u32[]{:S(2)}, u32[]{:S(2)}) collective-permute-start(bf16[4,5,32,512]{3,2,1,0:T(8,128)(2,1)S(1)} %pad_maximum_fusion.own4), channel_id=1, source_target_pairs={{0,192},{1,65},{2,194},{3,67},{4,196},{5,69},{6,198},{7,71},{8,200... | collective-permute-start | bytes 1966088 | tf_op jit(solution)/shard_map/ppermute | solution.py:47
  123.3 11.2 %all-to-all-start.3 = ((bf16[4,5,32,512]{3,2,1,0:T(8,128)(2,1)}), bf16[4,5,32,512]{3,2,1,0:T(8,128)(2,1)S(1)}, u32[]{:S(2)}, u32[]{:S(2)}) async-start(bf16[4,5,32,512]{3,2,1,0:T(8,128)(2,1)} %broadcast_in_dim.10), calls=%async_computation.3 | async-start | bytes 1310720 | tf_op jit(solution)/shard_map/all_to_all | solution.py:21
  134.5 19.8 %copy-start = (f32[5,32,512]{2,1,0:T(8,128)S(1)}, f32[5,32,512]{2,1,0:T(8,128)}, u32[]{:S(2)}) copy-start(f32[5,32,512]{2,1,0:T(8,128)} %left.1) | copy-start | bytes 983044
  134.5 19.8 %copy-start.1 = (f32[5,32,512]{2,1,0:T(8,128)S(1)}, f32[5,32,512]{2,1,0:T(8,128)}, u32[]{:S(2)}) copy-start(f32[5,32,512]{2,1,0:T(8,128)} %right.1) | copy-start | bytes 983044
  134.5 19.8 %copy-start.2 = (bf16[5,512,512]{2,1,0:T(8,128)(2,1)S(1)}, bf16[5,512,512]{2,1,0:T(8,128)(2,1)}, u32[]{:S(2)}) copy-start(bf16[5,512,512]{2,1,0:T(8,128)(2,1)} %shard_map.94.middle) | copy-start | bytes 7864324
  134.5 12.8 %collective-permute-start.9 = (bf16[4,5,32,512]{3,2,1,0:T(8,128)(2,1)S(1)}, bf16[4,5,32,512]{3,2,1,0:T(8,128)(2,1)S(1)}, u32[]{:S(2)}, u32[]{:S(2)}) collective-permute-start(bf16[4,5,32,512]{3,2,1,0:T(8,128)(2,1)S(1)} %all-to-all-done.3.own4), channel_id=1, source_target_pairs={{0,960},{1,321},{2,962},{3,323},{4,964},{5,325},{6,966},{7,327},{8... | collective-permute-start | bytes 1966088 | tf_op jit(solution)/shard_map/ppermute | solution.py:47
  136.6 16.8 %collective-permute-start.8 = (bf16[4,5,32,512]{3,2,1,0:T(8,128)(2,1)S(1)}, bf16[4,5,32,512]{3,2,1,0:T(8,128)(2,1)S(1)}, u32[]{:S(2)}, u32[]{:S(2)}) collective-permute-start(bf16[4,5,32,512]{3,2,1,0:T(8,128)(2,1)S(1)} %all-to-all-done.3.own4), channel_id=1, source_target_pairs={{0,768},{1,257},{2,770},{3,259},{4,772},{5,261},{6,774},{7,263},{8... | collective-permute-start | bytes 1966088 | tf_op jit(solution)/shard_map/ppermute | solution.py:47
  140.0 14.2 %collective-permute-start.7 = (bf16[4,5,32,512]{3,2,1,0:T(8,128)(2,1)S(1)}, bf16[4,5,32,512]{3,2,1,0:T(8,128)(2,1)S(1)}, u32[]{:S(2)}, u32[]{:S(2)}) collective-permute-start(bf16[4,5,32,512]{3,2,1,0:T(8,128)(2,1)S(1)} %all-to-all-done.3.own4), channel_id=1, source_target_pairs={{0,192},{1,65},{2,194},{3,67},{4,196},{5,69},{6,198},{7,71},{8,200... | collective-permute-start | bytes 1966088 | tf_op jit(solution)/shard_map/ppermute | solution.py:47

commit v10 on v9

--- a/solution.py
+++ b/solution.py
@@ -207,14 +207,10 @@
 
     summed = summed.reshape(blocks, row_tiles, 2, 4, col_tiles, 128)
     pieces = summed.transpose(1, 4, 2, 0, 3, 5).reshape(n_z, blocks * 4, 128)
-    pieces, right_eigen, owner_map, my_dp, my_core, left_root = lax.optimization_barrier(
-        (pieces, right_eigen, owner_map, my_dp, my_core, left_root)
-    )
+    pieces, left_root = lax.optimization_barrier((pieces, left_root))
     root4 = jnp.stack([left_root] + [swap_corner(left_root, a, b, 1) for a, b in MOVES])
-    where = jnp.stack([my_dp, my_core]).astype(jnp.int32)
-    factor = ((right_eigen + epsilon) ** (-0.25))[:, None, :]
     spread = lax.all_to_all(pieces, "z", split_axis=0, concat_axis=0, tiled=True)
-    spread, where, factor = lax.optimization_barrier((spread, where, factor))
+    spread, owner_map, my_core = lax.optimization_barrier((spread, owner_map, my_core))
     swapped = lax.ppermute(spread, "core", [(0, 1), (1, 0)])
     held = jnp.concatenate([t.reshape(n_z * blocks, 4 * 128) for t in (spread, swapped)])
 
@@ -230,11 +226,15 @@
     pick = (jnp.arange(n_z * cap, dtype=jnp.int32)[:, None] == place[None, :]).astype(jnp.bfloat16)
     chosen = jnp.dot(pick, held, preferred_element_type=jnp.float32).astype(jnp.bfloat16)
     deliver = chosen.reshape(n_z, cap, 4, 128)
-    deliver, right_basis, factor = lax.optimization_barrier((deliver, right_basis, factor))
+    deliver, right_basis, right_eigen, my_dp, my_core = lax.optimization_barrier(
+        (deliver, right_basis, right_eigen, my_dp, my_core)
+    )
+    where = jnp.stack([my_dp, my_core]).astype(jnp.int32)
+    factor = ((right_eigen + epsilon) ** (-0.25))[:, None, :]
     middle = middle_step(right_basis, factor)
     roots = [root4] + [swap_corner(root4, a, b, 0) for a, b in MOVES]
     arrived = lax.all_to_all(deliver, "z", split_axis=0, concat_axis=0, tiled=True)
-    arrived, middle = lax.optimization_barrier((arrived, middle))
+    arrived, middle, where = lax.optimization_barrier((arrived, middle, where))
 
     owned = arrived.reshape(row_tiles, col_tiles, 2, cap, 4, 128)
     owned = owned.transpose(3, 0, 2, 4, 1, 5).reshape(cap, rows, width)

time: 163 us -> 162 us (level)
  blocking collectives: 19.3 us -> 75.1 us
  starting transfers between devices: 73 us -> 40.5 us
  waiting for transfers between devices: 48 us -> 24.6 us
    all_to_all x0 -> x1, blocking collectives: none -> 55.8 us  [body(): lax.all_to_all(pieces, 'z', split_axis=0, concat_axis=0, tiled=True)]
    all_to_all x1 -> x0, starting transfers between devices: 32.6 us -> none  [body(): lax.all_to_all(pieces, 'z', split_axis=0, concat_axis=0, tiled=True)]
    all_to_all x1 -> x0, waiting for transfers between devices: 22 us -> none  [body(): lax.all_to_all(pieces, 'z', split_axis=0, concat_axis=0, tiled=True)]
  transfers between devices with their start and end apart: 13 -> 12, of which waited for: 8 -> 7; matrix products, arithmetic and copies ran while one was open for 2% -> 2% of each run, Pallas kernels for 5% -> 5%
where the time goes in v10:
time: 162 us; the launch traced here: 159 us
  blocking collectives  75.1 us (46%)
  starting transfers between devices  40.5 us (25%)
  waiting for transfers between devices  24.6 us (15%)
  Pallas kernels  12.8 us (8%)
  local copies, waits for them, and re-layouts  4.21 us (3%)
    all_to_all x1, blocking collectives, body(): lax.all_to_all(pieces, 'z', split_axis=0, concat_axis=0, tiled=True)  55.8 us
    ppermute x9, starting transfers between devices, swap_corner(): return lax.ppermute(x, ALL, pairs)  27.8 us
    all_to_all x1, blocking collectives, body(): parts = lax.all_to_all(sent, 'dp', split_axis=0, concat_axis=0, tiled=True)  19.3 us
    ppermute x9, waiting for transfers between devices, swap_corner(): return lax.ppermute(x, ALL, pairs)  14.1 us
    all_to_all x1, waiting for transfers between devices, broadcast_gather(): lax.all_to_all(copies, axis, split_axis=0, concat_axis=0, tiled=True, axi...  7.63 us
    pallas_call x1, Pallas kernels, middle_step(): pl.pallas_call(middle_kernel, grid=(cap,), in_specs=[whole, pl.BlockSpec(...  6.57 us
    pallas_call x1, Pallas kernels, slot_step(): pl.pallas_call(slot_kernel, in_specs=[pl.BlockSpec(memory_space=pltpu.SME...  5.47 us
    ppermute x1, starting transfers between devices, body(): swapped = lax.ppermute(spread, 'core', [(0, 1), (1, 0)])  5.31 us
  transfers between devices with their start and end apart: 12, of which 7 were waited for; matrix products, arithmetic and copies ran while one was open for 2% of the time, Pallas kernels for 5%

profile of v10, /device:TPU:1, one launch (start us, length us, event | category | flops | bytes accessed | tf_op | source)
XLA Modules:
  0.0 159.0 jit_solution(12735941355424805033)
XLA Ops:
  0.6 1.3 copy.19
  2.0 19.3 %all_to_all.20 = bf16[16,2,32,512]{3,2,1,0:T(8,128)(2,1)S(1)} all-to-all(bf16[16,2,32,512]{3,2,1,0:T(8,128)(2,1)S(1)} %copy.19), channel_id=1, replica_groups=mesh['dp'=16,'z'=32,'core'=2] {'dp'}, dimensions={0} | all-to-all | bytes 2097152 | tf_op jit(solution)/shard_map/all_to_all | solution.py:205
  21.5 55.8 %all_to_all.21 = bf16[32,8,128]{2,1,0:T(8,128)(2,1)S(1)} all-to-all(bf16[32,8,128]{2,1,0:T(8,128)(2,1)S(1)} %bitcast.19), channel_id=1, replica_groups=mesh['dp'=16,'z'=32,'core'=2] {'z'}, dimensions={0} | all-to-all | bytes 131072 | tf_op jit(solution)/shard_map/all_to_all | solution.py:212
  77.3 5.3 %collective-permute-start = (bf16[32,8,128]{2,1,0:T(8,128)(2,1)S(1)}, bf16[32,8,128]{2,1,0:T(8,128)(2,1)S(1)}, u32[]{:S(2)}, u32[]{:S(2)}) collective-permute-start(bf16[32,8,128]{2,1,0:T(8,128)(2,1)S(1)} %all_to_all.21), channel_id=1, source_target_pairs={{0,1},{1,0},{2,3},{3,2},{4,5},{5,4},{6,7},{7,6},{8,9},{9,8},{10,11... | collective-permute-start | bytes 196616 | tf_op jit(solution)/shard_map/ppermute | solution.py:214
  84.5 3.9 %all-to-all-start.2 = ((bf16[32,5,4,128]{3,2,1,0:T(4,128)(2,1)}), bf16[32,5,4,128]{3,2,1,0:T(4,128)(2,1)S(1)}, u32[]{:S(2)}, u32[]{:S(2)}) async-start(bf16[32,5,4,128]{3,2,1,0:T(4,128)(2,1)} %reshape.44), calls=%async_computation.2 | async-start | bytes 327680 | tf_op jit(solution)/shard_map/all_to_all | solution.py:236
  88.4 3.0 %collective-permute-start.3 = (bf16[5,32,512]{2,1,0:T(8,128)(2,1)S(1)}, bf16[5,32,512]{2,1,0:T(8,128)(2,1)S(1)}, u32[]{:S(2)}, u32[]{:S(2)}) collective-permute-start(bf16[5,32,512]{2,1,0:T(8,128)(2,1)S(1)} %copy-done.3), channel_id=1, source_target_pairs={{0,320},{1,961},{2,322},{3,963},{4,324},{5,965},{6,326},{7,967},{8... | collective-permute-start | bytes 491528 | tf_op jit(solution)/shard_map/ppermute | solution.py:47
  91.4 3.9 %collective-permute-start.2 = (bf16[5,32,512]{2,1,0:T(8,128)(2,1)S(1)}, bf16[5,32,512]{2,1,0:T(8,128)(2,1)S(1)}, u32[]{:S(2)}, u32[]{:S(2)}) collective-permute-start(bf16[5,32,512]{2,1,0:T(8,128)(2,1)S(1)} %copy-done.3), channel_id=1, source_target_pairs={{0,256},{1,769},{2,258},{3,771},{4,260},{5,773},{6,262},{7,775},{8... | collective-permute-start | bytes 491528 | tf_op jit(solution)/shard_map/ppermute | solution.py:47
  95.3 3.9 %collective-permute-start.1 = (bf16[5,32,512]{2,1,0:T(8,128)(2,1)S(1)}, bf16[5,32,512]{2,1,0:T(8,128)(2,1)S(1)}, u32[]{:S(2)}, u32[]{:S(2)}) collective-permute-start(bf16[5,32,512]{2,1,0:T(8,128)(2,1)S(1)} %copy-done.3), channel_id=1, source_target_pairs={{0,64},{1,193},{2,66},{3,195},{4,68},{5,197},{6,70},{7,199},{8,72}... | collective-permute-start | bytes 491528 | tf_op jit(solution)/shard_map/ppermute | solution.py:47
  99.2 3.7 %collective-permute-done.1 = bf16[5,32,512]{2,1,0:T(8,128)(2,1)S(1)} collective-permute-done((bf16[5,32,512]{2,1,0:T(8,128)(2,1)S(1)}, bf16[5,32,512]{2,1,0:T(8,128)(2,1)S(1)}, u32[]{:S(2)}, u32[]{:S(2)}) %collective-permute-start.1) | collective-permute-done | bytes 163872 | tf_op jit(solution)/shard_map/ppermute | solution.py:47
  103.0 1.9 %collective-permute-start.6 = (bf16[4,5,32,512]{3,2,1,0:T(8,128)(2,1)S(1)}, bf16[4,5,32,512]{3,2,1,0:T(8,128)(2,1)S(1)}, u32[]{:S(2)}, u32[]{:S(2)}) collective-permute-start(bf16[4,5,32,512]{3,2,1,0:T(8,128)(2,1)S(1)} %pad_maximum_fusion.own4), channel_id=1, source_target_pairs={{0,960},{1,321},{2,962},{3,323},{4,964},{5,325},{6,966},{7,327},{8... | collective-permute-start | bytes 1966088 | tf_op jit(solution)/shard_map/ppermute | solution.py:47
  104.9 2.0 %collective-permute-start.5 = (bf16[4,5,32,512]{3,2,1,0:T(8,128)(2,1)S(1)}, bf16[4,5,32,512]{3,2,1,0:T(8,128)(2,1)S(1)}, u32[]{:S(2)}, u32[]{:S(2)}) collective-permute-start(bf16[4,5,32,512]{3,2,1,0:T(8,128)(2,1)S(1)} %pad_maximum_fusion.own4), channel_id=1, source_target_pairs={{0,768},{1,257},{2,770},{3,259},{4,772},{5,261},{6,774},{7,263},{8... | collective-permute-start | bytes 1966088 | tf_op jit(solution)/shard_map/ppermute | solution.py:47
  106.9 4.4 %collective-permute-start.4 = (bf16[4,5,32,512]{3,2,1,0:T(8,128)(2,1)S(1)}, bf16[4,5,32,512]{3,2,1,0:T(8,128)(2,1)S(1)}, u32[]{:S(2)}, u32[]{:S(2)}) collective-permute-start(bf16[4,5,32,512]{3,2,1,0:T(8,128)(2,1)S(1)} %pad_maximum_fusion.own4), channel_id=1, source_target_pairs={{0,192},{1,65},{2,194},{3,67},{4,196},{5,69},{6,198},{7,71},{8,200... | collective-permute-start | bytes 1966088 | tf_op jit(solution)/shard_map/ppermute | solution.py:47
  112.0 6.6 %shard_map.94.middle = bf16[5,512,512]{2,1,0:T(8,128)(2,1)} custom-call(bf16[5,512,512]{2,1,0:T(8,128)(2,1)} %basis, f32[5,1,512]{2,1,0:T(1,128)} %broadcast_in_dim.8.factor), custom_call_target="tpu_custom_call" | custom-call | flops 2684354560 | bytes 5242880 | tf_op jit(solution)/shard_map/pallas_call | solution.py:120
  118.7 2.8 %all-to-all-done.2 = bf16[32,5,4,128]{3,2,1,0:T(4,128)(2,1)S(1)} async-done(((bf16[32,5,4,128]{3,2,1,0:T(4,128)(2,1)}), bf16[32,5,4,128]{3,2,1,0:T(4,128)(2,1)S(1)}, u32[]{:S(2)}, u32[]{:S(2)}) %all-to-all-start.2) | async-done | bytes 163872 | tf_op jit(solution)/shard_map/all_to_all | solution.py:236
  121.6 0.9 broadcast_in_dim.10
  122.5 3.5 %all-to-all-start.3 = ((bf16[4,5,32,512]{3,2,1,0:T(8,128)(2,1)}), bf16[4,5,32,512]{3,2,1,0:T(8,128)(2,1)S(1)}, u32[]{:S(2)}, u32[]{:S(2)}) async-start(bf16[4,5,32,512]{3,2,1,0:T(8,128)(2,1)} %broadcast_in_dim.10), calls=%async_computation.3 | async-start | bytes 1310720 | tf_op jit(solution)/shard_map/all_to_all | solution.py:21
  126.0 7.6 %all-to-all-done.3.own4 = bf16[4,5,32,512]{3,2,1,0:T(8,128)(2,1)S(1)} async-done(((bf16[4,5,32,512]{3,2,1,0:T(8,128)(2,1)}), bf16[4,5,32,512]{3,2,1,0:T(8,128)(2,1)S(1)}, u32[]{:S(2)}, u32[]{:S(2)}) %all-to-all-start.3) | async-done | bytes 655392 | tf_op jit(solution)/shard_map/all_to_all | solution.py:21
  133.7 2.2 %collective-permute-start.9 = (bf16[4,5,32,512]{3,2,1,0:T(8,128)(2,1)S(1)}, bf16[4,5,32,512]{3,2,1,0:T(8,128)(2,1)S(1)}, u32[]{:S(2)}, u32[]{:S(2)}) collective-permute-start(bf16[4,5,32,512]{3,2,1,0:T(8,128)(2,1)S(1)} %all-to-all-done.3.own4), channel_id=1, source_target_pairs={{0,960},{1,321},{2,962},{3,323},{4,964},{5,325},{6,966},{7,327},{8... | collective-permute-start | bytes 1966088 | tf_op jit(solution)/shard_map/ppermute | solution.py:47
  135.9 3.4 %collective-permute-start.8 = (bf16[4,5,32,512]{3,2,1,0:T(8,128)(2,1)S(1)}, bf16[4,5,32,512]{3,2,1,0:T(8,128)(2,1)S(1)}, u32[]{:S(2)}, u32[]{:S(2)}) collective-permute-start(bf16[4,5,32,512]{3,2,1,0:T(8,128)(2,1)S(1)} %all-to-all-done.3.own4), channel_id=1, source_target_pairs={{0,768},{1,257},{2,770},{3,259},{4,772},{5,261},{6,774},{7,263},{8... | collective-permute-start | bytes 1966088 | tf_op jit(solution)/shard_map/ppermute | solution.py:47
  139.3 3.1 %collective-permute-start.7 = (bf16[4,5,32,512]{3,2,1,0:T(8,128)(2,1)S(1)}, bf16[4,5,32,512]{3,2,1,0:T(8,128)(2,1)S(1)}, u32[]{:S(2)}, u32[]{:S(2)}) collective-permute-start(bf16[4,5,32,512]{3,2,1,0:T(8,128)(2,1)S(1)} %all-to-all-done.3.own4), channel_id=1, source_target_pairs={{0,192},{1,65},{2,194},{3,67},{4,196},{5,69},{6,198},{7,71},{8,200... | collective-permute-start | bytes 1966088 | tf_op jit(solution)/shard_map/ppermute | solution.py:47
  143.1 3.4 %collective-permute-done.9.corner4 = bf16[4,5,32,512]{3,2,1,0:T(8,128)(2,1)S(1)} collective-permute-done((bf16[4,5,32,512]{3,2,1,0:T(8,128)(2,1)S(1)}, bf16[4,5,32,512]{3,2,1,0:T(8,128)(2,1)S(1)}, u32[]{:S(2)}, u32[]{:S(2)}) %collective-permute-start.9) | collective-permute-done | bytes 655392 | tf_op jit(solution)/shard_map/ppermute | solution.py:47
  146.5 6.1 %collective-permute-done.8.across4 = bf16[4,5,32,512]{3,2,1,0:T(8,128)(2,1)S(1)} collective-permute-done((bf16[4,5,32,512]{3,2,1,0:T(8,128)(2,1)S(1)}, bf16[4,5,32,512]{3,2,1,0:T(8,128)(2,1)S(1)}, u32[]{:S(2)}, u32[]{:S(2)}) %collective-permute-start.8) | collective-permute-done | bytes 655392 | tf_op jit(solution)/shard_map/ppermute | solution.py:47
  152.7 0.8 collective-permute-done.7.along4
  153.5 5.5 %shard_map.96 = (bf16[5,512,512]{2,1,0:T(8,128)(2,1)}, f32[5,32,512]{2,1,0:T(8,128)}, f32[5,32,512]{2,1,0:T(8,128)}) custom-call(s32[2]{0:T(128)S(1)} %pad_add_fusion.1.where, bf16[4,5,32,512]{3,2,1,0:T(8,128)(2,1)S(1)} %all-to-all-done.3.own4, bf16[4,5,32,512]{3,2,1,0:T(8,128)(2,1)S(1)} %collective-permute-done.7.along4, ...), custom_call_target="tpu_custom_call" | custom-call | flops 3355443200 | bytes 13107200 | tf_op jit(solution)/shard_map/pallas_call | solution.py:172
  (39 shorter events, 3.7 us)
Async XLA Ops:
  0.6 82.0 %copy-start.5 = (s32[128]{0:T(128)S(1)}, s32[128]{0:T(128)}, u32[]{:S(2)}) copy-start(s32[128]{0:T(128)} %param.8) | copy-start | bytes 1540
  2.0 86.4 %copy-start.3 = (bf16[5,32,512]{2,1,0:T(8,128)(2,1)S(1)}, bf16[5,32,512]{2,1,0:T(8,128)(2,1)}, u32[]{:S(2)}) copy-start(bf16[5,32,512]{2,1,0:T(8,128)(2,1)} %param.9) | copy-start | bytes 491524
  2.0 109.4 %copy-start.4 = (f32[5,512]{1,0:T(8,128)S(1)}, f32[5,512]{1,0:T(8,128)}, u32[]{:S(2)}) copy-start(f32[5,512]{1,0:T(8,128)} %param.11) | copy-start | bytes 30724
  77.3 6.2 %collective-permute-start = (bf16[32,8,128]{2,1,0:T(8,128)(2,1)S(1)}, bf16[32,8,128]{2,1,0:T(8,128)(2,1)S(1)}, u32[]{:S(2)}, u32[]{:S(2)}) collective-permute-start(bf16[32,8,128]{2,1,0:T(8,128)(2,1)S(1)} %all_to_all.21), channel_id=1, source_target_pairs={{0,1},{1,0},{2,3},{3,2},{4,5},{5,4},{6,7},{7,6},{8,9},{9,8},{10,11... | collective-permute-start | bytes 196616 | tf_op jit(solution)/shard_map/ppermute | solution.py:214
  84.5 37.0 %all-to-all-start.2 = ((bf16[32,5,4,128]{3,2,1,0:T(4,128)(2,1)}), bf16[32,5,4,128]{3,2,1,0:T(4,128)(2,1)S(1)}, u32[]{:S(2)}, u32[]{:S(2)}) async-start(bf16[32,5,4,128]{3,2,1,0:T(4,128)(2,1)} %reshape.44), calls=%async_computation.2 | async-start | bytes 327680 | tf_op jit(solution)/shard_map/all_to_all | solution.py:236
  88.4 10.8 %collective-permute-start.3 = (bf16[5,32,512]{2,1,0:T(8,128)(2,1)S(1)}, bf16[5,32,512]{2,1,0:T(8,128)(2,1)S(1)}, u32[]{:S(2)}, u32[]{:S(2)}) collective-permute-start(bf16[5,32,512]{2,1,0:T(8,128)(2,1)S(1)} %copy-done.3), channel_id=1, source_target_pairs={{0,320},{1,961},{2,322},{3,963},{4,324},{5,965},{6,326},{7,967},{8... | collective-permute-start | bytes 491528 | tf_op jit(solution)/shard_map/ppermute | solution.py:47
  91.4 7.8 %collective-permute-start.2 = (bf16[5,32,512]{2,1,0:T(8,128)(2,1)S(1)}, bf16[5,32,512]{2,1,0:T(8,128)(2,1)S(1)}, u32[]{:S(2)}, u32[]{:S(2)}) collective-permute-start(bf16[5,32,512]{2,1,0:T(8,128)(2,1)S(1)} %copy-done.3), channel_id=1, source_target_pairs={{0,256},{1,769},{2,258},{3,771},{4,260},{5,773},{6,262},{7,775},{8... | collective-permute-start | bytes 491528 | tf_op jit(solution)/shard_map/ppermute | solution.py:47
  95.3 7.6 %collective-permute-start.1 = (bf16[5,32,512]{2,1,0:T(8,128)(2,1)S(1)}, bf16[5,32,512]{2,1,0:T(8,128)(2,1)S(1)}, u32[]{:S(2)}, u32[]{:S(2)}) collective-permute-start(bf16[5,32,512]{2,1,0:T(8,128)(2,1)S(1)} %copy-done.3), channel_id=1, source_target_pairs={{0,64},{1,193},{2,66},{3,195},{4,68},{5,197},{6,70},{7,199},{8,72}... | collective-permute-start | bytes 491528 | tf_op jit(solution)/shard_map/ppermute | solution.py:47
  103.0 23.1 %collective-permute-start.6 = (bf16[4,5,32,512]{3,2,1,0:T(8,128)(2,1)S(1)}, bf16[4,5,32,512]{3,2,1,0:T(8,128)(2,1)S(1)}, u32[]{:S(2)}, u32[]{:S(2)}) collective-permute-start(bf16[4,5,32,512]{3,2,1,0:T(8,128)(2,1)S(1)} %pad_maximum_fusion.own4), channel_id=1, source_target_pairs={{0,960},{1,321},{2,962},{3,323},{4,964},{5,325},{6,966},{7,327},{8... | collective-permute-start | bytes 1966088 | tf_op jit(solution)/shard_map/ppermute | solution.py:47
  104.9 21.1 %collective-permute-start.5 = (bf16[4,5,32,512]{3,2,1,0:T(8,128)(2,1)S(1)}, bf16[4,5,32,512]{3,2,1,0:T(8,128)(2,1)S(1)}, u32[]{:S(2)}, u32[]{:S(2)}) collective-permute-start(bf16[4,5,32,512]{3,2,1,0:T(8,128)(2,1)S(1)} %pad_maximum_fusion.own4), channel_id=1, source_target_pairs={{0,768},{1,257},{2,770},{3,259},{4,772},{5,261},{6,774},{7,263},{8... | collective-permute-start | bytes 1966088 | tf_op jit(solution)/shard_map/ppermute | solution.py:47
  106.9 19.1 %collective-permute-start.4 = (bf16[4,5,32,512]{3,2,1,0:T(8,128)(2,1)S(1)}, bf16[4,5,32,512]{3,2,1,0:T(8,128)(2,1)S(1)}, u32[]{:S(2)}, u32[]{:S(2)}) collective-permute-start(bf16[4,5,32,512]{3,2,1,0:T(8,128)(2,1)S(1)} %pad_maximum_fusion.own4), channel_id=1, source_target_pairs={{0,192},{1,65},{2,194},{3,67},{4,196},{5,69},{6,198},{7,71},{8,200... | collective-permute-start | bytes 1966088 | tf_op jit(solution)/shard_map/ppermute | solution.py:47
  122.5 11.2 %all-to-all-start.3 = ((bf16[4,5,32,512]{3,2,1,0:T(8,128)(2,1)}), bf16[4,5,32,512]{3,2,1,0:T(8,128)(2,1)S(1)}, u32[]{:S(2)}, u32[]{:S(2)}) async-start(bf16[4,5,32,512]{3,2,1,0:T(8,128)(2,1)} %broadcast_in_dim.10), calls=%async_computation.3 | async-start | bytes 1310720 | tf_op jit(solution)/shard_map/all_to_all | solution.py:21
  133.7 19.8 %copy-start = (f32[5,32,512]{2,1,0:T(8,128)S(1)}, f32[5,32,512]{2,1,0:T(8,128)}, u32[]{:S(2)}) copy-start(f32[5,32,512]{2,1,0:T(8,128)} %left.1) | copy-start | bytes 983044
  133.7 19.8 %copy-start.1 = (f32[5,32,512]{2,1,0:T(8,128)S(1)}, f32[5,32,512]{2,1,0:T(8,128)}, u32[]{:S(2)}) copy-start(f32[5,32,512]{2,1,0:T(8,128)} %right.1) | copy-start | bytes 983044
  133.7 19.8 %copy-start.2 = (bf16[5,512,512]{2,1,0:T(8,128)(2,1)S(1)}, bf16[5,512,512]{2,1,0:T(8,128)(2,1)}, u32[]{:S(2)}) copy-start(bf16[5,512,512]{2,1,0:T(8,128)(2,1)} %shard_map.94.middle) | copy-start | bytes 7864324
  133.7 12.8 %collective-permute-start.9 = (bf16[4,5,32,512]{3,2,1,0:T(8,128)(2,1)S(1)}, bf16[4,5,32,512]{3,2,1,0:T(8,128)(2,1)S(1)}, u32[]{:S(2)}, u32[]{:S(2)}) collective-permute-start(bf16[4,5,32,512]{3,2,1,0:T(8,128)(2,1)S(1)} %all-to-all-done.3.own4), channel_id=1, source_target_pairs={{0,960},{1,321},{2,962},{3,323},{4,964},{5,325},{6,966},{7,327},{8... | collective-permute-start | bytes 1966088 | tf_op jit(solution)/shard_map/ppermute | solution.py:47
  135.9 16.8 %collective-permute-start.8 = (bf16[4,5,32,512]{3,2,1,0:T(8,128)(2,1)S(1)}, bf16[4,5,32,512]{3,2,1,0:T(8,128)(2,1)S(1)}, u32[]{:S(2)}, u32[]{:S(2)}) collective-permute-start(bf16[4,5,32,512]{3,2,1,0:T(8,128)(2,1)S(1)} %all-to-all-done.3.own4), channel_id=1, source_target_pairs={{0,768},{1,257},{2,770},{3,259},{4,772},{5,261},{6,774},{7,263},{8... | collective-permute-start | bytes 1966088 | tf_op jit(solution)/shard_map/ppermute | solution.py:47
  139.3 14.2 %collective-permute-start.7 = (bf16[4,5,32,512]{3,2,1,0:T(8,128)(2,1)S(1)}, bf16[4,5,32,512]{3,2,1,0:T(8,128)(2,1)S(1)}, u32[]{:S(2)}, u32[]{:S(2)}) collective-permute-start(bf16[4,5,32,512]{3,2,1,0:T(8,128)(2,1)S(1)} %all-to-all-done.3.own4), channel_id=1, source_target_pairs={{0,192},{1,65},{2,194},{3,67},{4,196},{5,69},{6,198},{7,71},{8,200... | collective-permute-start | bytes 1966088 | tf_op jit(solution)/shard_map/ppermute | solution.py:47
